TPU v7x, 32 devices: a whole 2x2x4 slice. The times are simulated.
32 devices in a mesh: depth: 4 (over y, core), freq: 8 (over z, x).
Axes of the slice: x: 2, y: 2, z: 4, core: 2. Of those that a mesh axis runs over, the one named last changes fastest.
Arguments:
- surface: float32 [64, 2, 64, 256], P('freq'), may hold values from -6 to 6
- freq_slot: int32 [64], P('freq'), may hold values from 0 to 63, each once
- tap_table: float32 [2, 9, 32, 64], replicated, may hold values from -2 to 2
- vel_index: int32 [4, 64, 256], P('depth'), may hold values from 0 to 31
Outputs:
- migrated_image: float32 [4, 64, 256], P('depth')
Inputs may be any that keep to these rules, and one draw needn't show every extreme that they name: `freq_slot`: each frequency of the table is named by exactly one slot.
All inputs are finite; a program needn't handle non-finite values.
Results may differ from a plain program's by a relative error of at most 0.00023.
Values sent between devices are 32-bit elements; how exact they have to be, the bound alone decides.
No kernel may reach another device: no remote copies, remote signals or barrier semaphores. Data moves between devices by JAX's collectives and lax.ppermute only.
A program may use at most 64 MiB of HBM per device.

v0:
```python
import math

import jax
import jax.numpy as jnp
from jax import lax
from jax.sharding import PartitionSpec as P


def shifted(value, axis, steps):
    count = lax.axis_size(axis)
    leading, last = (max(0, -steps), min(count, count - steps))
    return lax.ppermute(value, axis, [(source, source + steps) for source in range(leading, last)])


def smooth(wavefield):
    lead = [(0, 0)] * (wavefield.ndim - 2)
    padded = jnp.pad(wavefield, lead + [(1, 1), (1, 1)])
    smoothed = 0.25 * padded[..., :-2, :] + 0.5 * padded[..., 1:-1, :] + 0.25 * padded[..., 2:, :]
    return 0.25 * smoothed[..., :-2] + 0.5 * smoothed[..., 1:-1] + 0.25 * smoothed[..., 2:]


def mcclellan(wavefield):
    return 2.0 * smooth(wavefield) - wavefield


def extrapolate(wavefield, coef_block):
    earlier = wavefield
    current = mcclellan(wavefield)
    real_acc = coef_block[:, 0, 0] * wavefield[:, 0] - coef_block[:, 1, 0] * wavefield[:, 1]
    imag_acc = coef_block[:, 0, 0] * wavefield[:, 1] + coef_block[:, 1, 0] * wavefield[:, 0]
    for degree in range(1, coef_block.shape[2]):
        if degree > 1:
            earlier, current = (current, 2.0 * mcclellan(current) - earlier)
        real_acc = (
            real_acc
            + coef_block[:, 0, degree] * current[:, 0]
            - coef_block[:, 1, degree] * current[:, 1]
        )
        imag_acc = (
            imag_acc
            + coef_block[:, 0, degree] * current[:, 1]
            + coef_block[:, 1, degree] * current[:, 0]
        )
    return jnp.stack([real_acc, imag_acc], axis=1)


def lookup(tap_part, vel_rows):
    entries = tap_part.shape[3]
    flat_rows = vel_rows.reshape(1, -1)
    one_hot = (flat_rows == jnp.arange(entries, dtype=jnp.int32)[:, None]).astype(jnp.float32)
    product = jnp.dot(
        tap_part.reshape(-1, entries),
        one_hot,
        precision=lax.Precision.HIGHEST,
        preferred_element_type=jnp.float32,
    )
    return product.reshape(tap_part.shape[:3] + vel_rows.shape)


def per_device(surface, freq_slot, tap_table, vel_index):
    local_count = surface.shape[0]
    depth_count = lax.axis_size("depth")
    depth_pos = lax.axis_index("depth")
    tap_rows = jnp.moveaxis(jnp.take(tap_table, freq_slot, axis=3), 3, 0)
    groups = 4
    batch_size = local_count // groups
    levels = vel_index.shape[0]
    all_coefs = lookup(tap_rows, vel_index)
    section_count = groups + depth_count - 1

    def run_slab(operands):
        wavefield, coef_part = operands
        wavefield = extrapolate(wavefield, coef_part[:, :, :, 0])
        layers = [jnp.sum(wavefield[:, 0], axis=0)]
        return (wavefield, jnp.stack(layers))

    def skip_slab(operands):
        return (operands[0], jnp.zeros((levels,) + operands[0].shape[2:], jnp.float32))

    def advance_section(section_no, state_pair):
        incoming, image_acc = state_pair
        member = section_no - depth_pos
        active = jnp.logical_and(member >= 0, member < groups)
        offset = jnp.clip(member, 0, groups - 1) * batch_size
        surface_part = lax.dynamic_slice_in_dim(surface, offset, batch_size, 0)
        wavefield = jnp.where(depth_pos == 0, surface_part, incoming)
        coef_part = lax.dynamic_slice_in_dim(all_coefs, offset, batch_size, 0)
        outgoing, layer_image = lax.cond(active, run_slab, skip_slab, (wavefield, coef_part))
        passed = shifted(outgoing, "depth", 1)
        return (passed, image_acc + layer_image)

    initial = (
        jnp.zeros((batch_size,) + surface.shape[1:], jnp.float32),
        jnp.zeros((levels,) + surface.shape[2:], jnp.float32),
    )
    _, image_part = lax.fori_loop(0, section_count, advance_section, initial)
    summed = lax.psum(image_part, "freq")
    return summed / math.sqrt(local_count * lax.axis_size("freq"))


def solution(mesh):
    in_specs = (P("freq", None, None, None), P("freq"), P(), P("depth", None, None))
    out_specs = P("depth", None, None)
    return jax.shard_map(
        per_device, mesh=mesh, in_specs=in_specs, out_specs=out_specs, check_vma=False
    )
```

profile of v0, /device:TPU:0, one launch (start us, length us, event | category | flops | bytes accessed | tf_op | source)
XLA Modules:
  0.0 220.3 jit_solution(6950985796061030533)
XLA Ops:
  7.9 1.2 copy.10
  9.9 11.0 %convolution_bitcast_fusion = f32[8,2,9,1,64,256]{5,2,4,1,0,3:T(8,128)} fusion(s32[64,256]{1,0:T(8,128)} %bitcast.346, f32[8,2,9,32,1]{3,1,2,0,4:T(2,128)S(1)} %select_bitcast_fusion), kind=kOutput, calls=%fused_computation.247 | convolution fusion | flops 906493952 | bytes 9521152 | tf_op jit(solution)/shard_map/dot_general | solution.py:51
  20.9 16.7 %copy.13 = f32[8,2,9,1,64,256]{5,4,3,2,1,0:T(8,128)} copy(f32[8,2,9,1,64,256]{5,2,4,1,0,3:T(8,128)} %convolution_bitcast_fusion) | data formatting | bytes 18874368
  37.6 96.9 %while.17 = (s32[]{:T(128)}, f32[2,2,64,256]{3,2,0,1:T(8,128)S(1)}, f32[1,64,256]{2,1,0:T(8,128)S(1)}, s32[]{:T(128)}, pred[]{:T(512)}, /*index=5*/f32[8,2,64,25...) while((s32[]{:T(128)}, f32[2,2,64,256]{3,2,0,1:T(8,128)S(1)}, ...), condition=%wide.region_4.5_spmd.clone, body=%wide.region_0.4_spmd.clone.sunk | while | flops 10850318 | bytes 38291264 | solution.py:96
  37.8 1.0 copy_select_fusion.2
  38.8 8.0 %conditional.3 = (f32[2,2,64,256]{3,2,0,1:T(8,128)S(1)}, f32[1,64,256]{2,1,0:T(8,128)S(1)}) conditional(s32[]{:T(128)} %convert_element_type.20, f32[2,2,64,256]{3,2,0,1:T(8,128)S(1)} %copy_select_fusion.2, (f32[8,2,9,1,64,256]{5,4,3,2,1,0:T(8,128)}, s32[]{:T(128)}, f32[2,2,64,256]{3,2,0,1:T(8,128)S(1)}) %tuple.55), branch_computations={%region_1.1_spmd, %region_2.3_spmd} | conditional | flops 10752000 | bytes 36258320 | solution.py:88
  43.6 1.9 copy_bitcast_fusion
  46.8 1.3 collective-permute-start
  48.1 1.1 collective-permute-done
  49.2 1.0 copy_select_fusion.2
  50.2 8.0 %conditional.3 = (f32[2,2,64,256]{3,2,0,1:T(8,128)S(1)}, f32[1,64,256]{2,1,0:T(8,128)S(1)}) conditional(s32[]{:T(128)} %convert_element_type.20, f32[2,2,64,256]{3,2,0,1:T(8,128)S(1)} %copy_select_fusion.2, (f32[8,2,9,1,64,256]{5,4,3,2,1,0:T(8,128)}, s32[]{:T(128)}, f32[2,2,64,256]{3,2,0,1:T(8,128)S(1)}) %tuple.55), branch_computations={%region_1.1_spmd, %region_2.3_spmd} | conditional | flops 10752000 | bytes 36258320 | solution.py:88
  55.0 1.9 copy_bitcast_fusion
  58.2 2.3 %collective-permute-start = (f32[2,2,64,256]{3,2,0,1:T(8,128)S(1)}, f32[2,2,64,256]{3,2,0,1:T(8,128)S(1)}, u32[]{:S(2)}, u32[]{:S(2)}) collective-permute-start(f32[2,2,64,256]{3,2,0,1:T(8,128)S(1)} %get-tuple-element.263), channel_id=1, source_target_pairs={{0,8},{8,16},{16,24},{1,9},{9,17},{17,25},{2,10},{10,18},{18,26},{... | collective-permute-start | bytes 786440 | tf_op jit(solution)/shard_map/while/body/eval_jaxpr/ppermute | solution.py:12
  60.5 1.1 collective-permute-done
  61.6 1.0 copy_select_fusion.2
  62.6 8.0 %conditional.3 = (f32[2,2,64,256]{3,2,0,1:T(8,128)S(1)}, f32[1,64,256]{2,1,0:T(8,128)S(1)}) conditional(s32[]{:T(128)} %convert_element_type.20, f32[2,2,64,256]{3,2,0,1:T(8,128)S(1)} %copy_select_fusion.2, (f32[8,2,9,1,64,256]{5,4,3,2,1,0:T(8,128)}, s32[]{:T(128)}, f32[2,2,64,256]{3,2,0,1:T(8,128)S(1)}) %tuple.55), branch_computations={%region_1.1_spmd, %region_2.3_spmd} | conditional | flops 10752000 | bytes 36258320 | solution.py:88
  67.4 1.9 copy_bitcast_fusion
  70.6 4.1 %collective-permute-start = (f32[2,2,64,256]{3,2,0,1:T(8,128)S(1)}, f32[2,2,64,256]{3,2,0,1:T(8,128)S(1)}, u32[]{:S(2)}, u32[]{:S(2)}) collective-permute-start(f32[2,2,64,256]{3,2,0,1:T(8,128)S(1)} %get-tuple-element.263), channel_id=1, source_target_pairs={{0,8},{8,16},{16,24},{1,9},{9,17},{17,25},{2,10},{10,18},{18,26},{... | collective-permute-start | bytes 786440 | tf_op jit(solution)/shard_map/while/body/eval_jaxpr/ppermute | solution.py:12
  74.7 1.1 collective-permute-done
  76.8 8.0 %conditional.3 = (f32[2,2,64,256]{3,2,0,1:T(8,128)S(1)}, f32[1,64,256]{2,1,0:T(8,128)S(1)}) conditional(s32[]{:T(128)} %convert_element_type.20, f32[2,2,64,256]{3,2,0,1:T(8,128)S(1)} %copy_select_fusion.2, (f32[8,2,9,1,64,256]{5,4,3,2,1,0:T(8,128)}, s32[]{:T(128)}, f32[2,2,64,256]{3,2,0,1:T(8,128)S(1)}) %tuple.55), branch_computations={%region_1.1_spmd, %region_2.3_spmd} | conditional | flops 10752000 | bytes 36258320 | solution.py:88
  81.6 1.9 copy_bitcast_fusion
  84.8 6.6 %collective-permute-start = (f32[2,2,64,256]{3,2,0,1:T(8,128)S(1)}, f32[2,2,64,256]{3,2,0,1:T(8,128)S(1)}, u32[]{:S(2)}, u32[]{:S(2)}) collective-permute-start(f32[2,2,64,256]{3,2,0,1:T(8,128)S(1)} %get-tuple-element.263), channel_id=1, source_target_pairs={{0,8},{8,16},{16,24},{1,9},{9,17},{17,25},{2,10},{10,18},{18,26},{... | collective-permute-start | bytes 786440 | tf_op jit(solution)/shard_map/while/body/eval_jaxpr/ppermute | solution.py:12
  91.4 1.1 collective-permute-done
  93.5 14.5 %collective-permute-start = (f32[2,2,64,256]{3,2,0,1:T(8,128)S(1)}, f32[2,2,64,256]{3,2,0,1:T(8,128)S(1)}, u32[]{:S(2)}, u32[]{:S(2)}) collective-permute-start(f32[2,2,64,256]{3,2,0,1:T(8,128)S(1)} %get-tuple-element.263), channel_id=1, source_target_pairs={{0,8},{8,16},{16,24},{1,9},{9,17},{17,25},{2,10},{10,18},{18,26},{... | collective-permute-start | bytes 786440 | tf_op jit(solution)/shard_map/while/body/eval_jaxpr/ppermute | solution.py:12
  108.0 1.1 collective-permute-done
  109.1 1.0 copy_select_fusion.2
  110.2 6.6 %collective-permute-start = (f32[2,2,64,256]{3,2,0,1:T(8,128)S(1)}, f32[2,2,64,256]{3,2,0,1:T(8,128)S(1)}, u32[]{:S(2)}, u32[]{:S(2)}) collective-permute-start(f32[2,2,64,256]{3,2,0,1:T(8,128)S(1)} %get-tuple-element.263), channel_id=1, source_target_pairs={{0,8},{8,16},{16,24},{1,9},{9,17},{17,25},{2,10},{10,18},{18,26},{... | collective-permute-start | bytes 786440 | tf_op jit(solution)/shard_map/while/body/eval_jaxpr/ppermute | solution.py:12
  116.8 1.1 collective-permute-done
  118.9 14.5 %collective-permute-start = (f32[2,2,64,256]{3,2,0,1:T(8,128)S(1)}, f32[2,2,64,256]{3,2,0,1:T(8,128)S(1)}, u32[]{:S(2)}, u32[]{:S(2)}) collective-permute-start(f32[2,2,64,256]{3,2,0,1:T(8,128)S(1)} %get-tuple-element.263), channel_id=1, source_target_pairs={{0,8},{8,16},{16,24},{1,9},{9,17},{17,25},{2,10},{10,18},{18,26},{... | collective-permute-start | bytes 786440 | tf_op jit(solution)/shard_map/while/body/eval_jaxpr/ppermute | solution.py:12
  133.4 1.1 collective-permute-done
  135.2 76.8 %all-reduce.10.cloned.1.call-done = f32[1,64,256]{2,1,0:T(8,128)} async-done(((f32[1,64,256]{2,1,0:T(8,128)}), f32[1,64,256]{2,1,0:T(8,128)}) %all-reduce.10.cloned.1.call-update) | async-done | bytes 65552 | tf_op jit(solution)/shard_map/psum | solution.py:97
  212.0 1.5 broadcast_multiply_fusion
  (107 shorter events, 29.5 us)
Async XLA Ops:
  6.5 205.5 %all-reduce.10.cloned.1.call-start = ((), (), s32[]{:S(2)}) async-start(), calls=%async_computation | async-start | bytes 131072 | tf_op jit(solution)/shard_map/psum | solution.py:97
  46.8 2.4 %collective-permute-start = (f32[2,2,64,256]{3,2,0,1:T(8,128)S(1)}, f32[2,2,64,256]{3,2,0,1:T(8,128)S(1)}, u32[]{:S(2)}, u32[]{:S(2)}) collective-permute-start(f32[2,2,64,256]{3,2,0,1:T(8,128)S(1)} %get-tuple-element.263), channel_id=1, source_target_pairs={{0,8},{8,16},{16,24},{1,9},{9,17},{17,25},{2,10},{10,18},{18,26},{... | collective-permute-start | bytes 786440 | tf_op jit(solution)/shard_map/while/body/eval_jaxpr/ppermute | solution.py:12
  58.2 3.4 %collective-permute-start = (f32[2,2,64,256]{3,2,0,1:T(8,128)S(1)}, f32[2,2,64,256]{3,2,0,1:T(8,128)S(1)}, u32[]{:S(2)}, u32[]{:S(2)}) collective-permute-start(f32[2,2,64,256]{3,2,0,1:T(8,128)S(1)} %get-tuple-element.263), channel_id=1, source_target_pairs={{0,8},{8,16},{16,24},{1,9},{9,17},{17,25},{2,10},{10,18},{18,26},{... | collective-permute-start | bytes 786440 | tf_op jit(solution)/shard_map/while/body/eval_jaxpr/ppermute | solution.py:12
  70.6 5.2 %collective-permute-start = (f32[2,2,64,256]{3,2,0,1:T(8,128)S(1)}, f32[2,2,64,256]{3,2,0,1:T(8,128)S(1)}, u32[]{:S(2)}, u32[]{:S(2)}) collective-permute-start(f32[2,2,64,256]{3,2,0,1:T(8,128)S(1)} %get-tuple-element.263), channel_id=1, source_target_pairs={{0,8},{8,16},{16,24},{1,9},{9,17},{17,25},{2,10},{10,18},{18,26},{... | collective-permute-start | bytes 786440 | tf_op jit(solution)/shard_map/while/body/eval_jaxpr/ppermute | solution.py:12
  84.8 7.7 %collective-permute-start = (f32[2,2,64,256]{3,2,0,1:T(8,128)S(1)}, f32[2,2,64,256]{3,2,0,1:T(8,128)S(1)}, u32[]{:S(2)}, u32[]{:S(2)}) collective-permute-start(f32[2,2,64,256]{3,2,0,1:T(8,128)S(1)} %get-tuple-element.263), channel_id=1, source_target_pairs={{0,8},{8,16},{16,24},{1,9},{9,17},{17,25},{2,10},{10,18},{18,26},{... | collective-permute-start | bytes 786440 | tf_op jit(solution)/shard_map/while/body/eval_jaxpr/ppermute | solution.py:12
  93.5 15.6 %collective-permute-start = (f32[2,2,64,256]{3,2,0,1:T(8,128)S(1)}, f32[2,2,64,256]{3,2,0,1:T(8,128)S(1)}, u32[]{:S(2)}, u32[]{:S(2)}) collective-permute-start(f32[2,2,64,256]{3,2,0,1:T(8,128)S(1)} %get-tuple-element.263), channel_id=1, source_target_pairs={{0,8},{8,16},{16,24},{1,9},{9,17},{17,25},{2,10},{10,18},{18,26},{... | collective-permute-start | bytes 786440 | tf_op jit(solution)/shard_map/while/body/eval_jaxpr/ppermute | solution.py:12
  110.2 7.7 %collective-permute-start = (f32[2,2,64,256]{3,2,0,1:T(8,128)S(1)}, f32[2,2,64,256]{3,2,0,1:T(8,128)S(1)}, u32[]{:S(2)}, u32[]{:S(2)}) collective-permute-start(f32[2,2,64,256]{3,2,0,1:T(8,128)S(1)} %get-tuple-element.263), channel_id=1, source_target_pairs={{0,8},{8,16},{16,24},{1,9},{9,17},{17,25},{2,10},{10,18},{18,26},{... | collective-permute-start | bytes 786440 | tf_op jit(solution)/shard_map/while/body/eval_jaxpr/ppermute | solution.py:12
  118.9 15.6 %collective-permute-start = (f32[2,2,64,256]{3,2,0,1:T(8,128)S(1)}, f32[2,2,64,256]{3,2,0,1:T(8,128)S(1)}, u32[]{:S(2)}, u32[]{:S(2)}) collective-permute-start(f32[2,2,64,256]{3,2,0,1:T(8,128)S(1)} %get-tuple-element.263), channel_id=1, source_target_pairs={{0,8},{8,16},{16,24},{1,9},{9,17},{17,25},{2,10},{10,18},{18,26},{... | collective-permute-start | bytes 786440 | tf_op jit(solution)/shard_map/while/body/eval_jaxpr/ppermute | solution.py:12
  134.5 0.6 copy-start
Sparse Core Ops, SparseCore 0:
  135.3 76.6 all-reduce.9
where the time goes:
time: 221 us; the launch traced here: 220 us
  waiting for transfers between devices  84.5 us (38%)
  starting transfers between devices  49.8 us (23%)
  other arithmetic  33.5 us (15%)
  local copies, waits for them, and re-layouts  26.9 us (12%)
  between operations  13.4 us (6%)
  matrix products  11 us (5%)
    psum x1, waiting for transfers between devices, per_device(): summed = lax.psum(image_part, 'freq')  76.8 us
    ppermute x7, starting transfers between devices, shifted(): lax.ppermute(value, axis, [(source, source + steps) for source in range(l...  49.8 us
    unnamed x4, local copies, waits for them, and re-layouts  18.6 us
    add x32, other arithmetic, smooth(): 0.25 * padded[..., :-2, :] + 0.5 * padded[..., 1:-1, :]  12 us
    dot_general x1, matrix products, lookup(): jnp.dot(tap_part.reshape(-1, entries), one_hot, precision=lax.Precision.H...  11 us
    ppermute x7, waiting for transfers between devices, shifted(): lax.ppermute(value, axis, [(source, source + steps) for source in range(l...  7.69 us
    squeeze x4, local copies, waits for them, and re-layouts, run_slab(): wavefield = extrapolate(wavefield, coef_part[:, :, :, 0])  7.68 us
    select_n x7, other arithmetic, advance_section(): wavefield = jnp.where(depth_pos == 0, surface_part, incoming)  6.89 us
  transfers between devices with their start and end apart: 8, of which 8 were waited for; matrix products, arithmetic and copies ran while one was open for 0% of the time, Pallas kernels for 0%

commit v1 on v0

v1 whole, which is shorter than its diff:
```python
import functools
import math

import jax
import jax.numpy as jnp
from jax import lax
from jax.experimental import pallas as pl
from jax.experimental.pallas import tpu as pltpu
from jax.sharding import PartitionSpec as P

SUB = 8
LANES = 128


def exchange(value, axis, distance):
    count = lax.axis_size(axis)
    return lax.ppermute(value, axis, [(i, i ^ distance) for i in range(count)])


def lane_take(vector, index):
    return jnp.take_along_axis(vector, index, axis=1, mode="promise_in_bounds")


def split_lanes(low, high, index, first_half):
    even = jnp.where(first_half, lane_take(low, index), lane_take(high, index))
    odd = jnp.where(first_half, lane_take(low, index + 1), lane_take(high, index + 1))
    return even, odd


def join_lanes(even, odd, index, is_even):
    low = jnp.where(is_even, lane_take(even, index), lane_take(odd, index))
    high = jnp.where(is_even, lane_take(even, index + LANES // 2), lane_take(odd, index + LANES // 2))
    return low, high


def column(value, rows):
    return [jnp.broadcast_to(value[r : r + 1], (SUB, LANES)) for r in rows]


def image_kernel(
    sizes, scale, slot_ref, surface_ref, tap_ref, *refs
):
    count, local_count, depth_count, levels, terms, entries, vel_count = sizes
    vel_refs = refs[:vel_count]
    keep_ref, send_ref, raw, raw_sem, halves, halves_i, index_ref, table, state, basis = refs[vel_count:]
    depth_pos = lax.axis_index("depth")
    members = [jnp.minimum(depth_pos * count + j, local_count - 1) for j in range(count)]
    copies = [
        pltpu.make_async_copy(surface_ref.at[members[j]], raw.at[j], raw_sem.at[j]) for j in range(count)
    ]
    for copy in copies:
        copy.start()

    lane = lax.broadcasted_iota(jnp.int32, (SUB, LANES), 1)
    row = lax.broadcasted_iota(jnp.int32, (SUB, LANES), 0)
    half = LANES // 2
    first_half = lane < half
    split_index = jnp.where(first_half, 2 * lane, 2 * lane - LANES)
    is_even = lane % 2 == 0
    join_index = lane // 2
    not_first = (lane > 0).astype(jnp.float32)
    not_last = (lane < LANES - 1).astype(jnp.float32)
    not_top = (row > 0).astype(jnp.float32)
    not_bottom = (row < SUB - 1).astype(jnp.float32)

    table_freqs = tap_ref.shape[1]
    freq_lane = lax.broadcasted_iota(jnp.int32, (SUB, table_freqs), 1)
    freq_row = lax.broadcasted_iota(jnp.int32, (SUB, table_freqs), 0)
    wanted = jnp.zeros((SUB, table_freqs), jnp.int32)
    for j in range(count):
        wanted = jnp.where(freq_row == j, slot_ref[members[j]], wanted)
    picked = lax.dot_general(
        (freq_lane == wanted).astype(jnp.float32),
        tap_ref[...],
        (((1,), (1,)), ((), ())),
        precision=lax.Precision.HIGHEST,
        preferred_element_type=jnp.float32,
    )
    per_vector = LANES // entries
    for j in range(count):
        for c in range(2):
            for k in range(terms):
                place = c * terms + k
                vector = place // per_vector
                whole = picked[:, vector * LANES : (vector + 1) * LANES]
                if whole.shape[1] < LANES:
                    whole = jnp.concatenate(
                        [whole, jnp.zeros((SUB, LANES - whole.shape[1]), jnp.float32)], axis=1
                    )
                turn = (place % per_vector) * entries
                if turn:
                    whole = pltpu.roll(whole, LANES - turn, 1)
                table[j, c, k] = jnp.broadcast_to(whole[j : j + 1], (SUB, LANES))

    slot = 0
    for vel_ref in vel_refs:
        for part in range(vel_ref.shape[0] // levels):
            target = jnp.bitwise_xor(depth_pos, slot)
            for level in range(levels):
                for h in range(2):
                    halves_i[h] = vel_ref[part * levels + level, :, h * LANES : (h + 1) * LANES]
                for x in range(SUB):
                    low, high = [halves_i[h, pl.ds(x, SUB, stride=SUB)] for h in range(2)]
                    even, odd = split_lanes(low, high, split_index, first_half)
                    index_ref[target * levels + level, x, 0] = even
                    index_ref[target * levels + level, x, 1] = odd
            slot += 1

    for j in range(count):
        copies[j].wait()
        valid = depth_pos * count + j < local_count
        for c in range(2):
            for h in range(2):
                halves[h] = raw[j, c, :, h * LANES : (h + 1) * LANES]
            for x in range(SUB):
                low, high = [halves[h, pl.ds(x, SUB, stride=SUB)] for h in range(2)]
                even, odd = split_lanes(low, high, split_index, first_half)
                state[j, c, x, 0] = jnp.where(valid, even, 0.0)
                state[j, c, x, 1] = jnp.where(valid, odd, 0.0)

    def spread(value):
        summed = []
        for p in range(2):
            u = [value[x][p] for x in range(SUB)]
            before = pltpu.roll(u[SUB - 1], 1, 0) * not_top
            after = pltpu.roll(u[0], SUB - 1, 0) * not_bottom
            line = [before] + u + [after]
            pairs = [line[i] + line[i + 1] for i in range(SUB + 1)]
            summed.append([pairs[i] + pairs[i + 1] for i in range(SUB)])
        out = []
        for x in range(SUB):
            even, odd = summed[0][x], summed[1][x]
            both = even + odd
            out.append(
                (
                    both + (even + pltpu.roll(odd, 1, 1) * not_first),
                    both + (odd + pltpu.roll(even, LANES - 1, 1) * not_last),
                )
            )
        return out

    def depth_step(z, carry):
        for j in range(count):
            for c in range(2):
                current = [[state[j, c, x, p] for p in range(2)] for x in range(SUB)]
                sums = None
                for k in range(1, terms):
                    wide = spread(current)
                    if k == 1:
                        sums = [[0.125 * wide[x][p] for p in range(2)] for x in range(SUB)]
                    else:
                        sums = [[0.25 * wide[x][p] - sums[x][p] for p in range(2)] for x in range(SUB)]
                    current = [[sums[x][p] - current[x][p] for p in range(2)] for x in range(SUB)]
                    for x in range(SUB):
                        for p in range(2):
                            basis[j, c, k - 1, x, p] = current[x][p]
        for x in range(SUB):
            layers = []
            for p in range(2):
                index = index_ref[z, x, p]
                layer = None
                for j in range(count):
                    real = imag = None
                    for k in range(terms):
                        coef_r = lane_take(table[j, 0, k], index)
                        coef_i = lane_take(table[j, 1, k], index)
                        if k == 0:
                            field_r, field_i = state[j, 0, x, p], state[j, 1, x, p]
                            real = coef_r * field_r - coef_i * field_i
                            imag = coef_r * field_i + coef_i * field_r
                        else:
                            field_r, field_i = basis[j, 0, k - 1, x, p], basis[j, 1, k - 1, x, p]
                            real = real + coef_r * field_r - coef_i * field_i
                            imag = imag + coef_r * field_i + coef_i * field_r
                    state[j, 0, x, p] = real
                    state[j, 1, x, p] = imag
                    layer = real if layer is None else layer + real
                layers.append(layer * scale)
            low, high = join_lanes(layers[0], layers[1], join_index, is_even)
            halves[0, pl.ds(x, SUB, stride=SUB)] = low
            halves[1, pl.ds(x, SUB, stride=SUB)] = high
        place = jnp.bitwise_xor(z // levels, depth_pos)
        level = z % levels

        def put(ref):
            at = (place // 2) * levels + level
            for h in range(2):
                ref[at, :, h * LANES : (h + 1) * LANES] = halves[h]

        pl.when(place % 2 == 0)(functools.partial(put, keep_ref))
        pl.when(place % 2 == 1)(functools.partial(put, send_ref))
        return carry

    lax.fori_loop(0, depth_count * levels, depth_step, 0)


def per_device(surface, freq_slot, tap_table, vel_index):
    local_count, _, rows, columns = surface.shape
    depth_count = lax.axis_size("depth")
    freq_count = lax.axis_size("freq")
    levels = vel_index.shape[0]
    _, terms, entries, table_freqs = tap_table.shape
    count = -(-local_count // depth_count)

    vel_parts = vel_index
    distance = 1
    order = []
    while distance < depth_count:
        order.append(distance)
        distance *= 2
    vel_parts = vel_index
    for distance in order:
        vel_parts = jnp.concatenate([vel_parts, exchange(vel_parts, "depth", distance)], axis=0)
    vels = [vel_parts]

    scale = 1.0 / math.sqrt(local_count * freq_count)
    sizes = (count, local_count, depth_count, levels, terms, entries, len(vels))
    half = jax.ShapeDtypeStruct((depth_count // 2 * levels, rows, columns), jnp.float32)
    vmem = pl.BlockSpec(memory_space=pltpu.VMEM)
    keep, send = pl.pallas_call(
        functools.partial(image_kernel, sizes, scale),
        out_shape=(half, half),
        in_specs=[
            pl.BlockSpec(memory_space=pltpu.SMEM),
            pl.BlockSpec(memory_space=pl.ANY),
            vmem,
        ]
        + [vmem] * len(vels),
        out_specs=(vmem, vmem),
        scratch_shapes=[
            pltpu.VMEM((count, 2, rows, columns), jnp.float32),
            pltpu.SemaphoreType.DMA((count,)),
            pltpu.VMEM((2, rows, LANES), jnp.float32),
            pltpu.VMEM((2, rows, LANES), jnp.int32),
            pltpu.VMEM((depth_count * levels, SUB, 2, SUB, LANES), jnp.int32),
            pltpu.VMEM((count, 2, terms, SUB, LANES), jnp.float32),
            pltpu.VMEM((count, 2, SUB, 2, SUB, LANES), jnp.float32),
            pltpu.VMEM((count, 2, terms - 1, SUB, 2, SUB, LANES), jnp.float32),
        ],
        compiler_params=pltpu.CompilerParams(vmem_limit_bytes=32 * 1024 * 1024),
    )(freq_slot, surface, tap_table.reshape(2 * terms * entries, table_freqs), *vels)

    image = keep + exchange(send, "depth", 1)
    distance = 2
    while distance < depth_count:
        image = image.reshape((-1, 2, levels, rows, columns))
        image = (image[:, 0] + exchange(image[:, 1], "depth", distance)).reshape((-1, rows, columns))
        distance *= 2
    distance = 1
    while distance < freq_count:
        image = image + exchange(image, "freq", distance)
        distance *= 2
    return image


def solution(mesh):
    in_specs = (P("freq", None, None, None), P("freq"), P(), P("depth", None, None))
    out_specs = P("depth", None, None)
    return jax.shard_map(
        per_device, mesh=mesh, in_specs=in_specs, out_specs=out_specs, check_vma=False
    )
```

time: 221 us -> 44.1 us (0.20)
  waiting for transfers between devices: 84.5 us -> 16.1 us
  starting transfers between devices: 49.8 us -> 12.4 us
  other arithmetic: 33.5 us -> 1.55 us
  local copies, waits for them, and re-layouts: 26.9 us -> 1.88 us
  between operations: 13.4 us -> 0.08 us
  Pallas kernels: 0 us -> 11.8 us
  matrix products: 11 us -> 0 us
    psum x1 -> x0, waiting for transfers between devices: 76.8 us -> none  [per_device(): summed = lax.psum(image_part, 'freq')]
    ppermute x7, starting transfers between devices: 49.8 us -> 12.4 us  [exchange(): return lax.ppermute(value, axis, [(i, i ^ distance) for i in range(count)])]
    unnamed x4 -> x8, local copies, waits for them, and re-layouts: 18.6 us -> 1.87 us
    add x43 -> x3, other arithmetic: 13.7 us -> 0.66 us  [per_device(): image = image + exchange(image, 'freq', distance)]
    pallas_call x0 -> x1, Pallas kernels: none -> 11.8 us  [per_device(): pl.pallas_call(functools.partial(image_kernel, sizes, scale), out_shape=(...]
    dot_general x1 -> x0, matrix products: 11 us -> none  [lookup(): jnp.dot(tap_part.reshape(-1, entries), one_hot, precision=lax.Precision.H...]
    ppermute x7, waiting for transfers between devices: 7.69 us -> 16.1 us  [exchange(): return lax.ppermute(value, axis, [(i, i ^ distance) for i in range(count)])]
    sub x36 -> x0, other arithmetic: 8.32 us -> none  [the longest x28 5.92 us: extrapolate(): earlier, current = (current, 2.0 * mcclellan(current) - earlier)]
  transfers between devices with their start and end apart: 8 -> 7, of which waited for: 8 -> 7; matrix products, arithmetic and copies ran while one was open for 0% -> 0% of each run, Pallas kernels for 0% -> 0%
where the time goes in v1:
time: 44.1 us; the launch traced here: 43.9 us
  waiting for transfers between devices  16.1 us (37%)
  starting transfers between devices  12.4 us (28%)
  Pallas kernels  11.8 us (27%)
  local copies, waits for them, and re-layouts  1.88 us (4%)
  other arithmetic  1.55 us (4%)
    ppermute x7, waiting for transfers between devices, exchange(): return lax.ppermute(value, axis, [(i, i ^ distance) for i in range(count)])  16.1 us
    ppermute x7, starting transfers between devices, exchange(): return lax.ppermute(value, axis, [(i, i ^ distance) for i in range(count)])  12.4 us
    pallas_call x1, Pallas kernels, per_device(): pl.pallas_call(functools.partial(image_kernel, sizes, scale), out_shape=(...  11.8 us
    unnamed x8, local copies, waits for them, and re-layouts  1.87 us
  transfers between devices with their start and end apart: 7, of which 7 were waited for; matrix products, arithmetic and copies ran while one was open for 0% of the time, Pallas kernels for 0%

profile of v1, /device:TPU:0, one launch (start us, length us, event | category | flops | bytes accessed | tf_op | source)
XLA Modules:
  0.0 43.9 jit_solution(14776938853982297790)
XLA Ops:
  0.0 0.0 copy-start.3
  0.0 0.5 %collective-permute-start = (s32[1,64,256]{2,1,0:T(8,128)}, s32[1,64,256]{2,1,0:T(8,128)S(1)}, u32[]{:S(2)}, u32[]{:S(2)}) collective-permute-start(s32[1,64,256]{2,1,0:T(8,128)} %param.7), channel_id=1, source_target_pairs={{0,8},{8,0},{16,24},{24,16},{1,9},{9,1},{17,25},{25,17},{2,10},{10... | collective-permute-start | bytes 196616 | tf_op jit(solution)/shard_map/ppermute | solution.py:17
  0.5 1.1 %collective-permute-done = s32[1,64,256]{2,1,0:T(8,128)S(1)} collective-permute-done((s32[1,64,256]{2,1,0:T(8,128)}, s32[1,64,256]{2,1,0:T(8,128)S(1)}, u32[]{:S(2)}, u32[]{:S(2)}) %collective-permute-start) | collective-permute-done | bytes 65568 | tf_op jit(solution)/shard_map/ppermute | solution.py:17
  1.6 0.8 %pad_add_fusion.1 = s32[2,64,256]{2,1,0:T(8,128)S(1)} fusion(s32[1,64,256]{2,1,0:T(8,128)S(1)} %collective-permute-done, s32[1,64,256]{2,1,0:T(8,128)} %param.7), kind=kLoop, calls=%fused_computation.1 | loop fusion | flops 32768 | bytes 262144 | tf_op jit(solution)/shard_map/concatenate | solution.py:213
  2.4 0.0 copy-start.1
  2.4 2.9 %collective-permute-start.1 = (s32[2,64,256]{2,1,0:T(8,128)S(1)}, s32[2,64,256]{2,1,0:T(8,128)S(1)}, u32[]{:S(2)}, u32[]{:S(2)}) collective-permute-start(s32[2,64,256]{2,1,0:T(8,128)S(1)} %pad_add_fusion.1), channel_id=1, source_target_pairs={{0,16},{8,24},{16,0},{24,8},{1,17},{9,25},{17,1},{25,9},{2,18},{10... | collective-permute-start | bytes 393224 | tf_op jit(solution)/shard_map/ppermute | solution.py:17
  5.4 3.8 %collective-permute-done.1 = s32[2,64,256]{2,1,0:T(8,128)S(1)} collective-permute-done((s32[2,64,256]{2,1,0:T(8,128)S(1)}, s32[2,64,256]{2,1,0:T(8,128)S(1)}, u32[]{:S(2)}, u32[]{:S(2)}) %collective-permute-start.1) | collective-permute-done | bytes 131104 | tf_op jit(solution)/shard_map/ppermute | solution.py:17
  9.2 0.0 copy-done.3
  9.2 0.0 copy-start.2
  9.2 0.0 copy-done.1
  9.2 0.6 %copy-done.2 = s32[8]{0:T(128)S(1)} copy-done((s32[8]{0:T(128)S(1)}, s32[8]{0:T(128)}, u32[]{:S(2)}) %copy-start.2) | copy-done | bytes 56
  9.9 0.0 copy-start
  9.9 1.2 %copy-done = f32[8,2,64,256]{3,2,1,0:T(8,128)S(1)} copy-done((f32[8,2,64,256]{3,2,1,0:T(8,128)S(1)}, f32[8,2,64,256]{3,2,1,0:T(8,128)}, u32[]{:S(2)}) %copy-start) | copy-done | bytes 1048600
  11.1 11.8 %shard_map.46 = (f32[2,64,256]{2,1,0:T(8,128)S(1)}, f32[2,64,256]{2,1,0:T(8,128)S(1)}) custom-call(s32[8]{0:T(128)S(1)} %copy-done.2, f32[8,2,64,256]{3,2,1,0:T(8,128)S(1)} %copy-done, f32[576,64]{1,0:T(8,128)S(1)} %bitcast.16, s32[4,64,256]{2,1,0:T(8,128)S(1)} %pad_add_fusion.refs_0_), custom_call_target="tpu_custom_call" | custom-call | tf_op jit(solution)/shard_map/pallas_call | solution.py:220
  22.9 0.1 collective-permute-start.2
  23.0 1.3 %collective-permute-done.2 = f32[2,64,256]{2,1,0:T(8,128)S(1)} collective-permute-done((f32[2,64,256]{2,1,0:T(8,128)S(1)}, f32[2,64,256]{2,1,0:T(8,128)S(1)}, u32[]{:S(2)}, u32[]{:S(2)}) %collective-permute-start.2) | collective-permute-done | bytes 131104 | tf_op jit(solution)/shard_map/ppermute | solution.py:17
  24.4 1.8 %collective-permute-start.3 = (f32[1,1,64,256]{3,2,1,0:T(8,128)S(1)}, f32[1,1,64,256]{3,2,1,0:T(8,128)S(1)}, u32[]{:S(2)}, u32[]{:S(2)}) collective-permute-start(f32[1,1,64,256]{3,2,1,0:T(8,128)S(1)} %slice_bitcast_fusion), channel_id=1, source_target_pairs={{0,16},{8,24},{16,0},{24,8},{1,17},{9,25},{17,1},{25,9},{2,18},{10... | collective-permute-start | bytes 196616 | tf_op jit(solution)/shard_map/ppermute | solution.py:17
  26.2 2.5 %collective-permute-done.3 = f32[1,1,64,256]{3,2,1,0:T(8,128)S(1)} collective-permute-done((f32[1,1,64,256]{3,2,1,0:T(8,128)S(1)}, f32[1,1,64,256]{3,2,1,0:T(8,128)S(1)}, u32[]{:S(2)}, u32[]{:S(2)}) %collective-permute-start.3) | collective-permute-done | bytes 65568 | tf_op jit(solution)/shard_map/ppermute | solution.py:17
  28.7 1.8 %collective-permute-start.4 = (f32[1,64,256]{2,1,0:T(8,128)S(1)}, f32[1,64,256]{2,1,0:T(8,128)S(1)}, u32[]{:S(2)}, u32[]{:S(2)}) collective-permute-start(f32[1,64,256]{2,1,0:T(8,128)S(1)} %fusion.1), channel_id=1, source_target_pairs={{0,1},{1,0},{2,3},{3,2},{4,5},{5,4},{6,7},{7,6},{8,9},{9,8},{10,11... | collective-permute-start | bytes 196616 | tf_op jit(solution)/shard_map/ppermute | solution.py:17
  30.5 2.6 %collective-permute-done.4 = f32[1,64,256]{2,1,0:T(8,128)S(1)} collective-permute-done((f32[1,64,256]{2,1,0:T(8,128)S(1)}, f32[1,64,256]{2,1,0:T(8,128)S(1)}, u32[]{:S(2)}, u32[]{:S(2)}) %collective-permute-start.4) | collective-permute-done | bytes 65568 | tf_op jit(solution)/shard_map/ppermute | solution.py:17
  33.1 1.9 %collective-permute-start.5 = (f32[1,64,256]{2,1,0:T(8,128)S(1)}, f32[1,64,256]{2,1,0:T(8,128)S(1)}, u32[]{:S(2)}, u32[]{:S(2)}) collective-permute-start(f32[1,64,256]{2,1,0:T(8,128)S(1)} %add.17), channel_id=1, source_target_pairs={{0,2},{1,3},{2,0},{3,1},{4,6},{5,7},{6,4},{7,5},{8,10},{9,11},{10,... | collective-permute-start | bytes 196616 | tf_op jit(solution)/shard_map/ppermute | solution.py:17
  34.9 2.5 %collective-permute-done.5 = f32[1,64,256]{2,1,0:T(8,128)S(1)} collective-permute-done((f32[1,64,256]{2,1,0:T(8,128)S(1)}, f32[1,64,256]{2,1,0:T(8,128)S(1)}, u32[]{:S(2)}, u32[]{:S(2)}) %collective-permute-start.5) | collective-permute-done | bytes 65568 | tf_op jit(solution)/shard_map/ppermute | solution.py:17
  37.4 3.5 %collective-permute-start.6 = (f32[1,64,256]{2,1,0:T(8,128)S(1)}, f32[1,64,256]{2,1,0:T(8,128)S(1)}, u32[]{:S(2)}, u32[]{:S(2)}) collective-permute-start(f32[1,64,256]{2,1,0:T(8,128)S(1)} %add.18), channel_id=1, source_target_pairs={{0,4},{1,5},{2,6},{3,7},{4,0},{5,1},{6,2},{7,3},{8,12},{9,13},{10,... | collective-permute-start | bytes 196616 | tf_op jit(solution)/shard_map/ppermute | solution.py:17
  41.0 2.3 %collective-permute-done.6 = f32[1,64,256]{2,1,0:T(8,128)S(1)} collective-permute-done((f32[1,64,256]{2,1,0:T(8,128)S(1)}, f32[1,64,256]{2,1,0:T(8,128)S(1)}, u32[]{:S(2)}, u32[]{:S(2)}) %collective-permute-start.6) | collective-permute-done | bytes 65568 | tf_op jit(solution)/shard_map/ppermute | solution.py:17
  43.2 0.6 %add.19 = f32[1,64,256]{2,1,0:T(8,128)} add(f32[1,64,256]{2,1,0:T(8,128)S(1)} %add.18, f32[1,64,256]{2,1,0:T(8,128)S(1)} %collective-permute-done.6) | non-fusion elementwise | flops 16384 | bytes 196608 | tf_op jit(solution)/shard_map/add | solution.py:251
  (6 shorter events, 0.1 us)
Async XLA Ops:
  0.0 9.2 %copy-start.3 = (s32[1,64,256]{2,1,0:T(8,128)S(1)}, s32[1,64,256]{2,1,0:T(8,128)}, u32[]{:S(2)}) copy-start(s32[1,64,256]{2,1,0:T(8,128)} %param.7) | copy-start | bytes 196612
  0.0 1.6 %collective-permute-start = (s32[1,64,256]{2,1,0:T(8,128)}, s32[1,64,256]{2,1,0:T(8,128)S(1)}, u32[]{:S(2)}, u32[]{:S(2)}) collective-permute-start(s32[1,64,256]{2,1,0:T(8,128)} %param.7), channel_id=1, source_target_pairs={{0,8},{8,0},{16,24},{24,16},{1,9},{9,1},{17,25},{25,17},{2,10},{10... | collective-permute-start | bytes 196616 | tf_op jit(solution)/shard_map/ppermute | solution.py:17
  2.4 6.8 %copy-start.1 = (f32[2,9,32,64]{3,2,1,0:T(8,128)S(1)}, f32[2,9,32,64]{3,2,1,0:T(8,128)}, u32[]{:S(2)}) copy-start(f32[2,9,32,64]{3,2,1,0:T(8,128)} %param.6) | copy-start | bytes 442372
  2.4 6.8 %collective-permute-start.1 = (s32[2,64,256]{2,1,0:T(8,128)S(1)}, s32[2,64,256]{2,1,0:T(8,128)S(1)}, u32[]{:S(2)}, u32[]{:S(2)}) collective-permute-start(s32[2,64,256]{2,1,0:T(8,128)S(1)} %pad_add_fusion.1), channel_id=1, source_target_pairs={{0,16},{8,24},{16,0},{24,8},{1,17},{9,25},{17,1},{25,9},{2,18},{10... | collective-permute-start | bytes 393224 | tf_op jit(solution)/shard_map/ppermute | solution.py:17
  9.2 0.7 %copy-start.2 = (s32[8]{0:T(128)S(1)}, s32[8]{0:T(128)}, u32[]{:S(2)}) copy-start(s32[8]{0:T(128)} %slot_ref.1) | copy-start | bytes 100
  9.9 1.2 %copy-start = (f32[8,2,64,256]{3,2,1,0:T(8,128)S(1)}, f32[8,2,64,256]{3,2,1,0:T(8,128)}, u32[]{:S(2)}) copy-start(f32[8,2,64,256]{3,2,1,0:T(8,128)} %surface_ref.1) | copy-start | bytes 3145732
  22.9 1.4 %collective-permute-start.2 = (f32[2,64,256]{2,1,0:T(8,128)S(1)}, f32[2,64,256]{2,1,0:T(8,128)S(1)}, u32[]{:S(2)}, u32[]{:S(2)}) collective-permute-start(f32[2,64,256]{2,1,0:T(8,128)S(1)} %get-tuple-element.8), channel_id=1, source_target_pairs={{0,8},{8,0},{16,24},{24,16},{1,9},{9,1},{17,25},{25,17},{2,10},{10... | collective-permute-start | bytes 393224 | tf_op jit(solution)/shard_map/ppermute | solution.py:17
  24.4 4.3 %collective-permute-start.3 = (f32[1,1,64,256]{3,2,1,0:T(8,128)S(1)}, f32[1,1,64,256]{3,2,1,0:T(8,128)S(1)}, u32[]{:S(2)}, u32[]{:S(2)}) collective-permute-start(f32[1,1,64,256]{3,2,1,0:T(8,128)S(1)} %slice_bitcast_fusion), channel_id=1, source_target_pairs={{0,16},{8,24},{16,0},{24,8},{1,17},{9,25},{17,1},{25,9},{2,18},{10... | collective-permute-start | bytes 196616 | tf_op jit(solution)/shard_map/ppermute | solution.py:17
  28.7 4.3 %collective-permute-start.4 = (f32[1,64,256]{2,1,0:T(8,128)S(1)}, f32[1,64,256]{2,1,0:T(8,128)S(1)}, u32[]{:S(2)}, u32[]{:S(2)}) collective-permute-start(f32[1,64,256]{2,1,0:T(8,128)S(1)} %fusion.1), channel_id=1, source_target_pairs={{0,1},{1,0},{2,3},{3,2},{4,5},{5,4},{6,7},{7,6},{8,9},{9,8},{10,11... | collective-permute-start | bytes 196616 | tf_op jit(solution)/shard_map/ppermute | solution.py:17
  33.1 4.3 %collective-permute-start.5 = (f32[1,64,256]{2,1,0:T(8,128)S(1)}, f32[1,64,256]{2,1,0:T(8,128)S(1)}, u32[]{:S(2)}, u32[]{:S(2)}) collective-permute-start(f32[1,64,256]{2,1,0:T(8,128)S(1)} %add.17), channel_id=1, source_target_pairs={{0,2},{1,3},{2,0},{3,1},{4,6},{5,7},{6,4},{7,5},{8,10},{9,11},{10,... | collective-permute-start | bytes 196616 | tf_op jit(solution)/shard_map/ppermute | solution.py:17
  37.4 5.8 %collective-permute-start.6 = (f32[1,64,256]{2,1,0:T(8,128)S(1)}, f32[1,64,256]{2,1,0:T(8,128)S(1)}, u32[]{:S(2)}, u32[]{:S(2)}) collective-permute-start(f32[1,64,256]{2,1,0:T(8,128)S(1)} %add.18), channel_id=1, source_target_pairs={{0,4},{1,5},{2,6},{3,7},{4,0},{5,1},{6,2},{7,3},{8,12},{9,13},{10,... | collective-permute-start | bytes 196616 | tf_op jit(solution)/shard_map/ppermute | solution.py:17

commit v2 on v0

v2 whole, which is shorter than its diff:
```python
import functools
import math

import jax
import jax.numpy as jnp
from jax import lax
from jax.experimental import pallas as pl
from jax.experimental.pallas import tpu as pltpu
from jax.sharding import PartitionSpec as P

SUB = 8
LANES = 128
PAIR = 2
QUAD = 4
ENTRY_SPAN = LANES // PAIR


def exchange(value, axis, flip):
    count = lax.axis_size(axis)
    return lax.ppermute(value, axis, [(i, i ^ flip) for i in range(count)])


def lane_take(vector, index):
    return jnp.take_along_axis(vector, index, axis=1, mode="promise_in_bounds")


def lane_number():
    return lax.broadcasted_iota(jnp.int32, (SUB, LANES), 1)


def edge_masks():
    lane = lane_number() % ENTRY_SPAN
    row = lax.broadcasted_iota(jnp.int32, (SUB, LANES), 0)
    return (
        (lane > 0).astype(jnp.float32),
        (lane < ENTRY_SPAN - 1).astype(jnp.float32),
        (row > 0).astype(jnp.float32),
        (row < SUB - 1).astype(jnp.float32),
    )


def chebyshev(start, terms, masks, put):
    left_mask, right_mask, top_mask, bottom_mask = masks
    current, sums = start, None
    for k in range(1, terms):
        lines = []
        for y in range(QUAD):
            column = [current[x][y] for x in range(SUB)]
            above = pltpu.roll(column[SUB - 1], 1, 0) * top_mask
            below = pltpu.roll(column[0], SUB - 1, 0) * bottom_mask
            lines.append([above] + column + [below])
        pairs = [lines[y][0] + lines[y][1] for y in range(QUAD)]
        following, following_sums = [], []
        for x in range(SUB):
            later = [lines[y][x + 1] + lines[y][x + 2] for y in range(QUAD)]
            line = [pairs[y] + later[y] for y in range(QUAD)]
            pairs = later
            left = pltpu.roll(line[QUAD - 1], 1, 1) * left_mask
            right = pltpu.roll(line[0], LANES - 1, 1) * right_mask
            line = [left] + line + [right]
            sides = [line[i] + line[i + 1] for i in range(QUAD + 1)]
            new, new_sums = [], []
            for y in range(QUAD):
                wide = sides[y] + sides[y + 1]
                total = 0.125 * wide if k == 1 else 0.25 * wide - sums[x][y]
                value = total - current[x][y]
                put(k, x, y, value)
                new.append(value)
                new_sums.append(total)
            following.append(new)
            following_sums.append(new_sums)
        current, sums = following, following_sums


def split_index(y):
    return (lane_number() % (LANES // QUAD)) * QUAD + y


def first_kernel(sizes, slot_ref, surface_ref, tap_ref, table_ref, basis_ref, raw, raw_sem, halves):
    groups, count, local_count, terms, entries = sizes
    first = lax.axis_index("depth") * count
    members = [jnp.minimum(first + j, local_count - 1) for j in range(count)]
    copies = [pltpu.make_async_copy(surface_ref.at[members[j]], raw.at[j], raw_sem.at[j]) for j in range(count)]
    for copy in copies:
        copy.start()

    table_freqs = tap_ref.shape[1]
    rows = -(-count // SUB) * SUB
    freq_lane = lax.broadcasted_iota(jnp.int32, (rows, table_freqs), 1)
    freq_row = lax.broadcasted_iota(jnp.int32, (rows, table_freqs), 0)
    wanted = jnp.zeros((rows, table_freqs), jnp.int32)
    for j in range(count):
        wanted = jnp.where(freq_row == j, slot_ref[members[j]], wanted)
    picked = lax.dot_general(
        (freq_lane == wanted).astype(jnp.float32),
        tap_ref[...],
        (((1,), (1,)), ((), ())),
        precision=lax.Precision.HIGHEST,
        preferred_element_type=jnp.float32,
    )
    lane = lane_number()
    per_vector = LANES // entries
    for g in range(groups):
        for c in range(2):
            for k in range(terms):
                place = c * terms + k
                vector = place // per_vector
                whole = picked[:, vector * LANES : (vector + 1) * LANES]
                if whole.shape[1] < LANES:
                    whole = jnp.concatenate([whole, jnp.zeros((rows, LANES - whole.shape[1]), jnp.float32)], axis=1)
                sides = []
                for i in range(PAIR):
                    turn = ((place % per_vector) * entries - i * ENTRY_SPAN) % LANES
                    turned = pltpu.roll(whole, LANES - turn, 1) if turn else whole
                    j = min(g * PAIR + i, count - 1)
                    sides.append(jnp.broadcast_to(turned[j : j + 1], (SUB, LANES)))
                table_ref[g, c, k] = jnp.where(lane < ENTRY_SPAN, sides[0], sides[1])

    for copy in copies:
        copy.wait()
    masks = edge_masks()
    in_low = lane % ENTRY_SPAN < ENTRY_SPAN // 2
    for g in range(groups):
        for c in range(2):
            for i in range(PAIR):
                j = min(g * PAIR + i, count - 1)
                for h in range(2):
                    halves[i, h] = raw[j, c, :, h * LANES : (h + 1) * LANES]
            start = []
            for x in range(SUB):
                line = []
                for y in range(QUAD):
                    index = split_index(y)
                    sides = []
                    for i in range(PAIR):
                        low, high = [lane_take(halves[i, h, pl.ds(x, SUB, stride=SUB)], index) for h in range(2)]
                        side = jnp.where(in_low, low, high)
                        j = g * PAIR + i
                        if j >= count:
                            side = jnp.zeros_like(side)
                        elif count * lax.axis_size("depth") > local_count:
                            side = jnp.where(first + j < local_count, side, 0.0)
                        sides.append(side)
                    value = jnp.where(lane < ENTRY_SPAN, sides[0], sides[1])
                    basis_ref[g, 0, c, x, y] = value
                    line.append(value)
                start.append(line)

            def put(k, x, y, value):
                basis_ref[g, k, c, x, y] = value

            chebyshev(start, terms, masks, put)


def image_kernel(sizes, scale, table_ref, first_ref, *refs):
    groups, depth_count, levels, terms = sizes
    vel_refs = refs[:depth_count]
    keep_ref, send_ref, halves, halves_i, index_ref, basis = refs[depth_count:]
    depth_pos = lax.axis_index("depth")
    depths = depth_count * levels
    lane = lane_number()
    in_low = lane % ENTRY_SPAN < ENTRY_SPAN // 2
    masks = edge_masks()

    table_base = jnp.where(lane < ENTRY_SPAN, 0, ENTRY_SPAN)
    for slot, vel_ref in enumerate(vel_refs):
        target = jnp.bitwise_xor(depth_pos, slot) * levels
        for level in range(levels):
            for h in range(2):
                halves_i[h] = vel_ref[level, :, h * LANES : (h + 1) * LANES]
            for x in range(SUB):
                low, high = [halves_i[h, pl.ds(x, SUB, stride=SUB)] for h in range(2)]
                for y in range(QUAD):
                    index = split_index(y)
                    entry = jnp.where(in_low, lane_take(low, index), lane_take(high, index))
                    index_ref[target + level, x, y] = entry + table_base

    low_index = lane // QUAD
    quarter = lane % QUAD

    def accumulate(z, source):
        for x in range(SUB):
            layers = []
            for y in range(QUAD):
                index = index_ref[z, x, y]
                layer = None
                for g in range(groups):
                    real = imag = None
                    for k in range(terms):
                        coef_r = lane_take(table_ref[g, 0, k], index)
                        coef_i = lane_take(table_ref[g, 1, k], index)
                        field_r, field_i = source[g, k, 0, x, y], source[g, k, 1, x, y]
                        if k == 0:
                            real = coef_r * field_r - coef_i * field_i
                            imag = coef_r * field_i + coef_i * field_r
                        else:
                            real = real + coef_r * field_r - coef_i * field_i
                            imag = imag + coef_r * field_i + coef_i * field_r
                    basis[g, 0, 0, x, y] = real
                    basis[g, 0, 1, x, y] = imag
                    layer = real if layer is None else layer + real
                layers.append((layer + pltpu.roll(layer, ENTRY_SPAN, 1)) * scale)
            for h in range(2):
                index = low_index + h * (LANES // QUAD)
                whole = lane_take(layers[0], index)
                for y in range(1, QUAD):
                    whole = jnp.where(quarter == y, lane_take(layers[y], index), whole)
                halves[h, pl.ds(x, SUB, stride=SUB)] = whole
        place = jnp.bitwise_xor(z // levels, depth_pos)
        level = z % levels

        def emit(ref):
            at = (place // 2) * levels + level
            for h in range(2):
                ref[at, :, h * LANES : (h + 1) * LANES] = halves[h]

        pl.when(place % 2 == 0)(functools.partial(emit, keep_ref))
        pl.when(place % 2 == 1)(functools.partial(emit, send_ref))

    accumulate(0, first_ref)

    def depth_step(z, carry):
        for g in range(groups):
            for c in range(2):
                start = [[basis[g, 0, c, x, y] for y in range(QUAD)] for x in range(SUB)]

                def put(k, x, y, value):
                    basis[g, k, c, x, y] = value

                chebyshev(start, terms, masks, put)
        accumulate(z, basis)
        return carry

    lax.fori_loop(1, depths, depth_step, 0)


def per_device(surface, freq_slot, tap_table, vel_index):
    local_count, _, rows, columns = surface.shape
    depth_count = lax.axis_size("depth")
    freq_count = lax.axis_size("freq")
    levels = vel_index.shape[0]
    _, terms, entries, table_freqs = tap_table.shape
    count = -(-local_count // depth_count)
    groups = -(-count // PAIR)
    depths = depth_count * levels
    vmem = pl.BlockSpec(memory_space=pltpu.VMEM)
    params = pltpu.CompilerParams(vmem_limit_bytes=40 * 1024 * 1024)

    vels = [vel_index] + [exchange(vel_index, "depth", flip) for flip in range(1, depth_count)]

    basis_shape = (groups, terms, 2, SUB, QUAD, SUB, LANES)
    table, basis = pl.pallas_call(
        functools.partial(first_kernel, (groups, count, local_count, terms, entries)),
        out_shape=(
            jax.ShapeDtypeStruct((groups, 2, terms, SUB, LANES), jnp.float32),
            jax.ShapeDtypeStruct(basis_shape, jnp.float32),
        ),
        in_specs=[
            pl.BlockSpec(memory_space=pltpu.SMEM),
            pl.BlockSpec(memory_space=pl.ANY),
            vmem,
        ],
        out_specs=(vmem, vmem),
        scratch_shapes=[
            pltpu.VMEM((count, 2, rows, columns), jnp.float32),
            pltpu.SemaphoreType.DMA((count,)),
            pltpu.VMEM((PAIR, 2, rows, LANES), jnp.float32),
        ],
        compiler_params=params,
        cost_estimate=pl.CostEstimate(flops=200_000_000, bytes_accessed=16_000_000, transcendentals=0),
    )(freq_slot, surface, tap_table.reshape(2 * terms * entries, table_freqs))

    scale = 1.0 / math.sqrt(local_count * freq_count)
    half = jax.ShapeDtypeStruct((depths // 2, rows, columns), jnp.float32)
    keep, send = pl.pallas_call(
        functools.partial(image_kernel, (groups, depth_count, levels, terms), scale),
        out_shape=(half, half),
        in_specs=[vmem] * (2 + depth_count),
        out_specs=(vmem, vmem),
        scratch_shapes=[
            pltpu.VMEM((2, rows, LANES), jnp.float32),
            pltpu.VMEM((2, rows, LANES), jnp.int32),
            pltpu.VMEM((depths, SUB, QUAD, SUB, LANES), jnp.int32),
            pltpu.VMEM(basis_shape, jnp.float32),
        ],
        compiler_params=params,
    )(table, basis, *vels)

    image = keep + exchange(send, "depth", 1)
    distance = 2
    while distance < depth_count:
        image = image.reshape((-1, 2, levels, rows, columns))
        image = (image[:, 0] + exchange(image[:, 1], "depth", distance)).reshape((-1, rows, columns))
        distance *= 2
    distance = 1
    while distance < freq_count:
        if distance == 1 and freq_count >= 4:
            image = image + exchange(image, "freq", 1) + (exchange(image, "freq", 2) + exchange(image, "freq", 3))
            distance = 4
        else:
            image = image + exchange(image, "freq", distance)
            distance *= 2
    return image


def solution(mesh):
    in_specs = (P("freq", None, None, None), P("freq"), P(), P("depth", None, None))
    out_specs = P("depth", None, None)
    return jax.shard_map(
        per_device, mesh=mesh, in_specs=in_specs, out_specs=out_specs, check_vma=False
    )
```

time: 221 us -> 42.1 us (0.19)
  waiting for transfers between devices: 84.5 us -> 10 us
  starting transfers between devices: 49.8 us -> 11.8 us
  other arithmetic: 33.5 us -> 0.68 us
  local copies, waits for them, and re-layouts: 26.9 us -> 3.68 us
  Pallas kernels: 0 us -> 15.6 us
  between operations: 13.4 us -> 0.08 us
  matrix products: 11 us -> 0 us
    psum x1 -> x0, waiting for transfers between devices: 76.8 us -> none  [per_device(): summed = lax.psum(image_part, 'freq')]
    ppermute x7 -> x9, starting transfers between devices: 49.8 us -> 11.8 us  [exchange(): return lax.ppermute(value, axis, [(i, i ^ flip) for i in range(count)])]
    pallas_call x0 -> x2, Pallas kernels: none -> 15.6 us  [the longest x1 12.7 us: per_device(): pl.pallas_call(functools.partial(image_kernel, (groups, depth_count, leve...]
    unnamed x4 -> x8, local copies, waits for them, and re-layouts: 18.6 us -> 3.67 us
    add x43 -> x2, other arithmetic: 13.7 us -> 0.66 us  [the longest x1 0.64 us: per_device(): image = image + exchange(image, 'freq', distance)]
    dot_general x1 -> x0, matrix products: 11 us -> none  [lookup(): jnp.dot(tap_part.reshape(-1, entries), one_hot, precision=lax.Precision.H...]
    sub x36 -> x0, other arithmetic: 8.32 us -> none  [the longest x28 5.92 us: extrapolate(): earlier, current = (current, 2.0 * mcclellan(current) - earlier)]
    squeeze x4 -> x1, local copies, waits for them, and re-layouts: 7.68 us -> 0.01 us  [per_device(): image[:, 1]]
  transfers between devices with their start and end apart: 8 -> 9, of which waited for: 8 -> 6; matrix products, arithmetic and copies ran while one was open for 0% -> 0% of each run, Pallas kernels for 0% -> 7%
where the time goes in v2:
time: 42.1 us; the launch traced here: 41.8 us
  Pallas kernels  15.6 us (37%)
  starting transfers between devices  11.8 us (28%)
  waiting for transfers between devices  10 us (24%)
  local copies, waits for them, and re-layouts  3.68 us (9%)
  other arithmetic  0.68 us (2%)
    pallas_call x1, Pallas kernels, per_device(): pl.pallas_call(functools.partial(image_kernel, (groups, depth_count, leve...  12.7 us
    ppermute x9, starting transfers between devices, exchange(): return lax.ppermute(value, axis, [(i, i ^ flip) for i in range(count)])  11.8 us
    ppermute x9, waiting for transfers between devices, exchange(): return lax.ppermute(value, axis, [(i, i ^ flip) for i in range(count)])  10 us
    unnamed x8, local copies, waits for them, and re-layouts  3.67 us
    pallas_call x1, Pallas kernels, per_device(): pl.pallas_call(functools.partial(first_kernel, (groups, count, local_coun...  2.83 us
  transfers between devices with their start and end apart: 9, of which 6 were waited for; matrix products, arithmetic and copies ran while one was open for 0% of the time, Pallas kernels for 7%

profile of v2, /device:TPU:0, one launch (start us, length us, event | category | flops | bytes accessed | tf_op | source)
XLA Modules:
  0.0 41.8 jit_solution(1790075087927478320)
XLA Ops:
  0.0 3.0 %collective-permute-start.1 = (s32[1,64,256]{2,1,0:T(8,128)}, s32[1,64,256]{2,1,0:T(8,128)S(1)}, u32[]{:S(2)}, u32[]{:S(2)}) collective-permute-start(s32[1,64,256]{2,1,0:T(8,128)} %refs_0_.1), channel_id=1, source_target_pairs={{0,16},{8,24},{16,0},{24,8},{1,17},{9,25},{17,1},{25,9},{2,18},{10... | collective-permute-start | bytes 196616 | tf_op jit(solution)/shard_map/ppermute | solution.py:20
  3.0 0.0 collective-permute-start
  3.0 0.1 collective-permute-start.2
  3.1 0.0 copy-start
  3.1 1.2 %copy-done = f32[8,2,64,256]{3,2,1,0:T(8,128)S(1)} copy-done((f32[8,2,64,256]{3,2,1,0:T(8,128)S(1)}, f32[8,2,64,256]{3,2,1,0:T(8,128)}, u32[]{:S(2)}) %copy-start) | copy-done | bytes 1048600
  4.3 0.0 copy-start.1
  4.3 1.0 %copy-done.1 = f32[2,9,32,64]{3,2,1,0:T(8,128)S(1)} copy-done((f32[2,9,32,64]{3,2,1,0:T(8,128)S(1)}, f32[2,9,32,64]{3,2,1,0:T(8,128)}, u32[]{:S(2)}) %copy-start.1) | copy-done | bytes 147480
  5.3 0.0 copy-start.3
  5.3 0.7 %copy-done.3 = s32[8]{0:T(128)S(1)} copy-done((s32[8]{0:T(128)S(1)}, s32[8]{0:T(128)}, u32[]{:S(2)}) %copy-start.3) | copy-done | bytes 56
  5.9 2.8 %shard_map.46 = (f32[1,2,9,8,128]{4,3,2,1,0:T(8,128)S(1)}, f32[1,9,2,8,4,8,128]{6,5,4,3,2,1,0:T(8,128)S(1)}) custom-call(s32[8]{0:T(128)S(1)} %copy-done.3, f32[8,2,64,256]{3,2,1,0:T(8,128)S(1)} %copy-done, f32[576,64]{1,0:T(8,128)S(1)} %bitcast.16), custom_call_target="tpu_custom_call" | custom-call | flops 200000000 | bytes 16000000 | tf_op jit(solution)/shard_map/pallas_call | solution.py:252
  8.8 0.0 collective-permute-done.1.refs_2_
  8.8 0.0 collective-permute-done.refs_1_
  8.8 0.0 collective-permute-done.2.refs_3_
  8.8 0.0 copy-start.2
  8.8 0.8 %copy-done.2 = s32[1,64,256]{2,1,0:T(8,128)S(1)} copy-done((s32[1,64,256]{2,1,0:T(8,128)S(1)}, s32[1,64,256]{2,1,0:T(8,128)}, u32[]{:S(2)}) %copy-start.2) | copy-done | bytes 65560
  9.6 12.7 %shard_map.47 = (f32[2,64,256]{2,1,0:T(8,128)S(1)}, f32[2,64,256]{2,1,0:T(8,128)S(1)}) custom-call(f32[1,2,9,8,128]{4,3,2,1,0:T(8,128)S(1)} %get-tuple-element.9.table_ref, f32[1,9,2,8,4,8,128]{6,5,4,3,2,1,0:T(8,128)S(1)} %get-tuple-element.10.first_ref, s32[1,64,256]{2,1,0:T(8,128)S(1)} %copy-done.2, s32[1,64,256]{2,1,0:T(8,128)S(1)} %collective-permute-done.refs_1_, ...), custom_call_target="tpu_custom_call" | custom-call | tf_op jit(solution)/shard_map/pallas_call | solution.py:275
  22.4 0.5 %collective-permute-start.3 = (f32[2,64,256]{2,1,0:T(8,128)S(1)}, f32[2,64,256]{2,1,0:T(8,128)S(1)}, u32[]{:S(2)}, u32[]{:S(2)}) collective-permute-start(f32[2,64,256]{2,1,0:T(8,128)S(1)} %get-tuple-element.12), channel_id=1, source_target_pairs={{0,8},{8,0},{16,24},{24,16},{1,9},{9,1},{17,25},{25,17},{2,10},{10... | collective-permute-start | bytes 393224 | tf_op jit(solution)/shard_map/ppermute | solution.py:20
  22.8 1.0 %collective-permute-done.3 = f32[2,64,256]{2,1,0:T(8,128)S(1)} collective-permute-done((f32[2,64,256]{2,1,0:T(8,128)S(1)}, f32[2,64,256]{2,1,0:T(8,128)S(1)}, u32[]{:S(2)}, u32[]{:S(2)}) %collective-permute-start.3) | collective-permute-done | bytes 131104 | tf_op jit(solution)/shard_map/ppermute | solution.py:20
  23.8 2.1 %collective-permute-start.4 = (f32[1,1,64,256]{3,2,1,0:T(8,128)S(1)}, f32[1,1,64,256]{3,2,1,0:T(8,128)S(1)}, u32[]{:S(2)}, u32[]{:S(2)}) collective-permute-start(f32[1,1,64,256]{3,2,1,0:T(8,128)S(1)} %slice_bitcast_fusion), channel_id=1, source_target_pairs={{0,16},{8,24},{16,0},{24,8},{1,17},{9,25},{17,1},{25,9},{2,18},{10... | collective-permute-start | bytes 196616 | tf_op jit(solution)/shard_map/ppermute | solution.py:20
  25.9 2.4 %collective-permute-done.4 = f32[1,1,64,256]{3,2,1,0:T(8,128)S(1)} collective-permute-done((f32[1,1,64,256]{3,2,1,0:T(8,128)S(1)}, f32[1,1,64,256]{3,2,1,0:T(8,128)S(1)}, u32[]{:S(2)}, u32[]{:S(2)}) %collective-permute-start.4) | collective-permute-done | bytes 65568 | tf_op jit(solution)/shard_map/ppermute | solution.py:20
  28.3 2.9 %collective-permute-start.7 = (f32[1,64,256]{2,1,0:T(8,128)S(1)}, f32[1,64,256]{2,1,0:T(8,128)S(1)}, u32[]{:S(2)}, u32[]{:S(2)}) collective-permute-start(f32[1,64,256]{2,1,0:T(8,128)S(1)} %fusion.1), channel_id=1, source_target_pairs={{0,3},{1,2},{2,1},{3,0},{4,7},{5,6},{6,5},{7,4},{8,11},{9,10},{10,... | collective-permute-start | bytes 196616 | tf_op jit(solution)/shard_map/ppermute | solution.py:20
  31.2 0.4 %collective-permute-start.6 = (f32[1,64,256]{2,1,0:T(8,128)S(1)}, f32[1,64,256]{2,1,0:T(8,128)S(1)}, u32[]{:S(2)}, u32[]{:S(2)}) collective-permute-start(f32[1,64,256]{2,1,0:T(8,128)S(1)} %fusion.1), channel_id=1, source_target_pairs={{0,2},{1,3},{2,0},{3,1},{4,6},{5,7},{6,4},{7,5},{8,10},{9,11},{10,... | collective-permute-start | bytes 196616 | tf_op jit(solution)/shard_map/ppermute | solution.py:20
  31.7 0.2 collective-permute-start.5
  31.9 2.1 %collective-permute-done.7 = f32[1,64,256]{2,1,0:T(8,128)S(1)} collective-permute-done((f32[1,64,256]{2,1,0:T(8,128)S(1)}, f32[1,64,256]{2,1,0:T(8,128)S(1)}, u32[]{:S(2)}, u32[]{:S(2)}) %collective-permute-start.7) | collective-permute-done | bytes 65568 | tf_op jit(solution)/shard_map/ppermute | solution.py:20
  34.0 1.5 %collective-permute-done.6 = f32[1,64,256]{2,1,0:T(8,128)S(1)} collective-permute-done((f32[1,64,256]{2,1,0:T(8,128)S(1)}, f32[1,64,256]{2,1,0:T(8,128)S(1)}, u32[]{:S(2)}, u32[]{:S(2)}) %collective-permute-start.6) | collective-permute-done | bytes 65568 | tf_op jit(solution)/shard_map/ppermute | solution.py:20
  35.5 0.4 %collective-permute-done.5 = f32[1,64,256]{2,1,0:T(8,128)S(1)} collective-permute-done((f32[1,64,256]{2,1,0:T(8,128)S(1)}, f32[1,64,256]{2,1,0:T(8,128)S(1)}, u32[]{:S(2)}, u32[]{:S(2)}) %collective-permute-start.5) | collective-permute-done | bytes 65568 | tf_op jit(solution)/shard_map/ppermute | solution.py:20
  36.0 2.7 %collective-permute-start.8 = (f32[1,64,256]{2,1,0:T(8,128)S(1)}, f32[1,64,256]{2,1,0:T(8,128)S(1)}, u32[]{:S(2)}, u32[]{:S(2)}) collective-permute-start(f32[1,64,256]{2,1,0:T(8,128)S(1)} %add_add_fusion), channel_id=1, source_target_pairs={{0,4},{1,5},{2,6},{3,7},{4,0},{5,1},{6,2},{7,3},{8,12},{9,13},{10,... | collective-permute-start | bytes 196616 | tf_op jit(solution)/shard_map/ppermute | solution.py:20
  38.6 2.6 %collective-permute-done.8 = f32[1,64,256]{2,1,0:T(8,128)S(1)} collective-permute-done((f32[1,64,256]{2,1,0:T(8,128)S(1)}, f32[1,64,256]{2,1,0:T(8,128)S(1)}, u32[]{:S(2)}, u32[]{:S(2)}) %collective-permute-start.8) | collective-permute-done | bytes 65568 | tf_op jit(solution)/shard_map/ppermute | solution.py:20
  41.2 0.6 %add.23 = f32[1,64,256]{2,1,0:T(8,128)} add(f32[1,64,256]{2,1,0:T(8,128)S(1)} %add_add_fusion, f32[1,64,256]{2,1,0:T(8,128)S(1)} %collective-permute-done.8) | non-fusion elementwise | flops 16384 | bytes 196608 | tf_op jit(solution)/shard_map/add | solution.py:301
  (4 shorter events, 0.1 us)
Async XLA Ops:
  0.0 8.8 %collective-permute-start.1 = (s32[1,64,256]{2,1,0:T(8,128)}, s32[1,64,256]{2,1,0:T(8,128)S(1)}, u32[]{:S(2)}, u32[]{:S(2)}) collective-permute-start(s32[1,64,256]{2,1,0:T(8,128)} %refs_0_.1), channel_id=1, source_target_pairs={{0,16},{8,24},{16,0},{24,8},{1,17},{9,25},{17,1},{25,9},{2,18},{10... | collective-permute-start | bytes 196616 | tf_op jit(solution)/shard_map/ppermute | solution.py:20
  3.0 5.8 %collective-permute-start = (s32[1,64,256]{2,1,0:T(8,128)}, s32[1,64,256]{2,1,0:T(8,128)S(1)}, u32[]{:S(2)}, u32[]{:S(2)}) collective-permute-start(s32[1,64,256]{2,1,0:T(8,128)} %refs_0_.1), channel_id=1, source_target_pairs={{0,8},{8,0},{16,24},{24,16},{1,9},{9,1},{17,25},{25,17},{2,10},{10... | collective-permute-start | bytes 196616 | tf_op jit(solution)/shard_map/ppermute | solution.py:20
  3.0 5.8 %collective-permute-start.2 = (s32[1,64,256]{2,1,0:T(8,128)}, s32[1,64,256]{2,1,0:T(8,128)S(1)}, u32[]{:S(2)}, u32[]{:S(2)}) collective-permute-start(s32[1,64,256]{2,1,0:T(8,128)} %refs_0_.1), channel_id=1, source_target_pairs={{0,24},{8,16},{16,8},{24,0},{1,25},{9,17},{17,9},{25,1},{2,26},{10... | collective-permute-start | bytes 196616 | tf_op jit(solution)/shard_map/ppermute | solution.py:20
  3.1 1.2 %copy-start = (f32[8,2,64,256]{3,2,1,0:T(8,128)S(1)}, f32[8,2,64,256]{3,2,1,0:T(8,128)}, u32[]{:S(2)}) copy-start(f32[8,2,64,256]{3,2,1,0:T(8,128)} %surface_ref.1) | copy-start | bytes 3145732
  4.3 1.0 %copy-start.1 = (f32[2,9,32,64]{3,2,1,0:T(8,128)S(1)}, f32[2,9,32,64]{3,2,1,0:T(8,128)}, u32[]{:S(2)}) copy-start(f32[2,9,32,64]{3,2,1,0:T(8,128)} %param.6) | copy-start | bytes 442372
  5.3 0.7 %copy-start.3 = (s32[8]{0:T(128)S(1)}, s32[8]{0:T(128)}, u32[]{:S(2)}) copy-start(s32[8]{0:T(128)} %slot_ref.1) | copy-start | bytes 100
  8.8 0.8 %copy-start.2 = (s32[1,64,256]{2,1,0:T(8,128)S(1)}, s32[1,64,256]{2,1,0:T(8,128)}, u32[]{:S(2)}) copy-start(s32[1,64,256]{2,1,0:T(8,128)} %refs_0_.1) | copy-start | bytes 196612
  22.4 1.4 %collective-permute-start.3 = (f32[2,64,256]{2,1,0:T(8,128)S(1)}, f32[2,64,256]{2,1,0:T(8,128)S(1)}, u32[]{:S(2)}, u32[]{:S(2)}) collective-permute-start(f32[2,64,256]{2,1,0:T(8,128)S(1)} %get-tuple-element.12), channel_id=1, source_target_pairs={{0,8},{8,0},{16,24},{24,16},{1,9},{9,1},{17,25},{25,17},{2,10},{10... | collective-permute-start | bytes 393224 | tf_op jit(solution)/shard_map/ppermute | solution.py:20
  23.8 4.5 %collective-permute-start.4 = (f32[1,1,64,256]{3,2,1,0:T(8,128)S(1)}, f32[1,1,64,256]{3,2,1,0:T(8,128)S(1)}, u32[]{:S(2)}, u32[]{:S(2)}) collective-permute-start(f32[1,1,64,256]{3,2,1,0:T(8,128)S(1)} %slice_bitcast_fusion), channel_id=1, source_target_pairs={{0,16},{8,24},{16,0},{24,8},{1,17},{9,25},{17,1},{25,9},{2,18},{10... | collective-permute-start | bytes 196616 | tf_op jit(solution)/shard_map/ppermute | solution.py:20
  28.3 5.7 %collective-permute-start.7 = (f32[1,64,256]{2,1,0:T(8,128)S(1)}, f32[1,64,256]{2,1,0:T(8,128)S(1)}, u32[]{:S(2)}, u32[]{:S(2)}) collective-permute-start(f32[1,64,256]{2,1,0:T(8,128)S(1)} %fusion.1), channel_id=1, source_target_pairs={{0,3},{1,2},{2,1},{3,0},{4,7},{5,6},{6,5},{7,4},{8,11},{9,10},{10,... | collective-permute-start | bytes 196616 | tf_op jit(solution)/shard_map/ppermute | solution.py:20
  31.2 4.3 %collective-permute-start.6 = (f32[1,64,256]{2,1,0:T(8,128)S(1)}, f32[1,64,256]{2,1,0:T(8,128)S(1)}, u32[]{:S(2)}, u32[]{:S(2)}) collective-permute-start(f32[1,64,256]{2,1,0:T(8,128)S(1)} %fusion.1), channel_id=1, source_target_pairs={{0,2},{1,3},{2,0},{3,1},{4,6},{5,7},{6,4},{7,5},{8,10},{9,11},{10,... | collective-permute-start | bytes 196616 | tf_op jit(solution)/shard_map/ppermute | solution.py:20
  31.7 4.3 %collective-permute-start.5 = (f32[1,64,256]{2,1,0:T(8,128)S(1)}, f32[1,64,256]{2,1,0:T(8,128)S(1)}, u32[]{:S(2)}, u32[]{:S(2)}) collective-permute-start(f32[1,64,256]{2,1,0:T(8,128)S(1)} %fusion.1), channel_id=1, source_target_pairs={{0,1},{1,0},{2,3},{3,2},{4,5},{5,4},{6,7},{7,6},{8,9},{9,8},{10,11... | collective-permute-start | bytes 196616 | tf_op jit(solution)/shard_map/ppermute | solution.py:20
  36.0 5.2 %collective-permute-start.8 = (f32[1,64,256]{2,1,0:T(8,128)S(1)}, f32[1,64,256]{2,1,0:T(8,128)S(1)}, u32[]{:S(2)}, u32[]{:S(2)}) collective-permute-start(f32[1,64,256]{2,1,0:T(8,128)S(1)} %add_add_fusion), channel_id=1, source_target_pairs={{0,4},{1,5},{2,6},{3,7},{4,0},{5,1},{6,2},{7,3},{8,12},{9,13},{10,... | collective-permute-start | bytes 196616 | tf_op jit(solution)/shard_map/ppermute | solution.py:20

commit v3 on v2

--- a/solution.py
+++ b/solution.py
@@ -76,13 +76,23 @@
     return (lane_number() % (LANES // QUAD)) * QUAD + y
 
 
-def first_kernel(sizes, slot_ref, surface_ref, tap_ref, table_ref, basis_ref, raw, raw_sem, halves):
+def first_kernel(
+    sizes, slot_hbm, surface_ref, tap_hbm, vel_hbm, table_ref, basis_ref, vel_ref, raw, raw_sem, halves, slot_ref, tap_ref, sems
+):
     groups, count, local_count, terms, entries = sizes
     first = lax.axis_index("depth") * count
     members = [jnp.minimum(first + j, local_count - 1) for j in range(count)]
+    slot_copy = pltpu.make_async_copy(slot_hbm, slot_ref, sems.at[0])
+    tap_copy = pltpu.make_async_copy(tap_hbm, tap_ref, sems.at[1])
+    vel_copy = pltpu.make_async_copy(vel_hbm, vel_ref, sems.at[2])
     copies = [pltpu.make_async_copy(surface_ref.at[members[j]], raw.at[j], raw_sem.at[j]) for j in range(count)]
+    slot_copy.start()
+    tap_copy.start()
     for copy in copies:
         copy.start()
+    vel_copy.start()
+    slot_copy.wait()
+    tap_copy.wait()
 
     table_freqs = tap_ref.shape[1]
     rows = -(-count // SUB) * SUB
@@ -125,15 +135,15 @@
             for i in range(PAIR):
                 j = min(g * PAIR + i, count - 1)
                 for h in range(2):
-                    halves[i, h] = raw[j, c, :, h * LANES : (h + 1) * LANES]
-            start = []
-            for x in range(SUB):
-                line = []
-                for y in range(QUAD):
-                    index = split_index(y)
+                    halves[g, c, i, h] = raw[j, c, :, h * LANES : (h + 1) * LANES]
+    for y in range(QUAD):
+        index = split_index(y)
+        for g in range(groups):
+            for c in range(2):
+                for x in range(SUB):
                     sides = []
                     for i in range(PAIR):
-                        low, high = [lane_take(halves[i, h, pl.ds(x, SUB, stride=SUB)], index) for h in range(2)]
+                        low, high = [lane_take(halves[g, c, i, h, pl.ds(x, SUB, stride=SUB)], index) for h in range(2)]
                         side = jnp.where(in_low, low, high)
                         j = g * PAIR + i
                         if j >= count:
@@ -141,46 +151,54 @@
                         elif count * lax.axis_size("depth") > local_count:
                             side = jnp.where(first + j < local_count, side, 0.0)
                         sides.append(side)
-                    value = jnp.where(lane < ENTRY_SPAN, sides[0], sides[1])
-                    basis_ref[g, 0, c, x, y] = value
-                    line.append(value)
-                start.append(line)
+                    basis_ref[g, 0, c, x, y] = jnp.where(lane < ENTRY_SPAN, sides[0], sides[1])
+    for g in range(groups):
+        for c in range(2):
+            start = [[basis_ref[g, 0, c, x, y] for y in range(QUAD)] for x in range(SUB)]
 
             def put(k, x, y, value):
                 basis_ref[g, k, c, x, y] = value
 
             chebyshev(start, terms, masks, put)
+    vel_copy.wait()
 
 
 def image_kernel(sizes, scale, table_ref, first_ref, *refs):
     groups, depth_count, levels, terms = sizes
     vel_refs = refs[:depth_count]
-    keep_ref, send_ref, halves, halves_i, index_ref, basis = refs[depth_count:]
+    keep_ref, send_ref, numbers, halves, index_ref, layers, basis = refs[depth_count:]
     depth_pos = lax.axis_index("depth")
     depths = depth_count * levels
-    lane = lane_number()
-    in_low = lane % ENTRY_SPAN < ENTRY_SPAN // 2
+    columns = QUAD * ENTRY_SPAN
     masks = edge_masks()
 
-    table_base = jnp.where(lane < ENTRY_SPAN, 0, ENTRY_SPAN)
+    source = lax.broadcasted_iota(jnp.int32, (columns, QUAD * LANES), 0)
+    place = lax.broadcasted_iota(jnp.int32, (columns, QUAD * LANES), 1)
+    split = (source == (place % ENTRY_SPAN) * QUAD + place // LANES).astype(jnp.float32).astype(jnp.bfloat16)
+
+    table_base = jnp.where(lane_number() < ENTRY_SPAN, 0, ENTRY_SPAN)
     for slot, vel_ref in enumerate(vel_refs):
         target = jnp.bitwise_xor(depth_pos, slot) * levels
         for level in range(levels):
-            for h in range(2):
-                halves_i[h] = vel_ref[level, :, h * LANES : (h + 1) * LANES]
+            spread = jnp.dot(
+                vel_ref[level].astype(jnp.float32).astype(jnp.bfloat16), split, preferred_element_type=jnp.float32
+            ).astype(jnp.int32)
+            for y in range(QUAD):
+                numbers[y] = spread[:, y * LANES : (y + 1) * LANES]
             for x in range(SUB):
-                low, high = [halves_i[h, pl.ds(x, SUB, stride=SUB)] for h in range(2)]
                 for y in range(QUAD):
-                    index = split_index(y)
-                    entry = jnp.where(in_low, lane_take(low, index), lane_take(high, index))
-                    index_ref[target + level, x, y] = entry + table_base
-
-    low_index = lane // QUAD
-    quarter = lane % QUAD
-
-    def accumulate(z, source):
+                    index_ref[target + level, x, y] = numbers[y, pl.ds(x, SUB, stride=SUB)] + table_base
+
+    def first_terms(k, carry):
+        for g in range(groups):
+            for c in range(2):
+                basis[g, k, c] = first_ref[g, k, c]
+        return carry
+
+    lax.fori_loop(0, terms, first_terms, 0)
+
+    def depth_step(z, carry):
         for x in range(SUB):
-            layers = []
             for y in range(QUAD):
                 index = index_ref[z, x, y]
                 layer = None
@@ -189,7 +207,7 @@
                     for k in range(terms):
                         coef_r = lane_take(table_ref[g, 0, k], index)
                         coef_i = lane_take(table_ref[g, 1, k], index)
-                        field_r, field_i = source[g, k, 0, x, y], source[g, k, 1, x, y]
+                        field_r, field_i = basis[g, k, 0, x, y], basis[g, k, 1, x, y]
                         if k == 0:
                             real = coef_r * field_r - coef_i * field_i
                             imag = coef_r * field_i + coef_i * field_r
@@ -199,13 +217,39 @@
                     basis[g, 0, 0, x, y] = real
                     basis[g, 0, 1, x, y] = imag
                     layer = real if layer is None else layer + real
-                layers.append((layer + pltpu.roll(layer, ENTRY_SPAN, 1)) * scale)
-            for h in range(2):
-                index = low_index + h * (LANES // QUAD)
-                whole = lane_take(layers[0], index)
-                for y in range(1, QUAD):
-                    whole = jnp.where(quarter == y, lane_take(layers[y], index), whole)
-                halves[h, pl.ds(x, SUB, stride=SUB)] = whole
+                layers[z, y, x * SUB : (x + 1) * SUB] = layer * scale
+
+        @pl.when(z < depths - 1)
+        def _():
+            for g in range(groups):
+                for c in range(2):
+                    start = [[basis[g, 0, c, x, y] for y in range(QUAD)] for x in range(SUB)]
+
+                    def put(k, x, y, value):
+                        basis[g, k, c, x, y] = value
+
+                    chebyshev(start, terms, masks, put)
+
+        return carry
+
+    lax.fori_loop(0, depths, depth_step, 0)
+
+    turned = lax.broadcasted_iota(jnp.int32, (LANES, columns), 0) % ENTRY_SPAN * QUAD
+    wanted = lax.broadcasted_iota(jnp.int32, (LANES, columns), 1)
+    joins = [(wanted == turned + y).astype(jnp.float32).astype(jnp.bfloat16) for y in range(QUAD)]
+
+    def join(z, carry):
+        whole = None
+        for y in range(QUAD):
+            rest = layers[z, y]
+            for part in range(3):
+                piece = rest.astype(jnp.bfloat16)
+                rest = rest - piece.astype(jnp.float32)
+                product = jnp.dot(piece, joins[y], preferred_element_type=jnp.float32)
+                whole = product if whole is None else whole + product
+        for h in range(2):
+            for x in range(SUB):
+                halves[h, pl.ds(x, SUB, stride=SUB)] = whole[x * SUB : (x + 1) * SUB, h * LANES : (h + 1) * LANES]
         place = jnp.bitwise_xor(z // levels, depth_pos)
         level = z % levels
 
@@ -216,22 +260,9 @@
 
         pl.when(place % 2 == 0)(functools.partial(emit, keep_ref))
         pl.when(place % 2 == 1)(functools.partial(emit, send_ref))
-
-    accumulate(0, first_ref)
-
-    def depth_step(z, carry):
-        for g in range(groups):
-            for c in range(2):
-                start = [[basis[g, 0, c, x, y] for y in range(QUAD)] for x in range(SUB)]
-
-                def put(k, x, y, value):
-                    basis[g, k, c, x, y] = value
-
-                chebyshev(start, terms, masks, put)
-        accumulate(z, basis)
         return carry
 
-    lax.fori_loop(1, depths, depth_step, 0)
+    lax.fori_loop(0, depths, join, 0)
 
 
 def per_device(surface, freq_slot, tap_table, vel_index):
@@ -246,29 +277,30 @@
     vmem = pl.BlockSpec(memory_space=pltpu.VMEM)
     params = pltpu.CompilerParams(vmem_limit_bytes=40 * 1024 * 1024)
 
-    vels = [vel_index] + [exchange(vel_index, "depth", flip) for flip in range(1, depth_count)]
+    vels = [exchange(vel_index, "depth", flip) for flip in range(1, depth_count)]
 
     basis_shape = (groups, terms, 2, SUB, QUAD, SUB, LANES)
-    table, basis = pl.pallas_call(
+    hbm = pl.BlockSpec(memory_space=pltpu.HBM)
+    table, basis, own_vel = pl.pallas_call(
         functools.partial(first_kernel, (groups, count, local_count, terms, entries)),
         out_shape=(
             jax.ShapeDtypeStruct((groups, 2, terms, SUB, LANES), jnp.float32),
             jax.ShapeDtypeStruct(basis_shape, jnp.float32),
+            jax.ShapeDtypeStruct(vel_index.shape, jnp.int32),
         ),
-        in_specs=[
-            pl.BlockSpec(memory_space=pltpu.SMEM),
-            pl.BlockSpec(memory_space=pl.ANY),
-            vmem,
-        ],
-        out_specs=(vmem, vmem),
+        in_specs=[hbm] * 4,
+        out_specs=(vmem, vmem, vmem),
         scratch_shapes=[
             pltpu.VMEM((count, 2, rows, columns), jnp.float32),
             pltpu.SemaphoreType.DMA((count,)),
-            pltpu.VMEM((PAIR, 2, rows, LANES), jnp.float32),
+            pltpu.VMEM((groups, 2, PAIR, 2, rows, LANES), jnp.float32),
+            pltpu.SMEM((local_count,), jnp.int32),
+            pltpu.VMEM((2 * terms * entries, table_freqs), jnp.float32),
+            pltpu.SemaphoreType.DMA((3,)),
         ],
         compiler_params=params,
         cost_estimate=pl.CostEstimate(flops=200_000_000, bytes_accessed=16_000_000, transcendentals=0),
-    )(freq_slot, surface, tap_table.reshape(2 * terms * entries, table_freqs))
+    )(freq_slot, surface, tap_table.reshape(2 * terms * entries, table_freqs), vel_index)
 
     scale = 1.0 / math.sqrt(local_count * freq_count)
     half = jax.ShapeDtypeStruct((depths // 2, rows, columns), jnp.float32)
@@ -278,13 +310,14 @@
         in_specs=[vmem] * (2 + depth_count),
         out_specs=(vmem, vmem),
         scratch_shapes=[
+            pltpu.VMEM((QUAD, rows, LANES), jnp.int32),
             pltpu.VMEM((2, rows, LANES), jnp.float32),
-            pltpu.VMEM((2, rows, LANES), jnp.int32),
             pltpu.VMEM((depths, SUB, QUAD, SUB, LANES), jnp.int32),
+            pltpu.VMEM((depths, QUAD, rows, LANES), jnp.float32),
             pltpu.VMEM(basis_shape, jnp.float32),
         ],
         compiler_params=params,
-    )(table, basis, *vels)
+    )(table, basis, own_vel, *vels)
 
     image = keep + exchange(send, "depth", 1)
     distance = 2

time: 42.1 us -> 36.1 us (0.86)
  Pallas kernels: 15.6 us -> 9.58 us
    pallas_call x1, Pallas kernels: 12.7 us -> 7.41 us  [per_device(): pl.pallas_call(functools.partial(image_kernel, (groups, depth_count, leve...]
    pallas_call x1, Pallas kernels: 2.83 us -> 2.17 us  [per_device(): pl.pallas_call(functools.partial(first_kernel, (groups, count, local_coun...]
  transfers between devices with their start and end apart: 9 -> 9, of which waited for: 6 -> 6; matrix products, arithmetic and copies ran while one was open for 0% -> 0% of each run, Pallas kernels for 7% -> 6%
where the time goes in v3:
time: 36.1 us; the launch traced here: 35.9 us
  starting transfers between devices  11.6 us (32%)
  waiting for transfers between devices  10.3 us (29%)
  Pallas kernels  9.58 us (27%)
  local copies, waits for them, and re-layouts  3.69 us (10%)
  other arithmetic  0.68 us (2%)
    ppermute x9, starting transfers between devices, exchange(): return lax.ppermute(value, axis, [(i, i ^ flip) for i in range(count)])  11.6 us
    ppermute x9, waiting for transfers between devices, exchange(): return lax.ppermute(value, axis, [(i, i ^ flip) for i in range(count)])  10.3 us
    pallas_call x1, Pallas kernels, per_device(): pl.pallas_call(functools.partial(image_kernel, (groups, depth_count, leve...  7.41 us
    unnamed x8, local copies, waits for them, and re-layouts  3.68 us
    pallas_call x1, Pallas kernels, per_device(): pl.pallas_call(functools.partial(first_kernel, (groups, count, local_coun...  2.17 us
  transfers between devices with their start and end apart: 9, of which 6 were waited for; matrix products, arithmetic and copies ran while one was open for 0% of the time, Pallas kernels for 6%

profile of v3, /device:TPU:0, one launch (start us, length us, event | category | flops | bytes accessed | tf_op | source)
XLA Modules:
  0.0 35.9 jit_solution(7430879373748935033)
XLA Ops:
  0.0 0.5 %collective-permute-start = (s32[1,64,256]{2,1,0:T(8,128)}, s32[1,64,256]{2,1,0:T(8,128)S(1)}, u32[]{:S(2)}, u32[]{:S(2)}) collective-permute-start(s32[1,64,256]{2,1,0:T(8,128)} %vel_hbm.1), channel_id=1, source_target_pairs={{0,8},{8,0},{16,24},{24,16},{1,9},{9,1},{17,25},{25,17},{2,10},{10... | collective-permute-start | bytes 196616 | tf_op jit(solution)/shard_map/ppermute | solution.py:20
  0.5 2.6 %collective-permute-start.2 = (s32[1,64,256]{2,1,0:T(8,128)}, s32[1,64,256]{2,1,0:T(8,128)S(1)}, u32[]{:S(2)}, u32[]{:S(2)}) collective-permute-start(s32[1,64,256]{2,1,0:T(8,128)} %vel_hbm.1), channel_id=1, source_target_pairs={{0,24},{8,16},{16,8},{24,0},{1,25},{9,17},{17,9},{25,1},{2,26},{10... | collective-permute-start | bytes 196616 | tf_op jit(solution)/shard_map/ppermute | solution.py:20
  3.1 0.0 collective-permute-start.1
  3.1 0.0 copy-start
  3.1 1.2 %copy-done = f32[8,2,64,256]{3,2,1,0:T(8,128)S(1)} copy-done((f32[8,2,64,256]{3,2,1,0:T(8,128)S(1)}, f32[8,2,64,256]{3,2,1,0:T(8,128)}, u32[]{:S(2)}) %copy-start) | copy-done | bytes 1048600
  4.3 0.0 copy-start.1
  4.3 1.0 %copy-done.1 = f32[2,9,32,64]{3,2,1,0:T(8,128)S(1)} copy-done((f32[2,9,32,64]{3,2,1,0:T(8,128)S(1)}, f32[2,9,32,64]{3,2,1,0:T(8,128)}, u32[]{:S(2)}) %copy-start.1) | copy-done | bytes 147480
  5.3 0.0 copy-start.2
  5.3 0.8 %copy-done.2 = s32[1,64,256]{2,1,0:T(8,128)S(1)} copy-done((s32[1,64,256]{2,1,0:T(8,128)S(1)}, s32[1,64,256]{2,1,0:T(8,128)}, u32[]{:S(2)}) %copy-start.2) | copy-done | bytes 65560
  6.1 0.0 copy-start.3
  6.1 0.7 %copy-done.3 = s32[8]{0:T(128)S(1)} copy-done((s32[8]{0:T(128)S(1)}, s32[8]{0:T(128)}, u32[]{:S(2)}) %copy-start.3) | copy-done | bytes 56
  6.8 2.2 %shard_map.46 = (f32[1,2,9,8,128]{4,3,2,1,0:T(8,128)S(1)}, f32[1,9,2,8,4,8,128]{6,5,4,3,2,1,0:T(8,128)S(1)}, s32[1,64,256]{2,1,0:T(8,128)S(1)}) custom-call(s32[8]{0:T(128)S(1)} %copy-done.3, f32[8,2,64,256]{3,2,1,0:T(8,128)S(1)} %copy-done, f32[576,64]{1,0:T(8,128)S(1)} %bitcast.16, s32[1,64,256]{2,1,0:T(8,128)S(1)} %copy-done.2), custom_call_target="tpu_custom_call" | custom-call | flops 200000000 | bytes 16000000 | tf_op jit(solution)/shard_map/pallas_call | solution.py:284
  8.9 0.0 collective-permute-done.refs_1_
  9.0 0.0 collective-permute-done.2.refs_3_
  9.0 0.0 collective-permute-done.1.refs_2_
  9.0 7.4 %shard_map.47 = (f32[2,64,256]{2,1,0:T(8,128)S(1)}, f32[2,64,256]{2,1,0:T(8,128)S(1)}) custom-call(f32[1,2,9,8,128]{4,3,2,1,0:T(8,128)S(1)} %get-tuple-element.10.table_ref, f32[1,9,2,8,4,8,128]{6,5,4,3,2,1,0:T(8,128)S(1)} %get-tuple-element.11.first_ref, s32[1,64,256]{2,1,0:T(8,128)S(1)} %get-tuple-element.12.refs_0_, ...), custom_call_target="tpu_custom_call" | custom-call | tf_op jit(solution)/shard_map/pallas_call | solution.py:307
  16.4 0.2 collective-permute-start.3
  16.6 1.2 %collective-permute-done.3 = f32[2,64,256]{2,1,0:T(8,128)S(1)} collective-permute-done((f32[2,64,256]{2,1,0:T(8,128)S(1)}, f32[2,64,256]{2,1,0:T(8,128)S(1)}, u32[]{:S(2)}, u32[]{:S(2)}) %collective-permute-start.3) | collective-permute-done | bytes 131104 | tf_op jit(solution)/shard_map/ppermute | solution.py:20
  17.8 2.1 %collective-permute-start.4 = (f32[1,1,64,256]{3,2,1,0:T(8,128)S(1)}, f32[1,1,64,256]{3,2,1,0:T(8,128)S(1)}, u32[]{:S(2)}, u32[]{:S(2)}) collective-permute-start(f32[1,1,64,256]{3,2,1,0:T(8,128)S(1)} %slice_bitcast_fusion), channel_id=1, source_target_pairs={{0,16},{8,24},{16,0},{24,8},{1,17},{9,25},{17,1},{25,9},{2,18},{10... | collective-permute-start | bytes 196616 | tf_op jit(solution)/shard_map/ppermute | solution.py:20
  19.9 2.4 %collective-permute-done.4 = f32[1,1,64,256]{3,2,1,0:T(8,128)S(1)} collective-permute-done((f32[1,1,64,256]{3,2,1,0:T(8,128)S(1)}, f32[1,1,64,256]{3,2,1,0:T(8,128)S(1)}, u32[]{:S(2)}, u32[]{:S(2)}) %collective-permute-start.4) | collective-permute-done | bytes 65568 | tf_op jit(solution)/shard_map/ppermute | solution.py:20
  22.4 2.9 %collective-permute-start.7 = (f32[1,64,256]{2,1,0:T(8,128)S(1)}, f32[1,64,256]{2,1,0:T(8,128)S(1)}, u32[]{:S(2)}, u32[]{:S(2)}) collective-permute-start(f32[1,64,256]{2,1,0:T(8,128)S(1)} %fusion.1), channel_id=1, source_target_pairs={{0,3},{1,2},{2,1},{3,0},{4,7},{5,6},{6,5},{7,4},{8,11},{9,10},{10,... | collective-permute-start | bytes 196616 | tf_op jit(solution)/shard_map/ppermute | solution.py:20
  25.3 0.4 %collective-permute-start.6 = (f32[1,64,256]{2,1,0:T(8,128)S(1)}, f32[1,64,256]{2,1,0:T(8,128)S(1)}, u32[]{:S(2)}, u32[]{:S(2)}) collective-permute-start(f32[1,64,256]{2,1,0:T(8,128)S(1)} %fusion.1), channel_id=1, source_target_pairs={{0,2},{1,3},{2,0},{3,1},{4,6},{5,7},{6,4},{7,5},{8,10},{9,11},{10,... | collective-permute-start | bytes 196616 | tf_op jit(solution)/shard_map/ppermute | solution.py:20
  25.7 0.2 collective-permute-start.5
  25.9 2.2 %collective-permute-done.7 = f32[1,64,256]{2,1,0:T(8,128)S(1)} collective-permute-done((f32[1,64,256]{2,1,0:T(8,128)S(1)}, f32[1,64,256]{2,1,0:T(8,128)S(1)}, u32[]{:S(2)}, u32[]{:S(2)}) %collective-permute-start.7) | collective-permute-done | bytes 65568 | tf_op jit(solution)/shard_map/ppermute | solution.py:20
  28.1 1.5 %collective-permute-done.6 = f32[1,64,256]{2,1,0:T(8,128)S(1)} collective-permute-done((f32[1,64,256]{2,1,0:T(8,128)S(1)}, f32[1,64,256]{2,1,0:T(8,128)S(1)}, u32[]{:S(2)}, u32[]{:S(2)}) %collective-permute-start.6) | collective-permute-done | bytes 65568 | tf_op jit(solution)/shard_map/ppermute | solution.py:20
  29.5 0.4 %collective-permute-done.5 = f32[1,64,256]{2,1,0:T(8,128)S(1)} collective-permute-done((f32[1,64,256]{2,1,0:T(8,128)S(1)}, f32[1,64,256]{2,1,0:T(8,128)S(1)}, u32[]{:S(2)}, u32[]{:S(2)}) %collective-permute-start.5) | collective-permute-done | bytes 65568 | tf_op jit(solution)/shard_map/ppermute | solution.py:20
  30.0 2.7 %collective-permute-start.8 = (f32[1,64,256]{2,1,0:T(8,128)S(1)}, f32[1,64,256]{2,1,0:T(8,128)S(1)}, u32[]{:S(2)}, u32[]{:S(2)}) collective-permute-start(f32[1,64,256]{2,1,0:T(8,128)S(1)} %add_add_fusion), channel_id=1, source_target_pairs={{0,4},{1,5},{2,6},{3,7},{4,0},{5,1},{6,2},{7,3},{8,12},{9,13},{10,... | collective-permute-start | bytes 196616 | tf_op jit(solution)/shard_map/ppermute | solution.py:20
  32.7 2.6 %collective-permute-done.8 = f32[1,64,256]{2,1,0:T(8,128)S(1)} collective-permute-done((f32[1,64,256]{2,1,0:T(8,128)S(1)}, f32[1,64,256]{2,1,0:T(8,128)S(1)}, u32[]{:S(2)}, u32[]{:S(2)}) %collective-permute-start.8) | collective-permute-done | bytes 65568 | tf_op jit(solution)/shard_map/ppermute | solution.py:20
  35.2 0.6 %add.23 = f32[1,64,256]{2,1,0:T(8,128)} add(f32[1,64,256]{2,1,0:T(8,128)S(1)} %add_add_fusion, f32[1,64,256]{2,1,0:T(8,128)S(1)} %collective-permute-done.8) | non-fusion elementwise | flops 16384 | bytes 196608 | tf_op jit(solution)/shard_map/add | solution.py:334
  (4 shorter events, 0.1 us)
Async XLA Ops:
  0.0 9.0 %collective-permute-start = (s32[1,64,256]{2,1,0:T(8,128)}, s32[1,64,256]{2,1,0:T(8,128)S(1)}, u32[]{:S(2)}, u32[]{:S(2)}) collective-permute-start(s32[1,64,256]{2,1,0:T(8,128)} %vel_hbm.1), channel_id=1, source_target_pairs={{0,8},{8,0},{16,24},{24,16},{1,9},{9,1},{17,25},{25,17},{2,10},{10... | collective-permute-start | bytes 196616 | tf_op jit(solution)/shard_map/ppermute | solution.py:20
  0.5 8.5 %collective-permute-start.2 = (s32[1,64,256]{2,1,0:T(8,128)}, s32[1,64,256]{2,1,0:T(8,128)S(1)}, u32[]{:S(2)}, u32[]{:S(2)}) collective-permute-start(s32[1,64,256]{2,1,0:T(8,128)} %vel_hbm.1), channel_id=1, source_target_pairs={{0,24},{8,16},{16,8},{24,0},{1,25},{9,17},{17,9},{25,1},{2,26},{10... | collective-permute-start | bytes 196616 | tf_op jit(solution)/shard_map/ppermute | solution.py:20
  3.1 5.9 %collective-permute-start.1 = (s32[1,64,256]{2,1,0:T(8,128)}, s32[1,64,256]{2,1,0:T(8,128)S(1)}, u32[]{:S(2)}, u32[]{:S(2)}) collective-permute-start(s32[1,64,256]{2,1,0:T(8,128)} %vel_hbm.1), channel_id=1, source_target_pairs={{0,16},{8,24},{16,0},{24,8},{1,17},{9,25},{17,1},{25,9},{2,18},{10... | collective-permute-start | bytes 196616 | tf_op jit(solution)/shard_map/ppermute | solution.py:20
  3.1 1.2 %copy-start = (f32[8,2,64,256]{3,2,1,0:T(8,128)S(1)}, f32[8,2,64,256]{3,2,1,0:T(8,128)}, u32[]{:S(2)}) copy-start(f32[8,2,64,256]{3,2,1,0:T(8,128)} %surface_ref.1) | copy-start | bytes 3145732
  4.3 1.0 %copy-start.1 = (f32[2,9,32,64]{3,2,1,0:T(8,128)S(1)}, f32[2,9,32,64]{3,2,1,0:T(8,128)}, u32[]{:S(2)}) copy-start(f32[2,9,32,64]{3,2,1,0:T(8,128)} %param.6) | copy-start | bytes 442372
  5.3 0.8 %copy-start.2 = (s32[1,64,256]{2,1,0:T(8,128)S(1)}, s32[1,64,256]{2,1,0:T(8,128)}, u32[]{:S(2)}) copy-start(s32[1,64,256]{2,1,0:T(8,128)} %vel_hbm.1) | copy-start | bytes 196612
  6.1 0.7 %copy-start.3 = (s32[8]{0:T(128)S(1)}, s32[8]{0:T(128)}, u32[]{:S(2)}) copy-start(s32[8]{0:T(128)} %slot_hbm.1) | copy-start | bytes 100
  16.4 1.4 %collective-permute-start.3 = (f32[2,64,256]{2,1,0:T(8,128)S(1)}, f32[2,64,256]{2,1,0:T(8,128)S(1)}, u32[]{:S(2)}, u32[]{:S(2)}) collective-permute-start(f32[2,64,256]{2,1,0:T(8,128)S(1)} %get-tuple-element.14), channel_id=1, source_target_pairs={{0,8},{8,0},{16,24},{24,16},{1,9},{9,1},{17,25},{25,17},{2,10},{10... | collective-permute-start | bytes 393224 | tf_op jit(solution)/shard_map/ppermute | solution.py:20
  17.8 4.5 %collective-permute-start.4 = (f32[1,1,64,256]{3,2,1,0:T(8,128)S(1)}, f32[1,1,64,256]{3,2,1,0:T(8,128)S(1)}, u32[]{:S(2)}, u32[]{:S(2)}) collective-permute-start(f32[1,1,64,256]{3,2,1,0:T(8,128)S(1)} %slice_bitcast_fusion), channel_id=1, source_target_pairs={{0,16},{8,24},{16,0},{24,8},{1,17},{9,25},{17,1},{25,9},{2,18},{10... | collective-permute-start | bytes 196616 | tf_op jit(solution)/shard_map/ppermute | solution.py:20
  22.4 5.7 %collective-permute-start.7 = (f32[1,64,256]{2,1,0:T(8,128)S(1)}, f32[1,64,256]{2,1,0:T(8,128)S(1)}, u32[]{:S(2)}, u32[]{:S(2)}) collective-permute-start(f32[1,64,256]{2,1,0:T(8,128)S(1)} %fusion.1), channel_id=1, source_target_pairs={{0,3},{1,2},{2,1},{3,0},{4,7},{5,6},{6,5},{7,4},{8,11},{9,10},{10,... | collective-permute-start | bytes 196616 | tf_op jit(solution)/shard_map/ppermute | solution.py:20
  25.3 4.3 %collective-permute-start.6 = (f32[1,64,256]{2,1,0:T(8,128)S(1)}, f32[1,64,256]{2,1,0:T(8,128)S(1)}, u32[]{:S(2)}, u32[]{:S(2)}) collective-permute-start(f32[1,64,256]{2,1,0:T(8,128)S(1)} %fusion.1), channel_id=1, source_target_pairs={{0,2},{1,3},{2,0},{3,1},{4,6},{5,7},{6,4},{7,5},{8,10},{9,11},{10,... | collective-permute-start | bytes 196616 | tf_op jit(solution)/shard_map/ppermute | solution.py:20
  25.7 4.3 %collective-permute-start.5 = (f32[1,64,256]{2,1,0:T(8,128)S(1)}, f32[1,64,256]{2,1,0:T(8,128)S(1)}, u32[]{:S(2)}, u32[]{:S(2)}) collective-permute-start(f32[1,64,256]{2,1,0:T(8,128)S(1)} %fusion.1), channel_id=1, source_target_pairs={{0,1},{1,0},{2,3},{3,2},{4,5},{5,4},{6,7},{7,6},{8,9},{9,8},{10,11... | collective-permute-start | bytes 196616 | tf_op jit(solution)/shard_map/ppermute | solution.py:20
  30.0 5.2 %collective-permute-start.8 = (f32[1,64,256]{2,1,0:T(8,128)S(1)}, f32[1,64,256]{2,1,0:T(8,128)S(1)}, u32[]{:S(2)}, u32[]{:S(2)}) collective-permute-start(f32[1,64,256]{2,1,0:T(8,128)S(1)} %add_add_fusion), channel_id=1, source_target_pairs={{0,4},{1,5},{2,6},{3,7},{4,0},{5,1},{6,2},{7,3},{8,12},{9,13},{10,... | collective-permute-start | bytes 196616 | tf_op jit(solution)/shard_map/ppermute | solution.py:20

commit v4 on v3

--- a/solution.py
+++ b/solution.py
@@ -166,7 +166,7 @@
 def image_kernel(sizes, scale, table_ref, first_ref, *refs):
     groups, depth_count, levels, terms = sizes
     vel_refs = refs[:depth_count]
-    keep_ref, send_ref, numbers, halves, index_ref, layers, basis = refs[depth_count:]
+    keep_ref, send_ref, numbers, index_ref, layers, basis = refs[depth_count:]
     depth_pos = lax.axis_index("depth")
     depths = depth_count * levels
     columns = QUAD * ENTRY_SPAN
@@ -217,7 +217,7 @@
                     basis[g, 0, 0, x, y] = real
                     basis[g, 0, 1, x, y] = imag
                     layer = real if layer is None else layer + real
-                layers[z, y, x * SUB : (x + 1) * SUB] = layer * scale
+                layers[z, y, pl.ds(x, SUB, stride=SUB)] = layer * scale
 
         @pl.when(z < depths - 1)
         def _():
@@ -236,33 +236,33 @@
 
     turned = lax.broadcasted_iota(jnp.int32, (LANES, columns), 0) % ENTRY_SPAN * QUAD
     wanted = lax.broadcasted_iota(jnp.int32, (LANES, columns), 1)
-    joins = [(wanted == turned + y).astype(jnp.float32).astype(jnp.bfloat16) for y in range(QUAD)]
-
-    def join(z, carry):
+    joins = jnp.concatenate([(wanted == turned + y).astype(jnp.float32).astype(jnp.bfloat16) for y in range(QUAD)], axis=0)
+    rows = layers.shape[2]
+    chunk = math.gcd(depths, 4)
+
+    def join(step, carry):
+        rest = jnp.concatenate(
+            [jnp.concatenate([layers[step * chunk + i, y] for y in range(QUAD)], axis=1) for i in range(chunk)], axis=0
+        )
         whole = None
-        for y in range(QUAD):
-            rest = layers[z, y]
-            for part in range(3):
-                piece = rest.astype(jnp.bfloat16)
-                rest = rest - piece.astype(jnp.float32)
-                product = jnp.dot(piece, joins[y], preferred_element_type=jnp.float32)
-                whole = product if whole is None else whole + product
-        for h in range(2):
-            for x in range(SUB):
-                halves[h, pl.ds(x, SUB, stride=SUB)] = whole[x * SUB : (x + 1) * SUB, h * LANES : (h + 1) * LANES]
-        place = jnp.bitwise_xor(z // levels, depth_pos)
-        level = z % levels
-
-        def emit(ref):
-            at = (place // 2) * levels + level
-            for h in range(2):
-                ref[at, :, h * LANES : (h + 1) * LANES] = halves[h]
-
-        pl.when(place % 2 == 0)(functools.partial(emit, keep_ref))
-        pl.when(place % 2 == 1)(functools.partial(emit, send_ref))
+        for part in range(2):
+            piece = rest.astype(jnp.bfloat16)
+            rest = rest - piece.astype(jnp.float32)
+            product = jnp.dot(piece, joins, preferred_element_type=jnp.float32)
+            whole = product if whole is None else whole + product
+        for i in range(chunk):
+            z = step * chunk + i
+            place = jnp.bitwise_xor(z // levels, depth_pos)
+            level = z % levels
+
+            def emit(ref):
+                ref[(place // 2) * levels + level] = whole[i * rows : (i + 1) * rows]
+
+            pl.when(place % 2 == 0)(functools.partial(emit, keep_ref))
+            pl.when(place % 2 == 1)(functools.partial(emit, send_ref))
         return carry
 
-    lax.fori_loop(0, depths, join, 0)
+    lax.fori_loop(0, depths // chunk, join, 0)
 
 
 def per_device(surface, freq_slot, tap_table, vel_index):
@@ -300,7 +300,12 @@
         ],
         compiler_params=params,
         cost_estimate=pl.CostEstimate(flops=200_000_000, bytes_accessed=16_000_000, transcendentals=0),
-    )(freq_slot, surface, tap_table.reshape(2 * terms * entries, table_freqs), vel_index)
+    )(
+        *[
+            pltpu.with_memory_space_constraint(array, pltpu.HBM)
+            for array in (freq_slot, surface, tap_table.reshape(2 * terms * entries, table_freqs), vel_index)
+        ]
+    )
 
     scale = 1.0 / math.sqrt(local_count * freq_count)
     half = jax.ShapeDtypeStruct((depths // 2, rows, columns), jnp.float32)
@@ -311,7 +316,6 @@
         out_specs=(vmem, vmem),
         scratch_shapes=[
             pltpu.VMEM((QUAD, rows, LANES), jnp.int32),
-            pltpu.VMEM((2, rows, LANES), jnp.float32),
             pltpu.VMEM((depths, SUB, QUAD, SUB, LANES), jnp.int32),
             pltpu.VMEM((depths, QUAD, rows, LANES), jnp.float32),
             pltpu.VMEM(basis_shape, jnp.float32),

time: 36.1 us -> 33.3 us (0.922)
  local copies, waits for them, and re-layouts: 3.69 us -> 0.01 us
  waiting for transfers between devices: 10.3 us -> 12.4 us
  starting transfers between devices: 11.6 us -> 10.8 us
  Pallas kernels: 9.58 us -> 9.17 us
    unnamed x8 -> x0, local copies, waits for them, and re-layouts: 3.68 us -> none
    ppermute x9, waiting for transfers between devices: 10.3 us -> 12.4 us  [exchange(): return lax.ppermute(value, axis, [(i, i ^ flip) for i in range(count)])]
    pallas_call x1, Pallas kernels: 7.41 us -> 6.58 us  [per_device(): pl.pallas_call(functools.partial(image_kernel, (groups, depth_count, leve...]
    ppermute x9, starting transfers between devices: 11.6 us -> 10.8 us  [exchange(): return lax.ppermute(value, axis, [(i, i ^ flip) for i in range(count)])]
    pallas_call x1, Pallas kernels: 2.17 us -> 2.59 us  [per_device(): pl.pallas_call(functools.partial(first_kernel, (groups, count, local_coun...]
  transfers between devices with their start and end apart: 9 -> 9, of which waited for: 6 -> 8; matrix products, arithmetic and copies ran while one was open for 0% -> 0% of each run, Pallas kernels for 6% -> 8%
where the time goes in v4:
time: 33.3 us; the launch traced here: 33.1 us
  waiting for transfers between devices  12.4 us (37%)
  starting transfers between devices  10.8 us (32%)
  Pallas kernels  9.17 us (28%)
  other arithmetic  0.68 us (2%)
    ppermute x9, waiting for transfers between devices, exchange(): return lax.ppermute(value, axis, [(i, i ^ flip) for i in range(count)])  12.4 us
    ppermute x9, starting transfers between devices, exchange(): return lax.ppermute(value, axis, [(i, i ^ flip) for i in range(count)])  10.8 us
    pallas_call x1, Pallas kernels, per_device(): pl.pallas_call(functools.partial(image_kernel, (groups, depth_count, leve...  6.58 us
    pallas_call x1, Pallas kernels, per_device(): pl.pallas_call(functools.partial(first_kernel, (groups, count, local_coun...  2.59 us
  transfers between devices with their start and end apart: 9, of which 8 were waited for; matrix products, arithmetic and copies ran while one was open for 0% of the time, Pallas kernels for 8%

profile of v4, /device:TPU:0, one launch (start us, length us, event | category | flops | bytes accessed | tf_op | source)
XLA Modules:
  0.0 33.1 jit_solution(11043203158109217780)
XLA Ops:
  0.0 0.5 %collective-permute-start = (s32[1,64,256]{2,1,0:T(8,128)}, s32[1,64,256]{2,1,0:T(8,128)S(1)}, u32[]{:S(2)}, u32[]{:S(2)}) collective-permute-start(s32[1,64,256]{2,1,0:T(8,128)} %vel_hbm.1), channel_id=1, source_target_pairs={{0,8},{8,0},{16,24},{24,16},{1,9},{9,1},{17,25},{25,17},{2,10},{10... | collective-permute-start | bytes 196616 | tf_op jit(solution)/shard_map/ppermute | solution.py:20
  0.5 2.6 %collective-permute-start.2 = (s32[1,64,256]{2,1,0:T(8,128)}, s32[1,64,256]{2,1,0:T(8,128)S(1)}, u32[]{:S(2)}, u32[]{:S(2)}) collective-permute-start(s32[1,64,256]{2,1,0:T(8,128)} %vel_hbm.1), channel_id=1, source_target_pairs={{0,24},{8,16},{16,8},{24,0},{1,25},{9,17},{17,9},{25,1},{2,26},{10... | collective-permute-start | bytes 196616 | tf_op jit(solution)/shard_map/ppermute | solution.py:20
  3.1 0.0 collective-permute-start.1
  3.1 2.6 %shard_map.46 = (f32[1,2,9,8,128]{4,3,2,1,0:T(8,128)S(1)}, f32[1,9,2,8,4,8,128]{6,5,4,3,2,1,0:T(8,128)S(1)}, s32[1,64,256]{2,1,0:T(8,128)S(1)}) custom-call(s32[8]{0:T(128)} %slot_hbm.1, f32[8,2,64,256]{3,2,1,0:T(8,128)} %surface_ref.1, f32[576,64]{1,0:T(8,128)} %bitcast.16, s32[1,64,256]{2,1,0:T(8,128)} %vel_hbm.1), custom_call_target="tpu_custom_call" | custom-call | flops 200000000 | bytes 16000000 | tf_op jit(solution)/shard_map/pallas_call | solution.py:284
  5.7 0.0 collective-permute-done.refs_1_
  5.7 0.1 collective-permute-done.2.refs_3_
  5.8 1.7 %collective-permute-done.1.refs_2_ = s32[1,64,256]{2,1,0:T(8,128)S(1)} collective-permute-done((s32[1,64,256]{2,1,0:T(8,128)}, s32[1,64,256]{2,1,0:T(8,128)S(1)}, u32[]{:S(2)}, u32[]{:S(2)}) %collective-permute-start.1) | collective-permute-done | bytes 65568 | tf_op jit(solution)/shard_map/ppermute | solution.py:20
  7.6 6.6 %shard_map.47 = (f32[2,64,256]{2,1,0:T(8,128)S(1)}, f32[2,64,256]{2,1,0:T(8,128)S(1)}) custom-call(f32[1,2,9,8,128]{4,3,2,1,0:T(8,128)S(1)} %get-tuple-element.10.table_ref, f32[1,9,2,8,4,8,128]{6,5,4,3,2,1,0:T(8,128)S(1)} %get-tuple-element.11.first_ref, s32[1,64,256]{2,1,0:T(8,128)S(1)} %get-tuple-element.12.refs_0_, ...), custom_call_target="tpu_custom_call" | custom-call | tf_op jit(solution)/shard_map/pallas_call | solution.py:312
  14.2 0.1 collective-permute-start.3
  14.2 1.3 %collective-permute-done.3 = f32[2,64,256]{2,1,0:T(8,128)S(1)} collective-permute-done((f32[2,64,256]{2,1,0:T(8,128)S(1)}, f32[2,64,256]{2,1,0:T(8,128)S(1)}, u32[]{:S(2)}, u32[]{:S(2)}) %collective-permute-start.3) | collective-permute-done | bytes 131104 | tf_op jit(solution)/shard_map/ppermute | solution.py:20
  15.6 1.5 %collective-permute-start.4 = (f32[1,1,64,256]{3,2,1,0:T(8,128)S(1)}, f32[1,1,64,256]{3,2,1,0:T(8,128)S(1)}, u32[]{:S(2)}, u32[]{:S(2)}) collective-permute-start(f32[1,1,64,256]{3,2,1,0:T(8,128)S(1)} %slice_bitcast_fusion), channel_id=1, source_target_pairs={{0,16},{8,24},{16,0},{24,8},{1,17},{9,25},{17,1},{25,9},{2,18},{10... | collective-permute-start | bytes 196616 | tf_op jit(solution)/shard_map/ppermute | solution.py:20
  17.1 2.8 %collective-permute-done.4 = f32[1,1,64,256]{3,2,1,0:T(8,128)S(1)} collective-permute-done((f32[1,1,64,256]{3,2,1,0:T(8,128)S(1)}, f32[1,1,64,256]{3,2,1,0:T(8,128)S(1)}, u32[]{:S(2)}, u32[]{:S(2)}) %collective-permute-start.4) | collective-permute-done | bytes 65568 | tf_op jit(solution)/shard_map/ppermute | solution.py:20
  19.9 2.6 %collective-permute-start.7 = (f32[1,64,256]{2,1,0:T(8,128)S(1)}, f32[1,64,256]{2,1,0:T(8,128)S(1)}, u32[]{:S(2)}, u32[]{:S(2)}) collective-permute-start(f32[1,64,256]{2,1,0:T(8,128)S(1)} %fusion.1), channel_id=1, source_target_pairs={{0,3},{1,2},{2,1},{3,0},{4,7},{5,6},{6,5},{7,4},{8,11},{9,10},{10,... | collective-permute-start | bytes 196616 | tf_op jit(solution)/shard_map/ppermute | solution.py:20
  22.5 0.5 %collective-permute-start.6 = (f32[1,64,256]{2,1,0:T(8,128)S(1)}, f32[1,64,256]{2,1,0:T(8,128)S(1)}, u32[]{:S(2)}, u32[]{:S(2)}) collective-permute-start(f32[1,64,256]{2,1,0:T(8,128)S(1)} %fusion.1), channel_id=1, source_target_pairs={{0,2},{1,3},{2,0},{3,1},{4,6},{5,7},{6,4},{7,5},{8,10},{9,11},{10,... | collective-permute-start | bytes 196616 | tf_op jit(solution)/shard_map/ppermute | solution.py:20
  23.0 0.5 %collective-permute-start.5 = (f32[1,64,256]{2,1,0:T(8,128)S(1)}, f32[1,64,256]{2,1,0:T(8,128)S(1)}, u32[]{:S(2)}, u32[]{:S(2)}) collective-permute-start(f32[1,64,256]{2,1,0:T(8,128)S(1)} %fusion.1), channel_id=1, source_target_pairs={{0,1},{1,0},{2,3},{3,2},{4,5},{5,4},{6,7},{7,6},{8,9},{9,8},{10,11... | collective-permute-start | bytes 196616 | tf_op jit(solution)/shard_map/ppermute | solution.py:20
  23.5 1.8 %collective-permute-done.7 = f32[1,64,256]{2,1,0:T(8,128)S(1)} collective-permute-done((f32[1,64,256]{2,1,0:T(8,128)S(1)}, f32[1,64,256]{2,1,0:T(8,128)S(1)}, u32[]{:S(2)}, u32[]{:S(2)}) %collective-permute-start.7) | collective-permute-done | bytes 65568 | tf_op jit(solution)/shard_map/ppermute | solution.py:20
  25.3 1.5 %collective-permute-done.6 = f32[1,64,256]{2,1,0:T(8,128)S(1)} collective-permute-done((f32[1,64,256]{2,1,0:T(8,128)S(1)}, f32[1,64,256]{2,1,0:T(8,128)S(1)}, u32[]{:S(2)}, u32[]{:S(2)}) %collective-permute-start.6) | collective-permute-done | bytes 65568 | tf_op jit(solution)/shard_map/ppermute | solution.py:20
  26.8 0.5 %collective-permute-done.5 = f32[1,64,256]{2,1,0:T(8,128)S(1)} collective-permute-done((f32[1,64,256]{2,1,0:T(8,128)S(1)}, f32[1,64,256]{2,1,0:T(8,128)S(1)}, u32[]{:S(2)}, u32[]{:S(2)}) %collective-permute-start.5) | collective-permute-done | bytes 65568 | tf_op jit(solution)/shard_map/ppermute | solution.py:20
  27.3 2.6 %collective-permute-start.8 = (f32[1,64,256]{2,1,0:T(8,128)S(1)}, f32[1,64,256]{2,1,0:T(8,128)S(1)}, u32[]{:S(2)}, u32[]{:S(2)}) collective-permute-start(f32[1,64,256]{2,1,0:T(8,128)S(1)} %add_add_fusion), channel_id=1, source_target_pairs={{0,4},{1,5},{2,6},{3,7},{4,0},{5,1},{6,2},{7,3},{8,12},{9,13},{10,... | collective-permute-start | bytes 196616 | tf_op jit(solution)/shard_map/ppermute | solution.py:20
  29.9 2.6 %collective-permute-done.8 = f32[1,64,256]{2,1,0:T(8,128)S(1)} collective-permute-done((f32[1,64,256]{2,1,0:T(8,128)S(1)}, f32[1,64,256]{2,1,0:T(8,128)S(1)}, u32[]{:S(2)}, u32[]{:S(2)}) %collective-permute-start.8) | collective-permute-done | bytes 65568 | tf_op jit(solution)/shard_map/ppermute | solution.py:20
  32.5 0.6 %add.23 = f32[1,64,256]{2,1,0:T(8,128)} add(f32[1,64,256]{2,1,0:T(8,128)S(1)} %add_add_fusion, f32[1,64,256]{2,1,0:T(8,128)S(1)} %collective-permute-done.8) | non-fusion elementwise | flops 16384 | bytes 196608 | tf_op jit(solution)/shard_map/add | solution.py:338
  (4 shorter events, 0.1 us)
Async XLA Ops:
  0.0 5.7 %collective-permute-start = (s32[1,64,256]{2,1,0:T(8,128)}, s32[1,64,256]{2,1,0:T(8,128)S(1)}, u32[]{:S(2)}, u32[]{:S(2)}) collective-permute-start(s32[1,64,256]{2,1,0:T(8,128)} %vel_hbm.1), channel_id=1, source_target_pairs={{0,8},{8,0},{16,24},{24,16},{1,9},{9,1},{17,25},{25,17},{2,10},{10... | collective-permute-start | bytes 196616 | tf_op jit(solution)/shard_map/ppermute | solution.py:20
  0.5 5.4 %collective-permute-start.2 = (s32[1,64,256]{2,1,0:T(8,128)}, s32[1,64,256]{2,1,0:T(8,128)S(1)}, u32[]{:S(2)}, u32[]{:S(2)}) collective-permute-start(s32[1,64,256]{2,1,0:T(8,128)} %vel_hbm.1), channel_id=1, source_target_pairs={{0,24},{8,16},{16,8},{24,0},{1,25},{9,17},{17,9},{25,1},{2,26},{10... | collective-permute-start | bytes 196616 | tf_op jit(solution)/shard_map/ppermute | solution.py:20
  3.1 4.5 %collective-permute-start.1 = (s32[1,64,256]{2,1,0:T(8,128)}, s32[1,64,256]{2,1,0:T(8,128)S(1)}, u32[]{:S(2)}, u32[]{:S(2)}) collective-permute-start(s32[1,64,256]{2,1,0:T(8,128)} %vel_hbm.1), channel_id=1, source_target_pairs={{0,16},{8,24},{16,0},{24,8},{1,17},{9,25},{17,1},{25,9},{2,18},{10... | collective-permute-start | bytes 196616 | tf_op jit(solution)/shard_map/ppermute | solution.py:20
  14.2 1.4 %collective-permute-start.3 = (f32[2,64,256]{2,1,0:T(8,128)S(1)}, f32[2,64,256]{2,1,0:T(8,128)S(1)}, u32[]{:S(2)}, u32[]{:S(2)}) collective-permute-start(f32[2,64,256]{2,1,0:T(8,128)S(1)} %get-tuple-element.14), channel_id=1, source_target_pairs={{0,8},{8,0},{16,24},{24,16},{1,9},{9,1},{17,25},{25,17},{2,10},{10... | collective-permute-start | bytes 393224 | tf_op jit(solution)/shard_map/ppermute | solution.py:20
  15.6 4.3 %collective-permute-start.4 = (f32[1,1,64,256]{3,2,1,0:T(8,128)S(1)}, f32[1,1,64,256]{3,2,1,0:T(8,128)S(1)}, u32[]{:S(2)}, u32[]{:S(2)}) collective-permute-start(f32[1,1,64,256]{3,2,1,0:T(8,128)S(1)} %slice_bitcast_fusion), channel_id=1, source_target_pairs={{0,16},{8,24},{16,0},{24,8},{1,17},{9,25},{17,1},{25,9},{2,18},{10... | collective-permute-start | bytes 196616 | tf_op jit(solution)/shard_map/ppermute | solution.py:20
  19.9 5.3 %collective-permute-start.7 = (f32[1,64,256]{2,1,0:T(8,128)S(1)}, f32[1,64,256]{2,1,0:T(8,128)S(1)}, u32[]{:S(2)}, u32[]{:S(2)}) collective-permute-start(f32[1,64,256]{2,1,0:T(8,128)S(1)} %fusion.1), channel_id=1, source_target_pairs={{0,3},{1,2},{2,1},{3,0},{4,7},{5,6},{6,5},{7,4},{8,11},{9,10},{10,... | collective-permute-start | bytes 196616 | tf_op jit(solution)/shard_map/ppermute | solution.py:20
  22.5 4.3 %collective-permute-start.6 = (f32[1,64,256]{2,1,0:T(8,128)S(1)}, f32[1,64,256]{2,1,0:T(8,128)S(1)}, u32[]{:S(2)}, u32[]{:S(2)}) collective-permute-start(f32[1,64,256]{2,1,0:T(8,128)S(1)} %fusion.1), channel_id=1, source_target_pairs={{0,2},{1,3},{2,0},{3,1},{4,6},{5,7},{6,4},{7,5},{8,10},{9,11},{10,... | collective-permute-start | bytes 196616 | tf_op jit(solution)/shard_map/ppermute | solution.py:20
  23.0 4.3 %collective-permute-start.5 = (f32[1,64,256]{2,1,0:T(8,128)S(1)}, f32[1,64,256]{2,1,0:T(8,128)S(1)}, u32[]{:S(2)}, u32[]{:S(2)}) collective-permute-start(f32[1,64,256]{2,1,0:T(8,128)S(1)} %fusion.1), channel_id=1, source_target_pairs={{0,1},{1,0},{2,3},{3,2},{4,5},{5,4},{6,7},{7,6},{8,9},{9,8},{10,11... | collective-permute-start | bytes 196616 | tf_op jit(solution)/shard_map/ppermute | solution.py:20
  27.3 5.2 %collective-permute-start.8 = (f32[1,64,256]{2,1,0:T(8,128)S(1)}, f32[1,64,256]{2,1,0:T(8,128)S(1)}, u32[]{:S(2)}, u32[]{:S(2)}) collective-permute-start(f32[1,64,256]{2,1,0:T(8,128)S(1)} %add_add_fusion), channel_id=1, source_target_pairs={{0,4},{1,5},{2,6},{3,7},{4,0},{5,1},{6,2},{7,3},{8,12},{9,13},{10,... | collective-permute-start | bytes 196616 | tf_op jit(solution)/shard_map/ppermute | solution.py:20

commit v5 on v4

--- a/solution.py
+++ b/solution.py
@@ -258,8 +258,9 @@
             def emit(ref):
                 ref[(place // 2) * levels + level] = whole[i * rows : (i + 1) * rows]
 
-            pl.when(place % 2 == 0)(functools.partial(emit, keep_ref))
-            pl.when(place % 2 == 1)(functools.partial(emit, send_ref))
+            side = jnp.bitwise_xor(place, place // 2) % 2
+            pl.when(side == 0)(functools.partial(emit, keep_ref))
+            pl.when(side == 1)(functools.partial(emit, send_ref))
         return carry
 
     lax.fori_loop(0, depths // chunk, join, 0)
@@ -277,7 +278,8 @@
     vmem = pl.BlockSpec(memory_space=pltpu.VMEM)
     params = pltpu.CompilerParams(vmem_limit_bytes=40 * 1024 * 1024)
 
-    vels = [exchange(vel_index, "depth", flip) for flip in range(1, depth_count)]
+    near = exchange(vel_index, "depth", 1)
+    far = [exchange(vel_index, "depth", flip) for flip in range(2, depth_count, 2)]
 
     basis_shape = (groups, terms, 2, SUB, QUAD, SUB, LANES)
     hbm = pl.BlockSpec(memory_space=pltpu.HBM)
@@ -307,6 +309,11 @@
         ]
     )
 
+    vels = [near]
+    for value in far:
+        value, table = lax.optimization_barrier((value, table))
+        vels += [value, exchange(value, "depth", 1)]
+
     scale = 1.0 / math.sqrt(local_count * freq_count)
     half = jax.ShapeDtypeStruct((depths // 2, rows, columns), jnp.float32)
     keep, send = pl.pallas_call(
@@ -327,7 +334,8 @@
     distance = 2
     while distance < depth_count:
         image = image.reshape((-1, 2, levels, rows, columns))
-        image = (image[:, 0] + exchange(image[:, 1], "depth", distance)).reshape((-1, rows, columns))
+        flip = 3 if distance == 2 else distance
+        image = (image[:, 0] + exchange(image[:, 1], "depth", flip)).reshape((-1, rows, columns))
         distance *= 2
     distance = 1
     while distance < freq_count:

time: 33.3 us -> 32.7 us (0.982)
  waiting for transfers between devices: 12.4 us -> 11 us
  starting transfers between devices: 10.8 us -> 11.6 us
    ppermute x9, waiting for transfers between devices: 12.4 us -> 11 us  [exchange(): return lax.ppermute(value, axis, [(i, i ^ flip) for i in range(count)])]
    ppermute x9, starting transfers between devices: 10.8 us -> 11.6 us  [exchange(): return lax.ppermute(value, axis, [(i, i ^ flip) for i in range(count)])]
  transfers between devices with their start and end apart: 9 -> 9, of which waited for: 8 -> 7; matrix products, arithmetic and copies ran while one was open for 0% -> 0% of each run, Pallas kernels for 8% -> 8%
where the time goes in v5:
time: 32.7 us; the launch traced here: 32.5 us
  starting transfers between devices  11.6 us (35%)
  waiting for transfers between devices  11 us (34%)
  Pallas kernels  9.17 us (28%)
  other arithmetic  0.68 us (2%)
    ppermute x9, starting transfers between devices, exchange(): return lax.ppermute(value, axis, [(i, i ^ flip) for i in range(count)])  11.6 us
    ppermute x9, waiting for transfers between devices, exchange(): return lax.ppermute(value, axis, [(i, i ^ flip) for i in range(count)])  11 us
    pallas_call x1, Pallas kernels, per_device(): pl.pallas_call(functools.partial(image_kernel, (groups, depth_count, leve...  6.58 us
    pallas_call x1, Pallas kernels, per_device(): pl.pallas_call(functools.partial(first_kernel, (groups, count, local_coun...  2.59 us
  transfers between devices with their start and end apart: 9, of which 7 were waited for; matrix products, arithmetic and copies ran while one was open for 0% of the time, Pallas kernels for 8%

profile of v5, /device:TPU:0, one launch (start us, length us, event | category | flops | bytes accessed | tf_op | source)
XLA Modules:
  0.0 32.5 jit_solution(15354783279844672062)
XLA Ops:
  0.0 3.0 %collective-permute-start = (s32[1,64,256]{2,1,0:T(8,128)}, s32[1,64,256]{2,1,0:T(8,128)S(1)}, u32[]{:S(2)}, u32[]{:S(2)}) collective-permute-start(s32[1,64,256]{2,1,0:T(8,128)} %vel_hbm.1), channel_id=1, source_target_pairs={{0,16},{8,24},{16,0},{24,8},{1,17},{9,25},{17,1},{25,9},{2,18},{10... | collective-permute-start | bytes 196616 | tf_op jit(solution)/shard_map/ppermute | solution.py:20
  3.0 0.0 collective-permute-start.1
  3.0 2.6 %shard_map.46 = (f32[1,2,9,8,128]{4,3,2,1,0:T(8,128)S(1)}, f32[1,9,2,8,4,8,128]{6,5,4,3,2,1,0:T(8,128)S(1)}, s32[1,64,256]{2,1,0:T(8,128)S(1)}) custom-call(s32[8]{0:T(128)} %slot_hbm.1, f32[8,2,64,256]{3,2,1,0:T(8,128)} %surface_ref.1, f32[576,64]{1,0:T(8,128)} %bitcast.16, s32[1,64,256]{2,1,0:T(8,128)} %vel_hbm.1), custom_call_target="tpu_custom_call" | custom-call | flops 200000000 | bytes 16000000 | tf_op jit(solution)/shard_map/pallas_call | solution.py:286
  5.6 0.0 collective-permute-done.refs_2_
  5.6 0.6 %collective-permute-start.2 = (s32[1,64,256]{2,1,0:T(8,128)S(1)}, s32[1,64,256]{2,1,0:T(8,128)S(1)}, u32[]{:S(2)}, u32[]{:S(2)}) collective-permute-start(s32[1,64,256]{2,1,0:T(8,128)S(1)} %collective-permute-done.refs_2_), channel_id=1, source_target_pairs={{0,8},{8,0},{16,24},{24,16},{1,9},{9,1},{17,25},{25,17},{2,10},{10... | collective-permute-start | bytes 196616 | tf_op jit(solution)/shard_map/ppermute | solution.py:20
  6.2 0.0 collective-permute-done.1.refs_1_
  6.2 0.9 %collective-permute-done.2.refs_3_ = s32[1,64,256]{2,1,0:T(8,128)S(1)} collective-permute-done((s32[1,64,256]{2,1,0:T(8,128)S(1)}, s32[1,64,256]{2,1,0:T(8,128)S(1)}, u32[]{:S(2)}, u32[]{:S(2)}) %collective-permute-start.2) | collective-permute-done | bytes 65568 | tf_op jit(solution)/shard_map/ppermute | solution.py:20
  7.1 6.6 %shard_map.47 = (f32[2,64,256]{2,1,0:T(8,128)S(1)}, f32[2,64,256]{2,1,0:T(8,128)S(1)}) custom-call(f32[1,2,9,8,128]{4,3,2,1,0:T(8,128)S(1)} %get-tuple-element.13.table_ref, f32[1,9,2,8,4,8,128]{6,5,4,3,2,1,0:T(8,128)S(1)} %get-tuple-element.14.first_ref, s32[1,64,256]{2,1,0:T(8,128)S(1)} %get-tuple-element.15.refs_0_, ...), custom_call_target="tpu_custom_call" | custom-call | tf_op jit(solution)/shard_map/pallas_call | solution.py:319
  13.6 0.4 %collective-permute-start.3 = (f32[2,64,256]{2,1,0:T(8,128)S(1)}, f32[2,64,256]{2,1,0:T(8,128)S(1)}, u32[]{:S(2)}, u32[]{:S(2)}) collective-permute-start(f32[2,64,256]{2,1,0:T(8,128)S(1)} %get-tuple-element.18), channel_id=1, source_target_pairs={{0,8},{8,0},{16,24},{24,16},{1,9},{9,1},{17,25},{25,17},{2,10},{10... | collective-permute-start | bytes 393224 | tf_op jit(solution)/shard_map/ppermute | solution.py:20
  14.1 1.0 %collective-permute-done.3 = f32[2,64,256]{2,1,0:T(8,128)S(1)} collective-permute-done((f32[2,64,256]{2,1,0:T(8,128)S(1)}, f32[2,64,256]{2,1,0:T(8,128)S(1)}, u32[]{:S(2)}, u32[]{:S(2)}) %collective-permute-start.3) | collective-permute-done | bytes 131104 | tf_op jit(solution)/shard_map/ppermute | solution.py:20
  15.1 1.5 %collective-permute-start.4 = (f32[1,1,64,256]{3,2,1,0:T(8,128)S(1)}, f32[1,1,64,256]{3,2,1,0:T(8,128)S(1)}, u32[]{:S(2)}, u32[]{:S(2)}) collective-permute-start(f32[1,1,64,256]{3,2,1,0:T(8,128)S(1)} %slice_bitcast_fusion), channel_id=1, source_target_pairs={{0,24},{8,16},{16,8},{24,0},{1,25},{9,17},{17,9},{25,1},{2,26},{10... | collective-permute-start | bytes 196616 | tf_op jit(solution)/shard_map/ppermute | solution.py:20
  16.6 2.5 %collective-permute-done.4 = f32[1,1,64,256]{3,2,1,0:T(8,128)S(1)} collective-permute-done((f32[1,1,64,256]{3,2,1,0:T(8,128)S(1)}, f32[1,1,64,256]{3,2,1,0:T(8,128)S(1)}, u32[]{:S(2)}, u32[]{:S(2)}) %collective-permute-start.4) | collective-permute-done | bytes 65568 | tf_op jit(solution)/shard_map/ppermute | solution.py:20
  19.1 2.8 %collective-permute-start.7 = (f32[1,64,256]{2,1,0:T(8,128)S(1)}, f32[1,64,256]{2,1,0:T(8,128)S(1)}, u32[]{:S(2)}, u32[]{:S(2)}) collective-permute-start(f32[1,64,256]{2,1,0:T(8,128)S(1)} %fusion.1), channel_id=1, source_target_pairs={{0,3},{1,2},{2,1},{3,0},{4,7},{5,6},{6,5},{7,4},{8,11},{9,10},{10,... | collective-permute-start | bytes 196616 | tf_op jit(solution)/shard_map/ppermute | solution.py:20
  21.9 0.5 %collective-permute-start.6 = (f32[1,64,256]{2,1,0:T(8,128)S(1)}, f32[1,64,256]{2,1,0:T(8,128)S(1)}, u32[]{:S(2)}, u32[]{:S(2)}) collective-permute-start(f32[1,64,256]{2,1,0:T(8,128)S(1)} %fusion.1), channel_id=1, source_target_pairs={{0,2},{1,3},{2,0},{3,1},{4,6},{5,7},{6,4},{7,5},{8,10},{9,11},{10,... | collective-permute-start | bytes 196616 | tf_op jit(solution)/shard_map/ppermute | solution.py:20
  22.4 0.3 collective-permute-start.5
  22.7 1.7 %collective-permute-done.7 = f32[1,64,256]{2,1,0:T(8,128)S(1)} collective-permute-done((f32[1,64,256]{2,1,0:T(8,128)S(1)}, f32[1,64,256]{2,1,0:T(8,128)S(1)}, u32[]{:S(2)}, u32[]{:S(2)}) %collective-permute-start.7) | collective-permute-done | bytes 65568 | tf_op jit(solution)/shard_map/ppermute | solution.py:20
  24.3 1.9 %collective-permute-done.6 = f32[1,64,256]{2,1,0:T(8,128)S(1)} collective-permute-done((f32[1,64,256]{2,1,0:T(8,128)S(1)}, f32[1,64,256]{2,1,0:T(8,128)S(1)}, u32[]{:S(2)}, u32[]{:S(2)}) %collective-permute-start.6) | collective-permute-done | bytes 65568 | tf_op jit(solution)/shard_map/ppermute | solution.py:20
  26.2 0.5 %collective-permute-done.5 = f32[1,64,256]{2,1,0:T(8,128)S(1)} collective-permute-done((f32[1,64,256]{2,1,0:T(8,128)S(1)}, f32[1,64,256]{2,1,0:T(8,128)S(1)}, u32[]{:S(2)}, u32[]{:S(2)}) %collective-permute-start.5) | collective-permute-done | bytes 65568 | tf_op jit(solution)/shard_map/ppermute | solution.py:20
  26.7 2.7 %collective-permute-start.8 = (f32[1,64,256]{2,1,0:T(8,128)S(1)}, f32[1,64,256]{2,1,0:T(8,128)S(1)}, u32[]{:S(2)}, u32[]{:S(2)}) collective-permute-start(f32[1,64,256]{2,1,0:T(8,128)S(1)} %add_add_fusion), channel_id=1, source_target_pairs={{0,4},{1,5},{2,6},{3,7},{4,0},{5,1},{6,2},{7,3},{8,12},{9,13},{10,... | collective-permute-start | bytes 196616 | tf_op jit(solution)/shard_map/ppermute | solution.py:20
  29.3 2.6 %collective-permute-done.8 = f32[1,64,256]{2,1,0:T(8,128)S(1)} collective-permute-done((f32[1,64,256]{2,1,0:T(8,128)S(1)}, f32[1,64,256]{2,1,0:T(8,128)S(1)}, u32[]{:S(2)}, u32[]{:S(2)}) %collective-permute-start.8) | collective-permute-done | bytes 65568 | tf_op jit(solution)/shard_map/ppermute | solution.py:20
  31.9 0.6 %add.23 = f32[1,64,256]{2,1,0:T(8,128)} add(f32[1,64,256]{2,1,0:T(8,128)S(1)} %add_add_fusion, f32[1,64,256]{2,1,0:T(8,128)S(1)} %collective-permute-done.8) | non-fusion elementwise | flops 16384 | bytes 196608 | tf_op jit(solution)/shard_map/add | solution.py:346
  (4 shorter events, 0.1 us)
Async XLA Ops:
  0.0 5.6 %collective-permute-start = (s32[1,64,256]{2,1,0:T(8,128)}, s32[1,64,256]{2,1,0:T(8,128)S(1)}, u32[]{:S(2)}, u32[]{:S(2)}) collective-permute-start(s32[1,64,256]{2,1,0:T(8,128)} %vel_hbm.1), channel_id=1, source_target_pairs={{0,16},{8,24},{16,0},{24,8},{1,17},{9,25},{17,1},{25,9},{2,18},{10... | collective-permute-start | bytes 196616 | tf_op jit(solution)/shard_map/ppermute | solution.py:20
  3.0 3.2 %collective-permute-start.1 = (s32[1,64,256]{2,1,0:T(8,128)}, s32[1,64,256]{2,1,0:T(8,128)S(1)}, u32[]{:S(2)}, u32[]{:S(2)}) collective-permute-start(s32[1,64,256]{2,1,0:T(8,128)} %vel_hbm.1), channel_id=1, source_target_pairs={{0,8},{8,0},{16,24},{24,16},{1,9},{9,1},{17,25},{25,17},{2,10},{10... | collective-permute-start | bytes 196616 | tf_op jit(solution)/shard_map/ppermute | solution.py:20
  5.6 1.5 %collective-permute-start.2 = (s32[1,64,256]{2,1,0:T(8,128)S(1)}, s32[1,64,256]{2,1,0:T(8,128)S(1)}, u32[]{:S(2)}, u32[]{:S(2)}) collective-permute-start(s32[1,64,256]{2,1,0:T(8,128)S(1)} %collective-permute-done.refs_2_), channel_id=1, source_target_pairs={{0,8},{8,0},{16,24},{24,16},{1,9},{9,1},{17,25},{25,17},{2,10},{10... | collective-permute-start | bytes 196616 | tf_op jit(solution)/shard_map/ppermute | solution.py:20
  13.6 1.4 %collective-permute-start.3 = (f32[2,64,256]{2,1,0:T(8,128)S(1)}, f32[2,64,256]{2,1,0:T(8,128)S(1)}, u32[]{:S(2)}, u32[]{:S(2)}) collective-permute-start(f32[2,64,256]{2,1,0:T(8,128)S(1)} %get-tuple-element.18), channel_id=1, source_target_pairs={{0,8},{8,0},{16,24},{24,16},{1,9},{9,1},{17,25},{25,17},{2,10},{10... | collective-permute-start | bytes 393224 | tf_op jit(solution)/shard_map/ppermute | solution.py:20
  15.1 4.0 %collective-permute-start.4 = (f32[1,1,64,256]{3,2,1,0:T(8,128)S(1)}, f32[1,1,64,256]{3,2,1,0:T(8,128)S(1)}, u32[]{:S(2)}, u32[]{:S(2)}) collective-permute-start(f32[1,1,64,256]{3,2,1,0:T(8,128)S(1)} %slice_bitcast_fusion), channel_id=1, source_target_pairs={{0,24},{8,16},{16,8},{24,0},{1,25},{9,17},{17,9},{25,1},{2,26},{10... | collective-permute-start | bytes 196616 | tf_op jit(solution)/shard_map/ppermute | solution.py:20
  19.1 5.2 %collective-permute-start.7 = (f32[1,64,256]{2,1,0:T(8,128)S(1)}, f32[1,64,256]{2,1,0:T(8,128)S(1)}, u32[]{:S(2)}, u32[]{:S(2)}) collective-permute-start(f32[1,64,256]{2,1,0:T(8,128)S(1)} %fusion.1), channel_id=1, source_target_pairs={{0,3},{1,2},{2,1},{3,0},{4,7},{5,6},{6,5},{7,4},{8,11},{9,10},{10,... | collective-permute-start | bytes 196616 | tf_op jit(solution)/shard_map/ppermute | solution.py:20
  21.9 4.3 %collective-permute-start.6 = (f32[1,64,256]{2,1,0:T(8,128)S(1)}, f32[1,64,256]{2,1,0:T(8,128)S(1)}, u32[]{:S(2)}, u32[]{:S(2)}) collective-permute-start(f32[1,64,256]{2,1,0:T(8,128)S(1)} %fusion.1), channel_id=1, source_target_pairs={{0,2},{1,3},{2,0},{3,1},{4,6},{5,7},{6,4},{7,5},{8,10},{9,11},{10,... | collective-permute-start | bytes 196616 | tf_op jit(solution)/shard_map/ppermute | solution.py:20
  22.4 4.3 %collective-permute-start.5 = (f32[1,64,256]{2,1,0:T(8,128)S(1)}, f32[1,64,256]{2,1,0:T(8,128)S(1)}, u32[]{:S(2)}, u32[]{:S(2)}) collective-permute-start(f32[1,64,256]{2,1,0:T(8,128)S(1)} %fusion.1), channel_id=1, source_target_pairs={{0,1},{1,0},{2,3},{3,2},{4,5},{5,4},{6,7},{7,6},{8,9},{9,8},{10,11... | collective-permute-start | bytes 196616 | tf_op jit(solution)/shard_map/ppermute | solution.py:20
  26.7 5.2 %collective-permute-start.8 = (f32[1,64,256]{2,1,0:T(8,128)S(1)}, f32[1,64,256]{2,1,0:T(8,128)S(1)}, u32[]{:S(2)}, u32[]{:S(2)}) collective-permute-start(f32[1,64,256]{2,1,0:T(8,128)S(1)} %add_add_fusion), channel_id=1, source_target_pairs={{0,4},{1,5},{2,6},{3,7},{4,0},{5,1},{6,2},{7,3},{8,12},{9,13},{10,... | collective-permute-start | bytes 196616 | tf_op jit(solution)/shard_map/ppermute | solution.py:20

commit v6 on v5

--- a/solution.py
+++ b/solution.py
@@ -13,6 +13,7 @@
 PAIR = 2
 QUAD = 4
 ENTRY_SPAN = LANES // PAIR
+EARLY = 2
 
 
 def exchange(value, axis, flip):
@@ -163,23 +164,14 @@
     vel_copy.wait()
 
 
-def image_kernel(sizes, scale, table_ref, first_ref, *refs):
-    groups, depth_count, levels, terms = sizes
-    vel_refs = refs[:depth_count]
-    keep_ref, send_ref, numbers, index_ref, layers, basis = refs[depth_count:]
-    depth_pos = lax.axis_index("depth")
-    depths = depth_count * levels
+def place_velocities(vel_refs, targets, numbers, index_ref):
     columns = QUAD * ENTRY_SPAN
-    masks = edge_masks()
-
     source = lax.broadcasted_iota(jnp.int32, (columns, QUAD * LANES), 0)
     place = lax.broadcasted_iota(jnp.int32, (columns, QUAD * LANES), 1)
     split = (source == (place % ENTRY_SPAN) * QUAD + place // LANES).astype(jnp.float32).astype(jnp.bfloat16)
-
     table_base = jnp.where(lane_number() < ENTRY_SPAN, 0, ENTRY_SPAN)
-    for slot, vel_ref in enumerate(vel_refs):
-        target = jnp.bitwise_xor(depth_pos, slot) * levels
-        for level in range(levels):
+    for vel_ref, target in zip(vel_refs, targets):
+        for level in range(vel_ref.shape[0]):
             spread = jnp.dot(
                 vel_ref[level].astype(jnp.float32).astype(jnp.bfloat16), split, preferred_element_type=jnp.float32
             ).astype(jnp.int32)
@@ -189,6 +181,35 @@
                 for y in range(QUAD):
                     index_ref[target + level, x, y] = numbers[y, pl.ds(x, SUB, stride=SUB)] + table_base
 
+
+def early_kernel(sizes, table_ref, *refs):
+    groups, levels, terms = sizes
+    vel_refs = refs[:-3]
+    coef_ref, numbers, index_ref = refs[-3:]
+    place_velocities(vel_refs, [slot * levels for slot in range(len(vel_refs))], numbers, index_ref)
+    for z in range(len(vel_refs) * levels):
+        for x in range(SUB):
+            for y in range(QUAD):
+                index = index_ref[z, x, y]
+                for g in range(groups):
+                    for c in range(2):
+                        for k in range(terms):
+                            coef_ref[z, g, c, k, x, y] = lane_take(table_ref[g, c, k], index)
+
+
+def image_kernel(sizes, scale, table_ref, first_ref, coef_ref, *refs):
+    groups, depth_count, levels, terms = sizes
+    early = coef_ref.shape[0] // levels
+    vel_refs = refs[: depth_count - early]
+    keep_ref, send_ref, numbers, index_ref, layers, basis = refs[depth_count - early :]
+    depth_pos = lax.axis_index("depth")
+    depths = depth_count * levels
+    columns = QUAD * ENTRY_SPAN
+    masks = edge_masks()
+
+    targets = [jnp.bitwise_xor(depth_pos, slot) * levels for slot in range(early, depth_count)]
+    place_velocities(vel_refs, targets, numbers, index_ref)
+
     def first_terms(k, carry):
         for g in range(groups):
             for c in range(2):
@@ -197,16 +218,15 @@
 
     lax.fori_loop(0, terms, first_terms, 0)
 
-    def depth_step(z, carry):
+    def accumulate(z, coefficients):
         for x in range(SUB):
             for y in range(QUAD):
-                index = index_ref[z, x, y]
+                coefficient = coefficients(x, y)
                 layer = None
                 for g in range(groups):
                     real = imag = None
                     for k in range(terms):
-                        coef_r = lane_take(table_ref[g, 0, k], index)
-                        coef_i = lane_take(table_ref[g, 1, k], index)
+                        coef_r, coef_i = coefficient(g, 0, k), coefficient(g, 1, k)
                         field_r, field_i = basis[g, k, 0, x, y], basis[g, k, 1, x, y]
                         if k == 0:
                             real = coef_r * field_r - coef_i * field_i
@@ -218,6 +238,22 @@
                     basis[g, 0, 1, x, y] = imag
                     layer = real if layer is None else layer + real
                 layers[z, y, pl.ds(x, SUB, stride=SUB)] = layer * scale
+
+    def depth_step(z, carry):
+        slot = jnp.bitwise_xor(z // levels, depth_pos)
+
+        @pl.when(slot < early)
+        def _():
+            at = slot * levels + z % levels
+            accumulate(z, lambda x, y: lambda g, c, k: coef_ref[at, g, c, k, x, y])
+
+        @pl.when(slot >= early)
+        def _():
+            def look_up(x, y):
+                index = index_ref[z, x, y]
+                return lambda g, c, k: lane_take(table_ref[g, c, k], index)
+
+            accumulate(z, look_up)
 
         @pl.when(z < depths - 1)
         def _():
@@ -309,17 +345,31 @@
         ]
     )
 
-    vels = [near]
+    vels = [own_vel, near]
     for value in far:
         value, table = lax.optimization_barrier((value, table))
         vels += [value, exchange(value, "depth", 1)]
 
     scale = 1.0 / math.sqrt(local_count * freq_count)
     half = jax.ShapeDtypeStruct((depths // 2, rows, columns), jnp.float32)
+    early = vels[:EARLY]
+    coefs = pl.pallas_call(
+        functools.partial(early_kernel, (groups, levels, terms)),
+        out_shape=jax.ShapeDtypeStruct((len(early) * levels, groups, 2, terms, SUB, QUAD, SUB, LANES), jnp.float32),
+        in_specs=[vmem] * (1 + len(early)),
+        out_specs=vmem,
+        scratch_shapes=[
+            pltpu.VMEM((QUAD, rows, LANES), jnp.int32),
+            pltpu.VMEM((len(early) * levels, SUB, QUAD, SUB, LANES), jnp.int32),
+        ],
+        compiler_params=params,
+        cost_estimate=pl.CostEstimate(flops=200_000_000, bytes_accessed=16_000_000, transcendentals=0),
+    )(table, *early)
+
     keep, send = pl.pallas_call(
         functools.partial(image_kernel, (groups, depth_count, levels, terms), scale),
         out_shape=(half, half),
-        in_specs=[vmem] * (2 + depth_count),
+        in_specs=[vmem] * (3 + depth_count - EARLY),
         out_specs=(vmem, vmem),
         scratch_shapes=[
             pltpu.VMEM((QUAD, rows, LANES), jnp.int32),
@@ -328,7 +378,7 @@
             pltpu.VMEM(basis_shape, jnp.float32),
         ],
         compiler_params=params,
-    )(table, basis, own_vel, *vels)
+    )(table, basis, coefs, *vels[EARLY:])
 
     image = keep + exchange(send, "depth", 1)
     distance = 2

time: 32.7 us -> 32.4 us (level)
  waiting for transfers between devices: 11 us -> 10.2 us
  Pallas kernels: 9.17 us -> 9.92 us
    pallas_call x0 -> x1, Pallas kernels: none -> 1.69 us  [per_device(): pl.pallas_call(functools.partial(early_kernel, (groups, levels, terms)),...]
    pallas_call x1, Pallas kernels: 6.58 us -> 5.64 us  [per_device(): pl.pallas_call(functools.partial(image_kernel, (groups, depth_count, leve...]
    ppermute x9, waiting for transfers between devices: 11 us -> 10.2 us  [exchange(): return lax.ppermute(value, axis, [(i, i ^ flip) for i in range(count)])]
    ppermute x9, starting transfers between devices: 11.6 us -> 11.3 us  [exchange(): return lax.ppermute(value, axis, [(i, i ^ flip) for i in range(count)])]
  transfers between devices with their start and end apart: 9 -> 9, of which waited for: 7 -> 6; matrix products, arithmetic and copies ran while one was open for 0% -> 0% of each run, Pallas kernels for 8% -> 13%
where the time goes in v6:
time: 32.4 us; the launch traced here: 32.2 us
  starting transfers between devices  11.3 us (35%)
  waiting for transfers between devices  10.2 us (31%)
  Pallas kernels  9.92 us (31%)
  other arithmetic  0.68 us (2%)
    ppermute x9, starting transfers between devices, exchange(): return lax.ppermute(value, axis, [(i, i ^ flip) for i in range(count)])  11.3 us
    ppermute x9, waiting for transfers between devices, exchange(): return lax.ppermute(value, axis, [(i, i ^ flip) for i in range(count)])  10.2 us
    pallas_call x1, Pallas kernels, per_device(): pl.pallas_call(functools.partial(image_kernel, (groups, depth_count, leve...  5.64 us
    pallas_call x1, Pallas kernels, per_device(): pl.pallas_call(functools.partial(first_kernel, (groups, count, local_coun...  2.59 us
    pallas_call x1, Pallas kernels, per_device(): pl.pallas_call(functools.partial(early_kernel, (groups, levels, terms)),...  1.69 us
  transfers between devices with their start and end apart: 9, of which 6 were waited for; matrix products, arithmetic and copies ran while one was open for 0% of the time, Pallas kernels for 13%

profile of v6, /device:TPU:0, one launch (start us, length us, event | category | flops | bytes accessed | tf_op | source)
XLA Modules:
  0.0 32.2 jit_solution(1777205041355749134)
XLA Ops:
  0.0 3.0 %collective-permute-start = (s32[1,64,256]{2,1,0:T(8,128)}, s32[1,64,256]{2,1,0:T(8,128)S(1)}, u32[]{:S(2)}, u32[]{:S(2)}) collective-permute-start(s32[1,64,256]{2,1,0:T(8,128)} %vel_hbm.1), channel_id=1, source_target_pairs={{0,16},{8,24},{16,0},{24,8},{1,17},{9,25},{17,1},{25,9},{2,18},{10... | collective-permute-start | bytes 196616 | tf_op jit(solution)/shard_map/ppermute | solution.py:21
  3.0 0.0 collective-permute-start.1
  3.0 2.6 %shard_map.46 = (f32[1,2,9,8,128]{4,3,2,1,0:T(8,128)S(1)}, f32[1,9,2,8,4,8,128]{6,5,4,3,2,1,0:T(8,128)S(1)}, s32[1,64,256]{2,1,0:T(8,128)S(1)}) custom-call(s32[8]{0:T(128)} %slot_hbm.1, f32[8,2,64,256]{3,2,1,0:T(8,128)} %surface_ref.1, f32[576,64]{1,0:T(8,128)} %bitcast.16, s32[1,64,256]{2,1,0:T(8,128)} %vel_hbm.1), custom_call_target="tpu_custom_call" | custom-call | flops 200000000 | bytes 16000000 | tf_op jit(solution)/shard_map/pallas_call | solution.py:322
  5.6 0.0 collective-permute-done.refs_0_
  5.6 0.6 %collective-permute-start.2 = (s32[1,64,256]{2,1,0:T(8,128)S(1)}, s32[1,64,256]{2,1,0:T(8,128)S(1)}, u32[]{:S(2)}, u32[]{:S(2)}) collective-permute-start(s32[1,64,256]{2,1,0:T(8,128)S(1)} %collective-permute-done.refs_0_), channel_id=1, source_target_pairs={{0,8},{8,0},{16,24},{24,16},{1,9},{9,1},{17,25},{25,17},{2,10},{10... | collective-permute-start | bytes 196616 | tf_op jit(solution)/shard_map/ppermute | solution.py:21
  6.2 0.0 collective-permute-done.1.refs_1_
  6.2 1.7 %shard_map.47.coef_ref = f32[2,1,2,9,8,4,8,128]{7,6,5,4,3,2,1,0:T(8,128)S(1)} custom-call(f32[1,2,9,8,128]{4,3,2,1,0:T(8,128)S(1)} %get-tuple-element.13.table_ref, s32[1,64,256]{2,1,0:T(8,128)S(1)} %get-tuple-element.15.refs_0_, s32[1,64,256]{2,1,0:T(8,128)S(1)} %collective-permute-done.1.refs_1_), custom_call_target="tpu_custom_call" | custom-call | flops 200000000 | bytes 16000000 | tf_op jit(solution)/shard_map/pallas_call | solution.py:356
  7.9 0.0 collective-permute-done.2.refs_1_
  7.9 5.6 %shard_map.48 = (f32[2,64,256]{2,1,0:T(8,128)S(1)}, f32[2,64,256]{2,1,0:T(8,128)S(1)}) custom-call(f32[1,2,9,8,128]{4,3,2,1,0:T(8,128)S(1)} %get-tuple-element.13.table_ref, f32[1,9,2,8,4,8,128]{6,5,4,3,2,1,0:T(8,128)S(1)} %get-tuple-element.14.first_ref, f32[2,1,2,9,8,4,8,128]{7,6,5,4,3,2,1,0:T(8,128)S(1)} %shard_map.47.coef_ref, ...), custom_call_target="tpu_custom_call" | custom-call | tf_op jit(solution)/shard_map/pallas_call | solution.py:369
  13.5 0.1 collective-permute-start.3
  13.6 1.3 %collective-permute-done.3 = f32[2,64,256]{2,1,0:T(8,128)S(1)} collective-permute-done((f32[2,64,256]{2,1,0:T(8,128)S(1)}, f32[2,64,256]{2,1,0:T(8,128)S(1)}, u32[]{:S(2)}, u32[]{:S(2)}) %collective-permute-start.3) | collective-permute-done | bytes 131104 | tf_op jit(solution)/shard_map/ppermute | solution.py:21
  15.0 1.5 %collective-permute-start.4 = (f32[1,1,64,256]{3,2,1,0:T(8,128)S(1)}, f32[1,1,64,256]{3,2,1,0:T(8,128)S(1)}, u32[]{:S(2)}, u32[]{:S(2)}) collective-permute-start(f32[1,1,64,256]{3,2,1,0:T(8,128)S(1)} %slice_bitcast_fusion), channel_id=1, source_target_pairs={{0,24},{8,16},{16,8},{24,0},{1,25},{9,17},{17,9},{25,1},{2,26},{10... | collective-permute-start | bytes 196616 | tf_op jit(solution)/shard_map/ppermute | solution.py:21
  16.4 2.6 %collective-permute-done.4 = f32[1,1,64,256]{3,2,1,0:T(8,128)S(1)} collective-permute-done((f32[1,1,64,256]{3,2,1,0:T(8,128)S(1)}, f32[1,1,64,256]{3,2,1,0:T(8,128)S(1)}, u32[]{:S(2)}, u32[]{:S(2)}) %collective-permute-start.4) | collective-permute-done | bytes 65568 | tf_op jit(solution)/shard_map/ppermute | solution.py:21
  19.1 2.5 %collective-permute-start.7 = (f32[1,64,256]{2,1,0:T(8,128)S(1)}, f32[1,64,256]{2,1,0:T(8,128)S(1)}, u32[]{:S(2)}, u32[]{:S(2)}) collective-permute-start(f32[1,64,256]{2,1,0:T(8,128)S(1)} %fusion.1), channel_id=1, source_target_pairs={{0,3},{1,2},{2,1},{3,0},{4,7},{5,6},{6,5},{7,4},{8,11},{9,10},{10,... | collective-permute-start | bytes 196616 | tf_op jit(solution)/shard_map/ppermute | solution.py:21
  21.6 0.5 %collective-permute-start.6 = (f32[1,64,256]{2,1,0:T(8,128)S(1)}, f32[1,64,256]{2,1,0:T(8,128)S(1)}, u32[]{:S(2)}, u32[]{:S(2)}) collective-permute-start(f32[1,64,256]{2,1,0:T(8,128)S(1)} %fusion.1), channel_id=1, source_target_pairs={{0,2},{1,3},{2,0},{3,1},{4,6},{5,7},{6,4},{7,5},{8,10},{9,11},{10,... | collective-permute-start | bytes 196616 | tf_op jit(solution)/shard_map/ppermute | solution.py:21
  22.1 0.6 %collective-permute-start.5 = (f32[1,64,256]{2,1,0:T(8,128)S(1)}, f32[1,64,256]{2,1,0:T(8,128)S(1)}, u32[]{:S(2)}, u32[]{:S(2)}) collective-permute-start(f32[1,64,256]{2,1,0:T(8,128)S(1)} %fusion.1), channel_id=1, source_target_pairs={{0,1},{1,0},{2,3},{3,2},{4,5},{5,4},{6,7},{7,6},{8,9},{9,8},{10,11... | collective-permute-start | bytes 196616 | tf_op jit(solution)/shard_map/ppermute | solution.py:21
  22.7 2.0 %collective-permute-done.7 = f32[1,64,256]{2,1,0:T(8,128)S(1)} collective-permute-done((f32[1,64,256]{2,1,0:T(8,128)S(1)}, f32[1,64,256]{2,1,0:T(8,128)S(1)}, u32[]{:S(2)}, u32[]{:S(2)}) %collective-permute-start.7) | collective-permute-done | bytes 65568 | tf_op jit(solution)/shard_map/ppermute | solution.py:21
  24.6 1.2 %collective-permute-done.6 = f32[1,64,256]{2,1,0:T(8,128)S(1)} collective-permute-done((f32[1,64,256]{2,1,0:T(8,128)S(1)}, f32[1,64,256]{2,1,0:T(8,128)S(1)}, u32[]{:S(2)}, u32[]{:S(2)}) %collective-permute-start.6) | collective-permute-done | bytes 65568 | tf_op jit(solution)/shard_map/ppermute | solution.py:21
  25.9 0.5 %collective-permute-done.5 = f32[1,64,256]{2,1,0:T(8,128)S(1)} collective-permute-done((f32[1,64,256]{2,1,0:T(8,128)S(1)}, f32[1,64,256]{2,1,0:T(8,128)S(1)}, u32[]{:S(2)}, u32[]{:S(2)}) %collective-permute-start.5) | collective-permute-done | bytes 65568 | tf_op jit(solution)/shard_map/ppermute | solution.py:21
  26.4 2.6 %collective-permute-start.8 = (f32[1,64,256]{2,1,0:T(8,128)S(1)}, f32[1,64,256]{2,1,0:T(8,128)S(1)}, u32[]{:S(2)}, u32[]{:S(2)}) collective-permute-start(f32[1,64,256]{2,1,0:T(8,128)S(1)} %add_add_fusion), channel_id=1, source_target_pairs={{0,4},{1,5},{2,6},{3,7},{4,0},{5,1},{6,2},{7,3},{8,12},{9,13},{10,... | collective-permute-start | bytes 196616 | tf_op jit(solution)/shard_map/ppermute | solution.py:21
  29.0 2.6 %collective-permute-done.8 = f32[1,64,256]{2,1,0:T(8,128)S(1)} collective-permute-done((f32[1,64,256]{2,1,0:T(8,128)S(1)}, f32[1,64,256]{2,1,0:T(8,128)S(1)}, u32[]{:S(2)}, u32[]{:S(2)}) %collective-permute-start.8) | collective-permute-done | bytes 65568 | tf_op jit(solution)/shard_map/ppermute | solution.py:21
  31.6 0.6 %add.23 = f32[1,64,256]{2,1,0:T(8,128)} add(f32[1,64,256]{2,1,0:T(8,128)S(1)} %add_add_fusion, f32[1,64,256]{2,1,0:T(8,128)S(1)} %collective-permute-done.8) | non-fusion elementwise | flops 16384 | bytes 196608 | tf_op jit(solution)/shard_map/add | solution.py:396
  (4 shorter events, 0.1 us)
Async XLA Ops:
  0.0 5.6 %collective-permute-start = (s32[1,64,256]{2,1,0:T(8,128)}, s32[1,64,256]{2,1,0:T(8,128)S(1)}, u32[]{:S(2)}, u32[]{:S(2)}) collective-permute-start(s32[1,64,256]{2,1,0:T(8,128)} %vel_hbm.1), channel_id=1, source_target_pairs={{0,16},{8,24},{16,0},{24,8},{1,17},{9,25},{17,1},{25,9},{2,18},{10... | collective-permute-start | bytes 196616 | tf_op jit(solution)/shard_map/ppermute | solution.py:21
  3.0 3.2 %collective-permute-start.1 = (s32[1,64,256]{2,1,0:T(8,128)}, s32[1,64,256]{2,1,0:T(8,128)S(1)}, u32[]{:S(2)}, u32[]{:S(2)}) collective-permute-start(s32[1,64,256]{2,1,0:T(8,128)} %vel_hbm.1), channel_id=1, source_target_pairs={{0,8},{8,0},{16,24},{24,16},{1,9},{9,1},{17,25},{25,17},{2,10},{10... | collective-permute-start | bytes 196616 | tf_op jit(solution)/shard_map/ppermute | solution.py:21
  5.6 2.3 %collective-permute-start.2 = (s32[1,64,256]{2,1,0:T(8,128)S(1)}, s32[1,64,256]{2,1,0:T(8,128)S(1)}, u32[]{:S(2)}, u32[]{:S(2)}) collective-permute-start(s32[1,64,256]{2,1,0:T(8,128)S(1)} %collective-permute-done.refs_0_), channel_id=1, source_target_pairs={{0,8},{8,0},{16,24},{24,16},{1,9},{9,1},{17,25},{25,17},{2,10},{10... | collective-permute-start | bytes 196616 | tf_op jit(solution)/shard_map/ppermute | solution.py:21
  13.5 1.4 %collective-permute-start.3 = (f32[2,64,256]{2,1,0:T(8,128)S(1)}, f32[2,64,256]{2,1,0:T(8,128)S(1)}, u32[]{:S(2)}, u32[]{:S(2)}) collective-permute-start(f32[2,64,256]{2,1,0:T(8,128)S(1)} %get-tuple-element.18), channel_id=1, source_target_pairs={{0,8},{8,0},{16,24},{24,16},{1,9},{9,1},{17,25},{25,17},{2,10},{10... | collective-permute-start | bytes 393224 | tf_op jit(solution)/shard_map/ppermute | solution.py:21
  15.0 4.1 %collective-permute-start.4 = (f32[1,1,64,256]{3,2,1,0:T(8,128)S(1)}, f32[1,1,64,256]{3,2,1,0:T(8,128)S(1)}, u32[]{:S(2)}, u32[]{:S(2)}) collective-permute-start(f32[1,1,64,256]{3,2,1,0:T(8,128)S(1)} %slice_bitcast_fusion), channel_id=1, source_target_pairs={{0,24},{8,16},{16,8},{24,0},{1,25},{9,17},{17,9},{25,1},{2,26},{10... | collective-permute-start | bytes 196616 | tf_op jit(solution)/shard_map/ppermute | solution.py:21
  19.1 5.5 %collective-permute-start.7 = (f32[1,64,256]{2,1,0:T(8,128)S(1)}, f32[1,64,256]{2,1,0:T(8,128)S(1)}, u32[]{:S(2)}, u32[]{:S(2)}) collective-permute-start(f32[1,64,256]{2,1,0:T(8,128)S(1)} %fusion.1), channel_id=1, source_target_pairs={{0,3},{1,2},{2,1},{3,0},{4,7},{5,6},{6,5},{7,4},{8,11},{9,10},{10,... | collective-permute-start | bytes 196616 | tf_op jit(solution)/shard_map/ppermute | solution.py:21
  21.6 4.3 %collective-permute-start.6 = (f32[1,64,256]{2,1,0:T(8,128)S(1)}, f32[1,64,256]{2,1,0:T(8,128)S(1)}, u32[]{:S(2)}, u32[]{:S(2)}) collective-permute-start(f32[1,64,256]{2,1,0:T(8,128)S(1)} %fusion.1), channel_id=1, source_target_pairs={{0,2},{1,3},{2,0},{3,1},{4,6},{5,7},{6,4},{7,5},{8,10},{9,11},{10,... | collective-permute-start | bytes 196616 | tf_op jit(solution)/shard_map/ppermute | solution.py:21
  22.1 4.3 %collective-permute-start.5 = (f32[1,64,256]{2,1,0:T(8,128)S(1)}, f32[1,64,256]{2,1,0:T(8,128)S(1)}, u32[]{:S(2)}, u32[]{:S(2)}) collective-permute-start(f32[1,64,256]{2,1,0:T(8,128)S(1)} %fusion.1), channel_id=1, source_target_pairs={{0,1},{1,0},{2,3},{3,2},{4,5},{5,4},{6,7},{7,6},{8,9},{9,8},{10,11... | collective-permute-start | bytes 196616 | tf_op jit(solution)/shard_map/ppermute | solution.py:21
  26.4 5.2 %collective-permute-start.8 = (f32[1,64,256]{2,1,0:T(8,128)S(1)}, f32[1,64,256]{2,1,0:T(8,128)S(1)}, u32[]{:S(2)}, u32[]{:S(2)}) collective-permute-start(f32[1,64,256]{2,1,0:T(8,128)S(1)} %add_add_fusion), channel_id=1, source_target_pairs={{0,4},{1,5},{2,6},{3,7},{4,0},{5,1},{6,2},{7,3},{8,12},{9,13},{10,... | collective-permute-start | bytes 196616 | tf_op jit(solution)/shard_map/ppermute | solution.py:21

commit v7 on v6

--- a/solution.py
+++ b/solution.py
@@ -210,15 +210,7 @@
     targets = [jnp.bitwise_xor(depth_pos, slot) * levels for slot in range(early, depth_count)]
     place_velocities(vel_refs, targets, numbers, index_ref)
 
-    def first_terms(k, carry):
-        for g in range(groups):
-            for c in range(2):
-                basis[g, k, c] = first_ref[g, k, c]
-        return carry
-
-    lax.fori_loop(0, terms, first_terms, 0)
-
-    def accumulate(z, coefficients):
+    def accumulate(z, coefficients, source):
         for x in range(SUB):
             for y in range(QUAD):
                 coefficient = coefficients(x, y)
@@ -227,7 +219,7 @@
                     real = imag = None
                     for k in range(terms):
                         coef_r, coef_i = coefficient(g, 0, k), coefficient(g, 1, k)
-                        field_r, field_i = basis[g, k, 0, x, y], basis[g, k, 1, x, y]
+                        field_r, field_i = source[g, k, 0, x, y], source[g, k, 1, x, y]
                         if k == 0:
                             real = coef_r * field_r - coef_i * field_i
                             imag = coef_r * field_i + coef_i * field_r
@@ -239,13 +231,13 @@
                     layer = real if layer is None else layer + real
                 layers[z, y, pl.ds(x, SUB, stride=SUB)] = layer * scale
 
-    def depth_step(z, carry):
+    def image_of(z, source):
         slot = jnp.bitwise_xor(z // levels, depth_pos)
 
         @pl.when(slot < early)
         def _():
             at = slot * levels + z % levels
-            accumulate(z, lambda x, y: lambda g, c, k: coef_ref[at, g, c, k, x, y])
+            accumulate(z, lambda x, y: lambda g, c, k: coef_ref[at, g, c, k, x, y], source)
 
         @pl.when(slot >= early)
         def _():
@@ -253,22 +245,22 @@
                 index = index_ref[z, x, y]
                 return lambda g, c, k: lane_take(table_ref[g, c, k], index)
 
-            accumulate(z, look_up)
-
-        @pl.when(z < depths - 1)
-        def _():
-            for g in range(groups):
-                for c in range(2):
-                    start = [[basis[g, 0, c, x, y] for y in range(QUAD)] for x in range(SUB)]
-
-                    def put(k, x, y, value):
-                        basis[g, k, c, x, y] = value
-
-                    chebyshev(start, terms, masks, put)
-
+            accumulate(z, look_up, source)
+
+    def depth_step(z, carry):
+        for g in range(groups):
+            for c in range(2):
+                start = [[basis[g, 0, c, x, y] for y in range(QUAD)] for x in range(SUB)]
+
+                def put(k, x, y, value):
+                    basis[g, k, c, x, y] = value
+
+                chebyshev(start, terms, masks, put)
+        image_of(z, basis)
         return carry
 
-    lax.fori_loop(0, depths, depth_step, 0)
+    image_of(0, first_ref)
+    lax.fori_loop(1, depths, depth_step, 0)
 
     turned = lax.broadcasted_iota(jnp.int32, (LANES, columns), 0) % ENTRY_SPAN * QUAD
     wanted = lax.broadcasted_iota(jnp.int32, (LANES, columns), 1)

time: 32.4 us -> 32.2 us (level)
  no operation moved by 1% of the time
where the time goes in v7:
time: 32.2 us; the launch traced here: 32 us
  starting transfers between devices  11.3 us (35%)
  waiting for transfers between devices  10.2 us (32%)
  Pallas kernels  9.71 us (30%)
  other arithmetic  0.68 us (2%)
    ppermute x9, starting transfers between devices, exchange(): return lax.ppermute(value, axis, [(i, i ^ flip) for i in range(count)])  11.3 us
    ppermute x9, waiting for transfers between devices, exchange(): return lax.ppermute(value, axis, [(i, i ^ flip) for i in range(count)])  10.2 us
    pallas_call x1, Pallas kernels, per_device(): pl.pallas_call(functools.partial(image_kernel, (groups, depth_count, leve...  5.43 us
    pallas_call x1, Pallas kernels, per_device(): pl.pallas_call(functools.partial(first_kernel, (groups, count, local_coun...  2.59 us
    pallas_call x1, Pallas kernels, per_device(): pl.pallas_call(functools.partial(early_kernel, (groups, levels, terms)),...  1.69 us
  transfers between devices with their start and end apart: 9, of which 6 were waited for; matrix products, arithmetic and copies ran while one was open for 0% of the time, Pallas kernels for 13%

profile of v7, /device:TPU:0, one launch (start us, length us, event | category | flops | bytes accessed | tf_op | source)
XLA Modules:
  0.0 32.0 jit_solution(8802406225405565585)
XLA Ops:
  0.0 3.0 %collective-permute-start = (s32[1,64,256]{2,1,0:T(8,128)}, s32[1,64,256]{2,1,0:T(8,128)S(1)}, u32[]{:S(2)}, u32[]{:S(2)}) collective-permute-start(s32[1,64,256]{2,1,0:T(8,128)} %vel_hbm.1), channel_id=1, source_target_pairs={{0,16},{8,24},{16,0},{24,8},{1,17},{9,25},{17,1},{25,9},{2,18},{10... | collective-permute-start | bytes 196616 | tf_op jit(solution)/shard_map/ppermute | solution.py:21
  3.0 0.0 collective-permute-start.1
  3.0 2.6 %shard_map.46 = (f32[1,2,9,8,128]{4,3,2,1,0:T(8,128)S(1)}, f32[1,9,2,8,4,8,128]{6,5,4,3,2,1,0:T(8,128)S(1)}, s32[1,64,256]{2,1,0:T(8,128)S(1)}) custom-call(s32[8]{0:T(128)} %slot_hbm.1, f32[8,2,64,256]{3,2,1,0:T(8,128)} %surface_ref.1, f32[576,64]{1,0:T(8,128)} %bitcast.16, s32[1,64,256]{2,1,0:T(8,128)} %vel_hbm.1), custom_call_target="tpu_custom_call" | custom-call | flops 200000000 | bytes 16000000 | tf_op jit(solution)/shard_map/pallas_call | solution.py:314
  5.6 0.0 collective-permute-done.refs_0_
  5.6 0.6 %collective-permute-start.2 = (s32[1,64,256]{2,1,0:T(8,128)S(1)}, s32[1,64,256]{2,1,0:T(8,128)S(1)}, u32[]{:S(2)}, u32[]{:S(2)}) collective-permute-start(s32[1,64,256]{2,1,0:T(8,128)S(1)} %collective-permute-done.refs_0_), channel_id=1, source_target_pairs={{0,8},{8,0},{16,24},{24,16},{1,9},{9,1},{17,25},{25,17},{2,10},{10... | collective-permute-start | bytes 196616 | tf_op jit(solution)/shard_map/ppermute | solution.py:21
  6.2 0.0 collective-permute-done.1.refs_1_
  6.2 1.7 %shard_map.47.coef_ref = f32[2,1,2,9,8,4,8,128]{7,6,5,4,3,2,1,0:T(8,128)S(1)} custom-call(f32[1,2,9,8,128]{4,3,2,1,0:T(8,128)S(1)} %get-tuple-element.13.table_ref, s32[1,64,256]{2,1,0:T(8,128)S(1)} %get-tuple-element.15.refs_0_, s32[1,64,256]{2,1,0:T(8,128)S(1)} %collective-permute-done.1.refs_1_), custom_call_target="tpu_custom_call" | custom-call | flops 200000000 | bytes 16000000 | tf_op jit(solution)/shard_map/pallas_call | solution.py:348
  7.9 0.0 collective-permute-done.2.refs_1_
  7.9 5.4 %shard_map.48 = (f32[2,64,256]{2,1,0:T(8,128)S(1)}, f32[2,64,256]{2,1,0:T(8,128)S(1)}) custom-call(f32[1,2,9,8,128]{4,3,2,1,0:T(8,128)S(1)} %get-tuple-element.13.table_ref, f32[1,9,2,8,4,8,128]{6,5,4,3,2,1,0:T(8,128)S(1)} %get-tuple-element.14.first_ref, f32[2,1,2,9,8,4,8,128]{7,6,5,4,3,2,1,0:T(8,128)S(1)} %shard_map.47.coef_ref, ...), custom_call_target="tpu_custom_call" | custom-call | tf_op jit(solution)/shard_map/pallas_call | solution.py:361
  13.3 0.1 collective-permute-start.3
  13.4 1.3 %collective-permute-done.3 = f32[2,64,256]{2,1,0:T(8,128)S(1)} collective-permute-done((f32[2,64,256]{2,1,0:T(8,128)S(1)}, f32[2,64,256]{2,1,0:T(8,128)S(1)}, u32[]{:S(2)}, u32[]{:S(2)}) %collective-permute-start.3) | collective-permute-done | bytes 131104 | tf_op jit(solution)/shard_map/ppermute | solution.py:21
  14.7 1.5 %collective-permute-start.4 = (f32[1,1,64,256]{3,2,1,0:T(8,128)S(1)}, f32[1,1,64,256]{3,2,1,0:T(8,128)S(1)}, u32[]{:S(2)}, u32[]{:S(2)}) collective-permute-start(f32[1,1,64,256]{3,2,1,0:T(8,128)S(1)} %slice_bitcast_fusion), channel_id=1, source_target_pairs={{0,24},{8,16},{16,8},{24,0},{1,25},{9,17},{17,9},{25,1},{2,26},{10... | collective-permute-start | bytes 196616 | tf_op jit(solution)/shard_map/ppermute | solution.py:21
  16.2 2.7 %collective-permute-done.4 = f32[1,1,64,256]{3,2,1,0:T(8,128)S(1)} collective-permute-done((f32[1,1,64,256]{3,2,1,0:T(8,128)S(1)}, f32[1,1,64,256]{3,2,1,0:T(8,128)S(1)}, u32[]{:S(2)}, u32[]{:S(2)}) %collective-permute-start.4) | collective-permute-done | bytes 65568 | tf_op jit(solution)/shard_map/ppermute | solution.py:21
  18.9 2.5 %collective-permute-start.7 = (f32[1,64,256]{2,1,0:T(8,128)S(1)}, f32[1,64,256]{2,1,0:T(8,128)S(1)}, u32[]{:S(2)}, u32[]{:S(2)}) collective-permute-start(f32[1,64,256]{2,1,0:T(8,128)S(1)} %fusion.1), channel_id=1, source_target_pairs={{0,3},{1,2},{2,1},{3,0},{4,7},{5,6},{6,5},{7,4},{8,11},{9,10},{10,... | collective-permute-start | bytes 196616 | tf_op jit(solution)/shard_map/ppermute | solution.py:21
  21.4 0.4 %collective-permute-start.6 = (f32[1,64,256]{2,1,0:T(8,128)S(1)}, f32[1,64,256]{2,1,0:T(8,128)S(1)}, u32[]{:S(2)}, u32[]{:S(2)}) collective-permute-start(f32[1,64,256]{2,1,0:T(8,128)S(1)} %fusion.1), channel_id=1, source_target_pairs={{0,2},{1,3},{2,0},{3,1},{4,6},{5,7},{6,4},{7,5},{8,10},{9,11},{10,... | collective-permute-start | bytes 196616 | tf_op jit(solution)/shard_map/ppermute | solution.py:21
  21.8 0.6 %collective-permute-start.5 = (f32[1,64,256]{2,1,0:T(8,128)S(1)}, f32[1,64,256]{2,1,0:T(8,128)S(1)}, u32[]{:S(2)}, u32[]{:S(2)}) collective-permute-start(f32[1,64,256]{2,1,0:T(8,128)S(1)} %fusion.1), channel_id=1, source_target_pairs={{0,1},{1,0},{2,3},{3,2},{4,5},{5,4},{6,7},{7,6},{8,9},{9,8},{10,11... | collective-permute-start | bytes 196616 | tf_op jit(solution)/shard_map/ppermute | solution.py:21
  22.4 2.0 %collective-permute-done.7 = f32[1,64,256]{2,1,0:T(8,128)S(1)} collective-permute-done((f32[1,64,256]{2,1,0:T(8,128)S(1)}, f32[1,64,256]{2,1,0:T(8,128)S(1)}, u32[]{:S(2)}, u32[]{:S(2)}) %collective-permute-start.7) | collective-permute-done | bytes 65568 | tf_op jit(solution)/shard_map/ppermute | solution.py:21
  24.4 1.2 %collective-permute-done.6 = f32[1,64,256]{2,1,0:T(8,128)S(1)} collective-permute-done((f32[1,64,256]{2,1,0:T(8,128)S(1)}, f32[1,64,256]{2,1,0:T(8,128)S(1)}, u32[]{:S(2)}, u32[]{:S(2)}) %collective-permute-start.6) | collective-permute-done | bytes 65568 | tf_op jit(solution)/shard_map/ppermute | solution.py:21
  25.7 0.4 %collective-permute-done.5 = f32[1,64,256]{2,1,0:T(8,128)S(1)} collective-permute-done((f32[1,64,256]{2,1,0:T(8,128)S(1)}, f32[1,64,256]{2,1,0:T(8,128)S(1)}, u32[]{:S(2)}, u32[]{:S(2)}) %collective-permute-start.5) | collective-permute-done | bytes 65568 | tf_op jit(solution)/shard_map/ppermute | solution.py:21
  26.1 2.7 %collective-permute-start.8 = (f32[1,64,256]{2,1,0:T(8,128)S(1)}, f32[1,64,256]{2,1,0:T(8,128)S(1)}, u32[]{:S(2)}, u32[]{:S(2)}) collective-permute-start(f32[1,64,256]{2,1,0:T(8,128)S(1)} %add_add_fusion), channel_id=1, source_target_pairs={{0,4},{1,5},{2,6},{3,7},{4,0},{5,1},{6,2},{7,3},{8,12},{9,13},{10,... | collective-permute-start | bytes 196616 | tf_op jit(solution)/shard_map/ppermute | solution.py:21
  28.8 2.6 %collective-permute-done.8 = f32[1,64,256]{2,1,0:T(8,128)S(1)} collective-permute-done((f32[1,64,256]{2,1,0:T(8,128)S(1)}, f32[1,64,256]{2,1,0:T(8,128)S(1)}, u32[]{:S(2)}, u32[]{:S(2)}) %collective-permute-start.8) | collective-permute-done | bytes 65568 | tf_op jit(solution)/shard_map/ppermute | solution.py:21
  31.4 0.6 %add.23 = f32[1,64,256]{2,1,0:T(8,128)} add(f32[1,64,256]{2,1,0:T(8,128)S(1)} %add_add_fusion, f32[1,64,256]{2,1,0:T(8,128)S(1)} %collective-permute-done.8) | non-fusion elementwise | flops 16384 | bytes 196608 | tf_op jit(solution)/shard_map/add | solution.py:388
  (4 shorter events, 0.1 us)
Async XLA Ops:
  0.0 5.6 %collective-permute-start = (s32[1,64,256]{2,1,0:T(8,128)}, s32[1,64,256]{2,1,0:T(8,128)S(1)}, u32[]{:S(2)}, u32[]{:S(2)}) collective-permute-start(s32[1,64,256]{2,1,0:T(8,128)} %vel_hbm.1), channel_id=1, source_target_pairs={{0,16},{8,24},{16,0},{24,8},{1,17},{9,25},{17,1},{25,9},{2,18},{10... | collective-permute-start | bytes 196616 | tf_op jit(solution)/shard_map/ppermute | solution.py:21
  3.0 3.2 %collective-permute-start.1 = (s32[1,64,256]{2,1,0:T(8,128)}, s32[1,64,256]{2,1,0:T(8,128)S(1)}, u32[]{:S(2)}, u32[]{:S(2)}) collective-permute-start(s32[1,64,256]{2,1,0:T(8,128)} %vel_hbm.1), channel_id=1, source_target_pairs={{0,8},{8,0},{16,24},{24,16},{1,9},{9,1},{17,25},{25,17},{2,10},{10... | collective-permute-start | bytes 196616 | tf_op jit(solution)/shard_map/ppermute | solution.py:21
  5.6 2.3 %collective-permute-start.2 = (s32[1,64,256]{2,1,0:T(8,128)S(1)}, s32[1,64,256]{2,1,0:T(8,128)S(1)}, u32[]{:S(2)}, u32[]{:S(2)}) collective-permute-start(s32[1,64,256]{2,1,0:T(8,128)S(1)} %collective-permute-done.refs_0_), channel_id=1, source_target_pairs={{0,8},{8,0},{16,24},{24,16},{1,9},{9,1},{17,25},{25,17},{2,10},{10... | collective-permute-start | bytes 196616 | tf_op jit(solution)/shard_map/ppermute | solution.py:21
  13.3 1.4 %collective-permute-start.3 = (f32[2,64,256]{2,1,0:T(8,128)S(1)}, f32[2,64,256]{2,1,0:T(8,128)S(1)}, u32[]{:S(2)}, u32[]{:S(2)}) collective-permute-start(f32[2,64,256]{2,1,0:T(8,128)S(1)} %get-tuple-element.18), channel_id=1, source_target_pairs={{0,8},{8,0},{16,24},{24,16},{1,9},{9,1},{17,25},{25,17},{2,10},{10... | collective-permute-start | bytes 393224 | tf_op jit(solution)/shard_map/ppermute | solution.py:21
  14.7 4.1 %collective-permute-start.4 = (f32[1,1,64,256]{3,2,1,0:T(8,128)S(1)}, f32[1,1,64,256]{3,2,1,0:T(8,128)S(1)}, u32[]{:S(2)}, u32[]{:S(2)}) collective-permute-start(f32[1,1,64,256]{3,2,1,0:T(8,128)S(1)} %slice_bitcast_fusion), channel_id=1, source_target_pairs={{0,24},{8,16},{16,8},{24,0},{1,25},{9,17},{17,9},{25,1},{2,26},{10... | collective-permute-start | bytes 196616 | tf_op jit(solution)/shard_map/ppermute | solution.py:21
  18.9 5.5 %collective-permute-start.7 = (f32[1,64,256]{2,1,0:T(8,128)S(1)}, f32[1,64,256]{2,1,0:T(8,128)S(1)}, u32[]{:S(2)}, u32[]{:S(2)}) collective-permute-start(f32[1,64,256]{2,1,0:T(8,128)S(1)} %fusion.1), channel_id=1, source_target_pairs={{0,3},{1,2},{2,1},{3,0},{4,7},{5,6},{6,5},{7,4},{8,11},{9,10},{10,... | collective-permute-start | bytes 196616 | tf_op jit(solution)/shard_map/ppermute | solution.py:21
  21.4 4.3 %collective-permute-start.6 = (f32[1,64,256]{2,1,0:T(8,128)S(1)}, f32[1,64,256]{2,1,0:T(8,128)S(1)}, u32[]{:S(2)}, u32[]{:S(2)}) collective-permute-start(f32[1,64,256]{2,1,0:T(8,128)S(1)} %fusion.1), channel_id=1, source_target_pairs={{0,2},{1,3},{2,0},{3,1},{4,6},{5,7},{6,4},{7,5},{8,10},{9,11},{10,... | collective-permute-start | bytes 196616 | tf_op jit(solution)/shard_map/ppermute | solution.py:21
  21.8 4.3 %collective-permute-start.5 = (f32[1,64,256]{2,1,0:T(8,128)S(1)}, f32[1,64,256]{2,1,0:T(8,128)S(1)}, u32[]{:S(2)}, u32[]{:S(2)}) collective-permute-start(f32[1,64,256]{2,1,0:T(8,128)S(1)} %fusion.1), channel_id=1, source_target_pairs={{0,1},{1,0},{2,3},{3,2},{4,5},{5,4},{6,7},{7,6},{8,9},{9,8},{10,11... | collective-permute-start | bytes 196616 | tf_op jit(solution)/shard_map/ppermute | solution.py:21
  26.1 5.2 %collective-permute-start.8 = (f32[1,64,256]{2,1,0:T(8,128)S(1)}, f32[1,64,256]{2,1,0:T(8,128)S(1)}, u32[]{:S(2)}, u32[]{:S(2)}) collective-permute-start(f32[1,64,256]{2,1,0:T(8,128)S(1)} %add_add_fusion), channel_id=1, source_target_pairs={{0,4},{1,5},{2,6},{3,7},{4,0},{5,1},{6,2},{7,3},{8,12},{9,13},{10,... | collective-permute-start | bytes 196616 | tf_op jit(solution)/shard_map/ppermute | solution.py:21

commit v8 on v7

--- a/solution.py
+++ b/solution.py
@@ -13,6 +13,7 @@
 PAIR = 2
 QUAD = 4
 ENTRY_SPAN = LANES // PAIR
+READY = 6
 EARLY = 2
 
 
@@ -185,10 +186,10 @@
 def early_kernel(sizes, table_ref, *refs):
     groups, levels, terms = sizes
     vel_refs = refs[:-3]
-    coef_ref, numbers, index_ref = refs[-3:]
+    coef_ref, index_ref, numbers = refs[-3:]
     place_velocities(vel_refs, [slot * levels for slot in range(len(vel_refs))], numbers, index_ref)
     for z in range(len(vel_refs) * levels):
-        for x in range(SUB):
+        for x in range(READY):
             for y in range(QUAD):
                 index = index_ref[z, x, y]
                 for g in range(groups):
@@ -197,7 +198,7 @@
                             coef_ref[z, g, c, k, x, y] = lane_take(table_ref[g, c, k], index)
 
 
-def image_kernel(sizes, scale, table_ref, first_ref, coef_ref, *refs):
+def image_kernel(sizes, scale, table_ref, first_ref, coef_ref, early_index_ref, *refs):
     groups, depth_count, levels, terms = sizes
     early = coef_ref.shape[0] // levels
     vel_refs = refs[: depth_count - early]
@@ -237,7 +238,14 @@
         @pl.when(slot < early)
         def _():
             at = slot * levels + z % levels
-            accumulate(z, lambda x, y: lambda g, c, k: coef_ref[at, g, c, k, x, y], source)
+
+            def read(x, y):
+                if x < READY:
+                    return lambda g, c, k: coef_ref[at, g, c, k, x, y]
+                index = early_index_ref[at, x, y]
+                return lambda g, c, k: lane_take(table_ref[g, c, k], index)
+
+            accumulate(z, read, source)
 
         @pl.when(slot >= early)
         def _():
@@ -345,15 +353,16 @@
     scale = 1.0 / math.sqrt(local_count * freq_count)
     half = jax.ShapeDtypeStruct((depths // 2, rows, columns), jnp.float32)
     early = vels[:EARLY]
-    coefs = pl.pallas_call(
+    early_depths = len(early) * levels
+    coefs, early_index = pl.pallas_call(
         functools.partial(early_kernel, (groups, levels, terms)),
-        out_shape=jax.ShapeDtypeStruct((len(early) * levels, groups, 2, terms, SUB, QUAD, SUB, LANES), jnp.float32),
+        out_shape=(
+            jax.ShapeDtypeStruct((early_depths, groups, 2, terms, READY, QUAD, SUB, LANES), jnp.float32),
+            jax.ShapeDtypeStruct((early_depths, SUB, QUAD, SUB, LANES), jnp.int32),
+        ),
         in_specs=[vmem] * (1 + len(early)),
-        out_specs=vmem,
-        scratch_shapes=[
-            pltpu.VMEM((QUAD, rows, LANES), jnp.int32),
-            pltpu.VMEM((len(early) * levels, SUB, QUAD, SUB, LANES), jnp.int32),
-        ],
+        out_specs=(vmem, vmem),
+        scratch_shapes=[pltpu.VMEM((QUAD, rows, LANES), jnp.int32)],
         compiler_params=params,
         cost_estimate=pl.CostEstimate(flops=200_000_000, bytes_accessed=16_000_000, transcendentals=0),
     )(table, *early)
@@ -361,7 +370,7 @@
     keep, send = pl.pallas_call(
         functools.partial(image_kernel, (groups, depth_count, levels, terms), scale),
         out_shape=(half, half),
-        in_specs=[vmem] * (3 + depth_count - EARLY),
+        in_specs=[vmem] * (4 + depth_count - EARLY),
         out_specs=(vmem, vmem),
         scratch_shapes=[
             pltpu.VMEM((QUAD, rows, LANES), jnp.int32),
@@ -370,7 +379,7 @@
             pltpu.VMEM(basis_shape, jnp.float32),
         ],
         compiler_params=params,
-    )(table, basis, coefs, *vels[EARLY:])
+    )(table, basis, coefs, early_index, *vels[EARLY:])
 
     image = keep + exchange(send, "depth", 1)
     distance = 2

time: 32.2 us -> 32 us (level)
    pallas_call x1, Pallas kernels: 1.69 us -> 1.34 us  [per_device(): pl.pallas_call(functools.partial(early_kernel, (groups, levels, terms)),...]
  transfers between devices with their start and end apart: 9 -> 9, of which waited for: 6 -> 6; matrix products, arithmetic and copies ran while one was open for 0% -> 0% of each run, Pallas kernels for 13% -> 12%
where the time goes in v8:
time: 32 us; the launch traced here: 31.9 us
  starting transfers between devices  11.3 us (35%)
  waiting for transfers between devices  10.3 us (32%)
  Pallas kernels  9.58 us (30%)
  other arithmetic  0.68 us (2%)
    ppermute x9, starting transfers between devices, exchange(): return lax.ppermute(value, axis, [(i, i ^ flip) for i in range(count)])  11.3 us
    ppermute x9, waiting for transfers between devices, exchange(): return lax.ppermute(value, axis, [(i, i ^ flip) for i in range(count)])  10.3 us
    pallas_call x1, Pallas kernels, per_device(): pl.pallas_call(functools.partial(image_kernel, (groups, depth_count, leve...  5.66 us
    pallas_call x1, Pallas kernels, per_device(): pl.pallas_call(functools.partial(first_kernel, (groups, count, local_coun...  2.59 us
    pallas_call x1, Pallas kernels, per_device(): pl.pallas_call(functools.partial(early_kernel, (groups, levels, terms)),...  1.34 us
  transfers between devices with their start and end apart: 9, of which 6 were waited for; matrix products, arithmetic and copies ran while one was open for 0% of the time, Pallas kernels for 12%

profile of v8, /device:TPU:0, one launch (start us, length us, event | category | flops | bytes accessed | tf_op | source)
XLA Modules:
  0.0 31.9 jit_solution(15726249260673463367)
XLA Ops:
  0.0 3.0 %collective-permute-start = (s32[1,64,256]{2,1,0:T(8,128)}, s32[1,64,256]{2,1,0:T(8,128)S(1)}, u32[]{:S(2)}, u32[]{:S(2)}) collective-permute-start(s32[1,64,256]{2,1,0:T(8,128)} %vel_hbm.1), channel_id=1, source_target_pairs={{0,16},{8,24},{16,0},{24,8},{1,17},{9,25},{17,1},{25,9},{2,18},{10... | collective-permute-start | bytes 196616 | tf_op jit(solution)/shard_map/ppermute | solution.py:22
  3.0 0.0 collective-permute-start.1
  3.0 2.6 %shard_map.46 = (f32[1,2,9,8,128]{4,3,2,1,0:T(8,128)S(1)}, f32[1,9,2,8,4,8,128]{6,5,4,3,2,1,0:T(8,128)S(1)}, s32[1,64,256]{2,1,0:T(8,128)S(1)}) custom-call(s32[8]{0:T(128)} %slot_hbm.1, f32[8,2,64,256]{3,2,1,0:T(8,128)} %surface_ref.1, f32[576,64]{1,0:T(8,128)} %bitcast.16, s32[1,64,256]{2,1,0:T(8,128)} %vel_hbm.1), custom_call_target="tpu_custom_call" | custom-call | flops 200000000 | bytes 16000000 | tf_op jit(solution)/shard_map/pallas_call | solution.py:322
  5.6 0.0 collective-permute-done.refs_0_
  5.6 0.6 %collective-permute-start.2 = (s32[1,64,256]{2,1,0:T(8,128)S(1)}, s32[1,64,256]{2,1,0:T(8,128)S(1)}, u32[]{:S(2)}, u32[]{:S(2)}) collective-permute-start(s32[1,64,256]{2,1,0:T(8,128)S(1)} %collective-permute-done.refs_0_), channel_id=1, source_target_pairs={{0,8},{8,0},{16,24},{24,16},{1,9},{9,1},{17,25},{25,17},{2,10},{10... | collective-permute-start | bytes 196616 | tf_op jit(solution)/shard_map/ppermute | solution.py:22
  6.2 0.0 collective-permute-done.1.refs_1_
  6.2 1.3 %shard_map.47 = (f32[2,1,2,9,6,4,8,128]{7,6,5,4,3,2,1,0:T(8,128)S(1)}, s32[2,8,4,8,128]{4,3,2,1,0:T(8,128)S(1)}) custom-call(f32[1,2,9,8,128]{4,3,2,1,0:T(8,128)S(1)} %get-tuple-element.15.table_ref, s32[1,64,256]{2,1,0:T(8,128)S(1)} %get-tuple-element.17.refs_0_, s32[1,64,256]{2,1,0:T(8,128)S(1)} %collective-permute-done.1.refs_1_), custom_call_target="tpu_custom_call" | custom-call | flops 200000000 | bytes 16000000 | tf_op jit(solution)/shard_map/pallas_call | solution.py:357
  7.5 0.0 collective-permute-done.2.refs_1_
  7.5 5.7 %shard_map.48 = (f32[2,64,256]{2,1,0:T(8,128)S(1)}, f32[2,64,256]{2,1,0:T(8,128)S(1)}) custom-call(f32[1,2,9,8,128]{4,3,2,1,0:T(8,128)S(1)} %get-tuple-element.15.table_ref, f32[1,9,2,8,4,8,128]{6,5,4,3,2,1,0:T(8,128)S(1)} %get-tuple-element.16.first_ref, f32[2,1,2,9,6,4,8,128]{7,6,5,4,3,2,1,0:T(8,128)S(1)} %get-tuple-element.18.coef_ref, ...), custom_call_target="tpu_custom_call" | custom-call | tf_op jit(solution)/shard_map/pallas_call | solution.py:370
  13.2 0.1 collective-permute-start.3
  13.3 1.3 %collective-permute-done.3 = f32[2,64,256]{2,1,0:T(8,128)S(1)} collective-permute-done((f32[2,64,256]{2,1,0:T(8,128)S(1)}, f32[2,64,256]{2,1,0:T(8,128)S(1)}, u32[]{:S(2)}, u32[]{:S(2)}) %collective-permute-start.3) | collective-permute-done | bytes 131104 | tf_op jit(solution)/shard_map/ppermute | solution.py:22
  14.6 1.5 %collective-permute-start.4 = (f32[1,1,64,256]{3,2,1,0:T(8,128)S(1)}, f32[1,1,64,256]{3,2,1,0:T(8,128)S(1)}, u32[]{:S(2)}, u32[]{:S(2)}) collective-permute-start(f32[1,1,64,256]{3,2,1,0:T(8,128)S(1)} %slice_bitcast_fusion), channel_id=1, source_target_pairs={{0,24},{8,16},{16,8},{24,0},{1,25},{9,17},{17,9},{25,1},{2,26},{10... | collective-permute-start | bytes 196616 | tf_op jit(solution)/shard_map/ppermute | solution.py:22
  16.1 2.7 %collective-permute-done.4 = f32[1,1,64,256]{3,2,1,0:T(8,128)S(1)} collective-permute-done((f32[1,1,64,256]{3,2,1,0:T(8,128)S(1)}, f32[1,1,64,256]{3,2,1,0:T(8,128)S(1)}, u32[]{:S(2)}, u32[]{:S(2)}) %collective-permute-start.4) | collective-permute-done | bytes 65568 | tf_op jit(solution)/shard_map/ppermute | solution.py:22
  18.8 2.5 %collective-permute-start.7 = (f32[1,64,256]{2,1,0:T(8,128)S(1)}, f32[1,64,256]{2,1,0:T(8,128)S(1)}, u32[]{:S(2)}, u32[]{:S(2)}) collective-permute-start(f32[1,64,256]{2,1,0:T(8,128)S(1)} %fusion.1), channel_id=1, source_target_pairs={{0,3},{1,2},{2,1},{3,0},{4,7},{5,6},{6,5},{7,4},{8,11},{9,10},{10,... | collective-permute-start | bytes 196616 | tf_op jit(solution)/shard_map/ppermute | solution.py:22
  21.3 0.5 %collective-permute-start.6 = (f32[1,64,256]{2,1,0:T(8,128)S(1)}, f32[1,64,256]{2,1,0:T(8,128)S(1)}, u32[]{:S(2)}, u32[]{:S(2)}) collective-permute-start(f32[1,64,256]{2,1,0:T(8,128)S(1)} %fusion.1), channel_id=1, source_target_pairs={{0,2},{1,3},{2,0},{3,1},{4,6},{5,7},{6,4},{7,5},{8,10},{9,11},{10,... | collective-permute-start | bytes 196616 | tf_op jit(solution)/shard_map/ppermute | solution.py:22
  21.7 0.6 %collective-permute-start.5 = (f32[1,64,256]{2,1,0:T(8,128)S(1)}, f32[1,64,256]{2,1,0:T(8,128)S(1)}, u32[]{:S(2)}, u32[]{:S(2)}) collective-permute-start(f32[1,64,256]{2,1,0:T(8,128)S(1)} %fusion.1), channel_id=1, source_target_pairs={{0,1},{1,0},{2,3},{3,2},{4,5},{5,4},{6,7},{7,6},{8,9},{9,8},{10,11... | collective-permute-start | bytes 196616 | tf_op jit(solution)/shard_map/ppermute | solution.py:22
  22.3 2.0 %collective-permute-done.7 = f32[1,64,256]{2,1,0:T(8,128)S(1)} collective-permute-done((f32[1,64,256]{2,1,0:T(8,128)S(1)}, f32[1,64,256]{2,1,0:T(8,128)S(1)}, u32[]{:S(2)}, u32[]{:S(2)}) %collective-permute-start.7) | collective-permute-done | bytes 65568 | tf_op jit(solution)/shard_map/ppermute | solution.py:22
  24.3 1.3 %collective-permute-done.6 = f32[1,64,256]{2,1,0:T(8,128)S(1)} collective-permute-done((f32[1,64,256]{2,1,0:T(8,128)S(1)}, f32[1,64,256]{2,1,0:T(8,128)S(1)}, u32[]{:S(2)}, u32[]{:S(2)}) %collective-permute-start.6) | collective-permute-done | bytes 65568 | tf_op jit(solution)/shard_map/ppermute | solution.py:22
  25.5 0.5 %collective-permute-done.5 = f32[1,64,256]{2,1,0:T(8,128)S(1)} collective-permute-done((f32[1,64,256]{2,1,0:T(8,128)S(1)}, f32[1,64,256]{2,1,0:T(8,128)S(1)}, u32[]{:S(2)}, u32[]{:S(2)}) %collective-permute-start.5) | collective-permute-done | bytes 65568 | tf_op jit(solution)/shard_map/ppermute | solution.py:22
  26.0 2.6 %collective-permute-start.8 = (f32[1,64,256]{2,1,0:T(8,128)S(1)}, f32[1,64,256]{2,1,0:T(8,128)S(1)}, u32[]{:S(2)}, u32[]{:S(2)}) collective-permute-start(f32[1,64,256]{2,1,0:T(8,128)S(1)} %add_add_fusion), channel_id=1, source_target_pairs={{0,4},{1,5},{2,6},{3,7},{4,0},{5,1},{6,2},{7,3},{8,12},{9,13},{10,... | collective-permute-start | bytes 196616 | tf_op jit(solution)/shard_map/ppermute | solution.py:22
  28.7 2.6 %collective-permute-done.8 = f32[1,64,256]{2,1,0:T(8,128)S(1)} collective-permute-done((f32[1,64,256]{2,1,0:T(8,128)S(1)}, f32[1,64,256]{2,1,0:T(8,128)S(1)}, u32[]{:S(2)}, u32[]{:S(2)}) %collective-permute-start.8) | collective-permute-done | bytes 65568 | tf_op jit(solution)/shard_map/ppermute | solution.py:22
  31.3 0.6 %add.23 = f32[1,64,256]{2,1,0:T(8,128)} add(f32[1,64,256]{2,1,0:T(8,128)S(1)} %add_add_fusion, f32[1,64,256]{2,1,0:T(8,128)S(1)} %collective-permute-done.8) | non-fusion elementwise | flops 16384 | bytes 196608 | tf_op jit(solution)/shard_map/add | solution.py:397
  (4 shorter events, 0.1 us)
Async XLA Ops:
  0.0 5.6 %collective-permute-start = (s32[1,64,256]{2,1,0:T(8,128)}, s32[1,64,256]{2,1,0:T(8,128)S(1)}, u32[]{:S(2)}, u32[]{:S(2)}) collective-permute-start(s32[1,64,256]{2,1,0:T(8,128)} %vel_hbm.1), channel_id=1, source_target_pairs={{0,16},{8,24},{16,0},{24,8},{1,17},{9,25},{17,1},{25,9},{2,18},{10... | collective-permute-start | bytes 196616 | tf_op jit(solution)/shard_map/ppermute | solution.py:22
  3.0 3.2 %collective-permute-start.1 = (s32[1,64,256]{2,1,0:T(8,128)}, s32[1,64,256]{2,1,0:T(8,128)S(1)}, u32[]{:S(2)}, u32[]{:S(2)}) collective-permute-start(s32[1,64,256]{2,1,0:T(8,128)} %vel_hbm.1), channel_id=1, source_target_pairs={{0,8},{8,0},{16,24},{24,16},{1,9},{9,1},{17,25},{25,17},{2,10},{10... | collective-permute-start | bytes 196616 | tf_op jit(solution)/shard_map/ppermute | solution.py:22
  5.6 1.9 %collective-permute-start.2 = (s32[1,64,256]{2,1,0:T(8,128)S(1)}, s32[1,64,256]{2,1,0:T(8,128)S(1)}, u32[]{:S(2)}, u32[]{:S(2)}) collective-permute-start(s32[1,64,256]{2,1,0:T(8,128)S(1)} %collective-permute-done.refs_0_), channel_id=1, source_target_pairs={{0,8},{8,0},{16,24},{24,16},{1,9},{9,1},{17,25},{25,17},{2,10},{10... | collective-permute-start | bytes 196616 | tf_op jit(solution)/shard_map/ppermute | solution.py:22
  13.2 1.4 %collective-permute-start.3 = (f32[2,64,256]{2,1,0:T(8,128)S(1)}, f32[2,64,256]{2,1,0:T(8,128)S(1)}, u32[]{:S(2)}, u32[]{:S(2)}) collective-permute-start(f32[2,64,256]{2,1,0:T(8,128)S(1)} %get-tuple-element.22), channel_id=1, source_target_pairs={{0,8},{8,0},{16,24},{24,16},{1,9},{9,1},{17,25},{25,17},{2,10},{10... | collective-permute-start | bytes 393224 | tf_op jit(solution)/shard_map/ppermute | solution.py:22
  14.6 4.1 %collective-permute-start.4 = (f32[1,1,64,256]{3,2,1,0:T(8,128)S(1)}, f32[1,1,64,256]{3,2,1,0:T(8,128)S(1)}, u32[]{:S(2)}, u32[]{:S(2)}) collective-permute-start(f32[1,1,64,256]{3,2,1,0:T(8,128)S(1)} %slice_bitcast_fusion), channel_id=1, source_target_pairs={{0,24},{8,16},{16,8},{24,0},{1,25},{9,17},{17,9},{25,1},{2,26},{10... | collective-permute-start | bytes 196616 | tf_op jit(solution)/shard_map/ppermute | solution.py:22
  18.8 5.5 %collective-permute-start.7 = (f32[1,64,256]{2,1,0:T(8,128)S(1)}, f32[1,64,256]{2,1,0:T(8,128)S(1)}, u32[]{:S(2)}, u32[]{:S(2)}) collective-permute-start(f32[1,64,256]{2,1,0:T(8,128)S(1)} %fusion.1), channel_id=1, source_target_pairs={{0,3},{1,2},{2,1},{3,0},{4,7},{5,6},{6,5},{7,4},{8,11},{9,10},{10,... | collective-permute-start | bytes 196616 | tf_op jit(solution)/shard_map/ppermute | solution.py:22
  21.3 4.3 %collective-permute-start.6 = (f32[1,64,256]{2,1,0:T(8,128)S(1)}, f32[1,64,256]{2,1,0:T(8,128)S(1)}, u32[]{:S(2)}, u32[]{:S(2)}) collective-permute-start(f32[1,64,256]{2,1,0:T(8,128)S(1)} %fusion.1), channel_id=1, source_target_pairs={{0,2},{1,3},{2,0},{3,1},{4,6},{5,7},{6,4},{7,5},{8,10},{9,11},{10,... | collective-permute-start | bytes 196616 | tf_op jit(solution)/shard_map/ppermute | solution.py:22
  21.7 4.3 %collective-permute-start.5 = (f32[1,64,256]{2,1,0:T(8,128)S(1)}, f32[1,64,256]{2,1,0:T(8,128)S(1)}, u32[]{:S(2)}, u32[]{:S(2)}) collective-permute-start(f32[1,64,256]{2,1,0:T(8,128)S(1)} %fusion.1), channel_id=1, source_target_pairs={{0,1},{1,0},{2,3},{3,2},{4,5},{5,4},{6,7},{7,6},{8,9},{9,8},{10,11... | collective-permute-start | bytes 196616 | tf_op jit(solution)/shard_map/ppermute | solution.py:22
  26.0 5.2 %collective-permute-start.8 = (f32[1,64,256]{2,1,0:T(8,128)S(1)}, f32[1,64,256]{2,1,0:T(8,128)S(1)}, u32[]{:S(2)}, u32[]{:S(2)}) collective-permute-start(f32[1,64,256]{2,1,0:T(8,128)S(1)} %add_add_fusion), channel_id=1, source_target_pairs={{0,4},{1,5},{2,6},{3,7},{4,0},{5,1},{6,2},{7,3},{8,12},{9,13},{10,... | collective-permute-start | bytes 196616 | tf_op jit(solution)/shard_map/ppermute | solution.py:22

commit v9 on v8

--- a/solution.py
+++ b/solution.py
@@ -13,7 +13,7 @@
 PAIR = 2
 QUAD = 4
 ENTRY_SPAN = LANES // PAIR
-READY = 6
+READY = 5
 EARLY = 2
 
 

time: 32 us -> 32 us (level)
  no operation moved by 1% of the time
where the time goes in v9:
time: 32 us; the launch traced here: 31.8 us
  starting transfers between devices  11.3 us (35%)
  waiting for transfers between devices  10.2 us (32%)
  Pallas kernels  9.53 us (30%)
  other arithmetic  0.68 us (2%)
    ppermute x9, starting transfers between devices, exchange(): return lax.ppermute(value, axis, [(i, i ^ flip) for i in range(count)])  11.3 us
    ppermute x9, waiting for transfers between devices, exchange(): return lax.ppermute(value, axis, [(i, i ^ flip) for i in range(count)])  10.2 us
    pallas_call x1, Pallas kernels, per_device(): pl.pallas_call(functools.partial(image_kernel, (groups, depth_count, leve...  5.76 us
    pallas_call x1, Pallas kernels, per_device(): pl.pallas_call(functools.partial(first_kernel, (groups, count, local_coun...  2.59 us
    pallas_call x1, Pallas kernels, per_device(): pl.pallas_call(functools.partial(early_kernel, (groups, levels, terms)),...  1.18 us
  transfers between devices with their start and end apart: 9, of which 6 were waited for; matrix products, arithmetic and copies ran while one was open for 0% of the time, Pallas kernels for 12%

profile of v9, /device:TPU:0, one launch (start us, length us, event | category | flops | bytes accessed | tf_op | source)
XLA Modules:
  0.0 31.8 jit_solution(819915694147617660)
XLA Ops:
  0.0 3.0 %collective-permute-start = (s32[1,64,256]{2,1,0:T(8,128)}, s32[1,64,256]{2,1,0:T(8,128)S(1)}, u32[]{:S(2)}, u32[]{:S(2)}) collective-permute-start(s32[1,64,256]{2,1,0:T(8,128)} %vel_hbm.1), channel_id=1, source_target_pairs={{0,16},{8,24},{16,0},{24,8},{1,17},{9,25},{17,1},{25,9},{2,18},{10... | collective-permute-start | bytes 196616 | tf_op jit(solution)/shard_map/ppermute | solution.py:22
  3.0 0.0 collective-permute-start.1
  3.0 2.6 %shard_map.46 = (f32[1,2,9,8,128]{4,3,2,1,0:T(8,128)S(1)}, f32[1,9,2,8,4,8,128]{6,5,4,3,2,1,0:T(8,128)S(1)}, s32[1,64,256]{2,1,0:T(8,128)S(1)}) custom-call(s32[8]{0:T(128)} %slot_hbm.1, f32[8,2,64,256]{3,2,1,0:T(8,128)} %surface_ref.1, f32[576,64]{1,0:T(8,128)} %bitcast.16, s32[1,64,256]{2,1,0:T(8,128)} %vel_hbm.1), custom_call_target="tpu_custom_call" | custom-call | flops 200000000 | bytes 16000000 | tf_op jit(solution)/shard_map/pallas_call | solution.py:322
  5.6 0.0 collective-permute-done.refs_0_
  5.6 0.6 %collective-permute-start.2 = (s32[1,64,256]{2,1,0:T(8,128)S(1)}, s32[1,64,256]{2,1,0:T(8,128)S(1)}, u32[]{:S(2)}, u32[]{:S(2)}) collective-permute-start(s32[1,64,256]{2,1,0:T(8,128)S(1)} %collective-permute-done.refs_0_), channel_id=1, source_target_pairs={{0,8},{8,0},{16,24},{24,16},{1,9},{9,1},{17,25},{25,17},{2,10},{10... | collective-permute-start | bytes 196616 | tf_op jit(solution)/shard_map/ppermute | solution.py:22
  6.2 0.0 collective-permute-done.1.refs_1_
  6.2 1.2 %shard_map.47 = (f32[2,1,2,9,5,4,8,128]{7,6,5,4,3,2,1,0:T(8,128)S(1)}, s32[2,8,4,8,128]{4,3,2,1,0:T(8,128)S(1)}) custom-call(f32[1,2,9,8,128]{4,3,2,1,0:T(8,128)S(1)} %get-tuple-element.15.table_ref, s32[1,64,256]{2,1,0:T(8,128)S(1)} %get-tuple-element.17.refs_0_, s32[1,64,256]{2,1,0:T(8,128)S(1)} %collective-permute-done.1.refs_1_), custom_call_target="tpu_custom_call" | custom-call | flops 200000000 | bytes 16000000 | tf_op jit(solution)/shard_map/pallas_call | solution.py:357
  7.3 0.0 collective-permute-done.2.refs_1_
  7.3 5.8 %shard_map.48 = (f32[2,64,256]{2,1,0:T(8,128)S(1)}, f32[2,64,256]{2,1,0:T(8,128)S(1)}) custom-call(f32[1,2,9,8,128]{4,3,2,1,0:T(8,128)S(1)} %get-tuple-element.15.table_ref, f32[1,9,2,8,4,8,128]{6,5,4,3,2,1,0:T(8,128)S(1)} %get-tuple-element.16.first_ref, f32[2,1,2,9,5,4,8,128]{7,6,5,4,3,2,1,0:T(8,128)S(1)} %get-tuple-element.18.coef_ref, ...), custom_call_target="tpu_custom_call" | custom-call | tf_op jit(solution)/shard_map/pallas_call | solution.py:370
  13.1 0.1 collective-permute-start.3
  13.2 1.3 %collective-permute-done.3 = f32[2,64,256]{2,1,0:T(8,128)S(1)} collective-permute-done((f32[2,64,256]{2,1,0:T(8,128)S(1)}, f32[2,64,256]{2,1,0:T(8,128)S(1)}, u32[]{:S(2)}, u32[]{:S(2)}) %collective-permute-start.3) | collective-permute-done | bytes 131104 | tf_op jit(solution)/shard_map/ppermute | solution.py:22
  14.6 1.5 %collective-permute-start.4 = (f32[1,1,64,256]{3,2,1,0:T(8,128)S(1)}, f32[1,1,64,256]{3,2,1,0:T(8,128)S(1)}, u32[]{:S(2)}, u32[]{:S(2)}) collective-permute-start(f32[1,1,64,256]{3,2,1,0:T(8,128)S(1)} %slice_bitcast_fusion), channel_id=1, source_target_pairs={{0,24},{8,16},{16,8},{24,0},{1,25},{9,17},{17,9},{25,1},{2,26},{10... | collective-permute-start | bytes 196616 | tf_op jit(solution)/shard_map/ppermute | solution.py:22
  16.0 2.7 %collective-permute-done.4 = f32[1,1,64,256]{3,2,1,0:T(8,128)S(1)} collective-permute-done((f32[1,1,64,256]{3,2,1,0:T(8,128)S(1)}, f32[1,1,64,256]{3,2,1,0:T(8,128)S(1)}, u32[]{:S(2)}, u32[]{:S(2)}) %collective-permute-start.4) | collective-permute-done | bytes 65568 | tf_op jit(solution)/shard_map/ppermute | solution.py:22
  18.7 2.5 %collective-permute-start.7 = (f32[1,64,256]{2,1,0:T(8,128)S(1)}, f32[1,64,256]{2,1,0:T(8,128)S(1)}, u32[]{:S(2)}, u32[]{:S(2)}) collective-permute-start(f32[1,64,256]{2,1,0:T(8,128)S(1)} %fusion.1), channel_id=1, source_target_pairs={{0,3},{1,2},{2,1},{3,0},{4,7},{5,6},{6,5},{7,4},{8,11},{9,10},{10,... | collective-permute-start | bytes 196616 | tf_op jit(solution)/shard_map/ppermute | solution.py:22
  21.2 0.4 %collective-permute-start.6 = (f32[1,64,256]{2,1,0:T(8,128)S(1)}, f32[1,64,256]{2,1,0:T(8,128)S(1)}, u32[]{:S(2)}, u32[]{:S(2)}) collective-permute-start(f32[1,64,256]{2,1,0:T(8,128)S(1)} %fusion.1), channel_id=1, source_target_pairs={{0,2},{1,3},{2,0},{3,1},{4,6},{5,7},{6,4},{7,5},{8,10},{9,11},{10,... | collective-permute-start | bytes 196616 | tf_op jit(solution)/shard_map/ppermute | solution.py:22
  21.7 0.6 %collective-permute-start.5 = (f32[1,64,256]{2,1,0:T(8,128)S(1)}, f32[1,64,256]{2,1,0:T(8,128)S(1)}, u32[]{:S(2)}, u32[]{:S(2)}) collective-permute-start(f32[1,64,256]{2,1,0:T(8,128)S(1)} %fusion.1), channel_id=1, source_target_pairs={{0,1},{1,0},{2,3},{3,2},{4,5},{5,4},{6,7},{7,6},{8,9},{9,8},{10,11... | collective-permute-start | bytes 196616 | tf_op jit(solution)/shard_map/ppermute | solution.py:22
  22.3 2.0 %collective-permute-done.7 = f32[1,64,256]{2,1,0:T(8,128)S(1)} collective-permute-done((f32[1,64,256]{2,1,0:T(8,128)S(1)}, f32[1,64,256]{2,1,0:T(8,128)S(1)}, u32[]{:S(2)}, u32[]{:S(2)}) %collective-permute-start.7) | collective-permute-done | bytes 65568 | tf_op jit(solution)/shard_map/ppermute | solution.py:22
  24.2 1.2 %collective-permute-done.6 = f32[1,64,256]{2,1,0:T(8,128)S(1)} collective-permute-done((f32[1,64,256]{2,1,0:T(8,128)S(1)}, f32[1,64,256]{2,1,0:T(8,128)S(1)}, u32[]{:S(2)}, u32[]{:S(2)}) %collective-permute-start.6) | collective-permute-done | bytes 65568 | tf_op jit(solution)/shard_map/ppermute | solution.py:22
  25.5 0.4 %collective-permute-done.5 = f32[1,64,256]{2,1,0:T(8,128)S(1)} collective-permute-done((f32[1,64,256]{2,1,0:T(8,128)S(1)}, f32[1,64,256]{2,1,0:T(8,128)S(1)}, u32[]{:S(2)}, u32[]{:S(2)}) %collective-permute-start.5) | collective-permute-done | bytes 65568 | tf_op jit(solution)/shard_map/ppermute | solution.py:22
  25.9 2.7 %collective-permute-start.8 = (f32[1,64,256]{2,1,0:T(8,128)S(1)}, f32[1,64,256]{2,1,0:T(8,128)S(1)}, u32[]{:S(2)}, u32[]{:S(2)}) collective-permute-start(f32[1,64,256]{2,1,0:T(8,128)S(1)} %add_add_fusion), channel_id=1, source_target_pairs={{0,4},{1,5},{2,6},{3,7},{4,0},{5,1},{6,2},{7,3},{8,12},{9,13},{10,... | collective-permute-start | bytes 196616 | tf_op jit(solution)/shard_map/ppermute | solution.py:22
  28.6 2.6 %collective-permute-done.8 = f32[1,64,256]{2,1,0:T(8,128)S(1)} collective-permute-done((f32[1,64,256]{2,1,0:T(8,128)S(1)}, f32[1,64,256]{2,1,0:T(8,128)S(1)}, u32[]{:S(2)}, u32[]{:S(2)}) %collective-permute-start.8) | collective-permute-done | bytes 65568 | tf_op jit(solution)/shard_map/ppermute | solution.py:22
  31.2 0.6 %add.23 = f32[1,64,256]{2,1,0:T(8,128)} add(f32[1,64,256]{2,1,0:T(8,128)S(1)} %add_add_fusion, f32[1,64,256]{2,1,0:T(8,128)S(1)} %collective-permute-done.8) | non-fusion elementwise | flops 16384 | bytes 196608 | tf_op jit(solution)/shard_map/add | solution.py:397
  (4 shorter events, 0.1 us)
Async XLA Ops:
  0.0 5.6 %collective-permute-start = (s32[1,64,256]{2,1,0:T(8,128)}, s32[1,64,256]{2,1,0:T(8,128)S(1)}, u32[]{:S(2)}, u32[]{:S(2)}) collective-permute-start(s32[1,64,256]{2,1,0:T(8,128)} %vel_hbm.1), channel_id=1, source_target_pairs={{0,16},{8,24},{16,0},{24,8},{1,17},{9,25},{17,1},{25,9},{2,18},{10... | collective-permute-start | bytes 196616 | tf_op jit(solution)/shard_map/ppermute | solution.py:22
  3.0 3.2 %collective-permute-start.1 = (s32[1,64,256]{2,1,0:T(8,128)}, s32[1,64,256]{2,1,0:T(8,128)S(1)}, u32[]{:S(2)}, u32[]{:S(2)}) collective-permute-start(s32[1,64,256]{2,1,0:T(8,128)} %vel_hbm.1), channel_id=1, source_target_pairs={{0,8},{8,0},{16,24},{24,16},{1,9},{9,1},{17,25},{25,17},{2,10},{10... | collective-permute-start | bytes 196616 | tf_op jit(solution)/shard_map/ppermute | solution.py:22
  5.6 1.8 %collective-permute-start.2 = (s32[1,64,256]{2,1,0:T(8,128)S(1)}, s32[1,64,256]{2,1,0:T(8,128)S(1)}, u32[]{:S(2)}, u32[]{:S(2)}) collective-permute-start(s32[1,64,256]{2,1,0:T(8,128)S(1)} %collective-permute-done.refs_0_), channel_id=1, source_target_pairs={{0,8},{8,0},{16,24},{24,16},{1,9},{9,1},{17,25},{25,17},{2,10},{10... | collective-permute-start | bytes 196616 | tf_op jit(solution)/shard_map/ppermute | solution.py:22
  13.1 1.4 %collective-permute-start.3 = (f32[2,64,256]{2,1,0:T(8,128)S(1)}, f32[2,64,256]{2,1,0:T(8,128)S(1)}, u32[]{:S(2)}, u32[]{:S(2)}) collective-permute-start(f32[2,64,256]{2,1,0:T(8,128)S(1)} %get-tuple-element.22), channel_id=1, source_target_pairs={{0,8},{8,0},{16,24},{24,16},{1,9},{9,1},{17,25},{25,17},{2,10},{10... | collective-permute-start | bytes 393224 | tf_op jit(solution)/shard_map/ppermute | solution.py:22
  14.6 4.1 %collective-permute-start.4 = (f32[1,1,64,256]{3,2,1,0:T(8,128)S(1)}, f32[1,1,64,256]{3,2,1,0:T(8,128)S(1)}, u32[]{:S(2)}, u32[]{:S(2)}) collective-permute-start(f32[1,1,64,256]{3,2,1,0:T(8,128)S(1)} %slice_bitcast_fusion), channel_id=1, source_target_pairs={{0,24},{8,16},{16,8},{24,0},{1,25},{9,17},{17,9},{25,1},{2,26},{10... | collective-permute-start | bytes 196616 | tf_op jit(solution)/shard_map/ppermute | solution.py:22
  18.7 5.5 %collective-permute-start.7 = (f32[1,64,256]{2,1,0:T(8,128)S(1)}, f32[1,64,256]{2,1,0:T(8,128)S(1)}, u32[]{:S(2)}, u32[]{:S(2)}) collective-permute-start(f32[1,64,256]{2,1,0:T(8,128)S(1)} %fusion.1), channel_id=1, source_target_pairs={{0,3},{1,2},{2,1},{3,0},{4,7},{5,6},{6,5},{7,4},{8,11},{9,10},{10,... | collective-permute-start | bytes 196616 | tf_op jit(solution)/shard_map/ppermute | solution.py:22
  21.2 4.3 %collective-permute-start.6 = (f32[1,64,256]{2,1,0:T(8,128)S(1)}, f32[1,64,256]{2,1,0:T(8,128)S(1)}, u32[]{:S(2)}, u32[]{:S(2)}) collective-permute-start(f32[1,64,256]{2,1,0:T(8,128)S(1)} %fusion.1), channel_id=1, source_target_pairs={{0,2},{1,3},{2,0},{3,1},{4,6},{5,7},{6,4},{7,5},{8,10},{9,11},{10,... | collective-permute-start | bytes 196616 | tf_op jit(solution)/shard_map/ppermute | solution.py:22
  21.7 4.3 %collective-permute-start.5 = (f32[1,64,256]{2,1,0:T(8,128)S(1)}, f32[1,64,256]{2,1,0:T(8,128)S(1)}, u32[]{:S(2)}, u32[]{:S(2)}) collective-permute-start(f32[1,64,256]{2,1,0:T(8,128)S(1)} %fusion.1), channel_id=1, source_target_pairs={{0,1},{1,0},{2,3},{3,2},{4,5},{5,4},{6,7},{7,6},{8,9},{9,8},{10,11... | collective-permute-start | bytes 196616 | tf_op jit(solution)/shard_map/ppermute | solution.py:22
  25.9 5.2 %collective-permute-start.8 = (f32[1,64,256]{2,1,0:T(8,128)S(1)}, f32[1,64,256]{2,1,0:T(8,128)S(1)}, u32[]{:S(2)}, u32[]{:S(2)}) collective-permute-start(f32[1,64,256]{2,1,0:T(8,128)S(1)} %add_add_fusion), channel_id=1, source_target_pairs={{0,4},{1,5},{2,6},{3,7},{4,0},{5,1},{6,2},{7,3},{8,12},{9,13},{10,... | collective-permute-start | bytes 196616 | tf_op jit(solution)/shard_map/ppermute | solution.py:22
